TPU v7x, 32 devices: a whole 2x2x4 slice. The times are simulated.
32 devices in a mesh: pix: 8 (over z, y), batch: 4 (over x, core).
Axes of the slice: x: 2, y: 2, z: 4, core: 2. Of those that a mesh axis runs over, the one named last changes fastest.
Arguments:
- fine_tokens: bfloat16 [32768, 512], P(('batch', 'pix')), parts along dimension 0, may hold values from -8 to 8
- parent_tokens: bfloat16 [8192, 512], P(('batch', 'pix')), parts along dimension 0, may hold values from -8 to 8
- shift_table: int32 [8192], P('pix'), may hold values from 0 to 8191, as said below
- parent_slot: int32 [2048], P('pix'), may hold values from 0 to 255, as said below
- fine_gain: float32 [512], replicated, may hold values from 0.1 to 1.9
- parent_gain: float32 [512], replicated, may hold values from 0.1 to 1.9
- w_qkv: bfloat16 [512, 1536], replicated, may hold values from -2 to 2
- w_parent: bfloat16 [512, 1024], replicated, may hold values from -2 to 2
- w_out: bfloat16 [1024, 512], replicated, may hold values from -0.1875 to 0.1875
Outputs:
- mixed: bfloat16 [32768, 512], P(('batch', 'pix')), parts along dimension 0
There are 4 independent parts, one for each index of `batch`. A program takes and returns all parts, laid end to end along the dimension named above; an argument that names none is the same for every part. Nothing has to cross between parts.
Inputs may be any that keep to these rules, and one draw needn't show every extreme that they name: Every entry shift_table[p] equals (p + o) mod 8192 with -128 <= o <= 128; on every device one entry has o = 128 and one o = -128. Over the stored rows of one owner j, parent_slot takes every value 0 to 255 once.
All inputs are finite; a program needn't handle non-finite values.
Results may differ from a plain program's by a relative error of at most 0.0018.
The roundings to bfloat16 on the way count: a program that leaves them out, or rounds other values in their place, can miss the bound.
Values may be sent and summed in bfloat16 or wider, within the bound.
No kernel may reach another device: no remote copies, remote signals or barrier semaphores. Data moves between devices by JAX's collectives and lax.ppermute only.
A program may use at most 64 MiB of HBM per device.

v0:
```python
import jax
import jax.numpy as jnp
from jax import lax
from jax.sharding import PartitionSpec as P

HEADS = 16
WIN = 256
HALO = 128
PWIN = 64


def with_halo(cells, sides, width):
    for axis, dim in sides:
        count = lax.axis_size(axis)
        head = lax.slice_in_dim(cells, 0, width, axis=dim)
        tail = lax.slice_in_dim(cells, cells.shape[dim] - width, cells.shape[dim], axis=dim)
        cells = jnp.concatenate(
            [
                lax.ppermute(tail, axis, [(i, (i + 1) % count) for i in range(count)]),
                cells,
                lax.ppermute(head, axis, [((i + 1) % count, i) for i in range(count)]),
            ],
            axis=dim,
        )
    return cells


def rms_rows(matrix, gain):
    values = matrix.astype(jnp.float32)
    factor = lax.rsqrt(jnp.mean(values * values, axis=-1, keepdims=True) + 1e-06)
    return (values * factor * gain).astype(jnp.bfloat16)


def attend(queries, key_heads, value_heads):
    scores = jnp.einsum("wrhe,wshe->whrs", queries, key_heads, preferred_element_type=jnp.float32)
    scores = scores / jnp.sqrt(jnp.float32(key_heads.shape[-1]))
    highest = jnp.max(scores, axis=-1, keepdims=True)
    powers = jnp.exp(scores - highest)
    weights = (powers / jnp.sum(powers, axis=-1, keepdims=True)).astype(jnp.bfloat16)
    result = jnp.einsum("whrs,wshe->wrhe", weights, value_heads, preferred_element_type=jnp.float32)
    return result.astype(jnp.bfloat16)


def on_device(
    fine_tokens,
    parent_tokens,
    shift_table,
    parent_slot,
    fine_gain,
    parent_gain,
    w_qkv,
    w_parent,
    w_out,
):
    row_count, features = fine_tokens.shape
    devices = lax.axis_size("pix")
    offset_rows = lax.axis_index("pix") * row_count
    all_rows = row_count * devices
    normed = rms_rows(fine_tokens, fine_gain)
    qkv = jnp.dot(normed, w_qkv, preferred_element_type=jnp.float32).astype(jnp.bfloat16)
    rims = with_halo(normed, (("pix", 0),), HALO)
    edge_rows = jnp.concatenate([rims[:HALO], rims[-HALO:]], axis=0)
    edge_kv = jnp.dot(edge_rows, w_qkv[:, features:], preferred_element_type=jnp.float32).astype(
        jnp.bfloat16
    )
    extended = jnp.concatenate([edge_kv[:HALO], qkv[:, features:], edge_kv[HALO:]], axis=0)
    local_index = jnp.mod(shift_table - offset_rows + HALO, all_rows)
    window_kv = jnp.take(extended, local_index, axis=0)
    arrived, slots = (
        lax.all_to_all(parent_tokens, "pix", split_axis=0, concat_axis=0, tiled=True),
        lax.all_to_all(parent_slot, "pix", split_axis=0, concat_axis=0, tiled=True),
    )
    ordered = jnp.zeros_like(arrived).at[slots].set(arrived)
    parent_kv = jnp.dot(
        rms_rows(ordered, parent_gain), w_parent, preferred_element_type=jnp.float32
    ).astype(jnp.bfloat16)
    head_size = features // HEADS
    windows = row_count // WIN
    queries = qkv[:, :features].reshape(windows, WIN, HEADS, head_size)
    self_keys = window_kv[:, :features].reshape(windows, WIN, HEADS, head_size)
    self_values = window_kv[:, features:].reshape(windows, WIN, HEADS, head_size)
    cross_keys = parent_kv[:, :features].reshape(windows, PWIN, HEADS, head_size)
    cross_values = parent_kv[:, features:].reshape(windows, PWIN, HEADS, head_size)
    self_out = attend(queries, self_keys, self_values).reshape(row_count, features)
    cross_out = attend(queries, cross_keys, cross_values).reshape(row_count, features)
    joined = jnp.concatenate([self_out, cross_out], axis=1)
    branch = jnp.dot(joined, w_out, preferred_element_type=jnp.float32)
    return (fine_tokens.astype(jnp.float32) + branch).astype(jnp.bfloat16)


def solution(mesh):
    return jax.shard_map(
        on_device,
        mesh=mesh,
        in_specs=(
            P(("batch", "pix"), None),
            P(("batch", "pix"), None),
            P("pix"),
            P("pix"),
            P(),
            P(),
            P(),
            P(),
            P(),
        ),
        out_specs=P(("batch", "pix"), None),
        check_vma=False,
    )
```

profile of v0, /device:TPU:0, one launch (start us, length us, event | category | flops | bytes accessed | tf_op | source)
XLA Modules:
  0.0 82.9 jit_solution(17545787363016354909)
XLA Ops:
  0.0 1.6 %fusion.12 = f32[1024]{0:T(1024)S(1)} fusion(bf16[1024,512]{1,0:T(8,128)(2,1)} %param.9), kind=kLoop, calls=%fused_computation.20 | loop fusion | flops 1571840 | bytes 1052672 | tf_op jit(solution)/shard_map/reduce_sum | solution.py:30
  1.6 1.5 %fusion.14 = bf16[1024,512]{1,0:T(8,128)(2,1)S(1)} fusion(bf16[1024,512]{1,0:T(8,128)(2,1)} %param.9, f32[512]{0:T(512)} %param.13, f32[1024]{0:T(1024)S(1)} %add_rsqrt_fusion), kind=kLoop, calls=%fused_computation.22 | loop fusion | flops 2097152 | bytes 2103296 | tf_op jit(solution)/shard_map/convert_element_type | solution.py:31
  3.2 0.7 fusion.62
  3.8 3.0 %collective-permute-start = (bf16[128,512]{1,0:T(8,128)(2,1)}, bf16[128,512]{1,0:T(8,128)(2,1)}, u32[]{:S(2)}, u32[]{:S(2)}) collective-permute-start(bf16[128,512]{1,0:T(8,128)(2,1)} %get-tuple-element.7), channel_id=1, source_target_pairs={{0,4},{4,8},{8,12},{12,16},{16,20},{20,24},{24,28},{28,0},{1,5},{5... | collective-permute-start | bytes 393224 | tf_op jit(solution)/shard_map/ppermute | solution.py:19
  6.8 3.0 %collective-permute-start.1 = (bf16[128,512]{1,0:T(8,128)(2,1)S(1)}, bf16[128,512]{1,0:T(8,128)(2,1)}, u32[]{:S(2)}, u32[]{:S(2)}) collective-permute-start(bf16[128,512]{1,0:T(8,128)(2,1)S(1)} %get-tuple-element.8), channel_id=1, source_target_pairs={{4,0},{8,4},{12,8},{16,12},{20,16},{24,20},{28,24},{0,28},{5,1},{9... | collective-permute-start | bytes 393224 | tf_op jit(solution)/shard_map/ppermute | solution.py:21
  9.8 0.7 all_to_all.16
  10.5 3.3 %all-to-all-start = ((s32[8,32,1]{1,2,0:T(1,128)}), s32[8,32,1]{1,2,0:T(1,128)S(1)}, u32[]{:S(2)}, u32[]{:S(2)}) async-start(s32[8,32,1]{1,2,0:T(1,128)} %bitcast.1), calls=%async_computation | async-start | bytes 8192 | tf_op jit(solution)/shard_map/all_to_all | solution.py:71
  13.8 4.9 %convolution_convert_fusion = bf16[1024,1536]{1,0:T(8,128)(2,1)} fusion(bf16[1024,512]{1,0:T(8,128)(2,1)S(1)} %fusion.14, bf16[512,1536]{1,0:T(8,128)(2,1)} %param.15), kind=kOutput, calls=%fused_computation.13 | convolution fusion | flops 1612185600 | bytes 5767168 | tf_op jit(solution)/shard_map/dot_general | solution.py:60
  18.7 1.2 %slice-done.1 = bf16[1024,512]{1,0:T(8,128)(2,1)S(1)} async-done(((bf16[1024,1536]{1,0:T(8,128)(2,1)}), bf16[1024,512]{1,0:T(8,128)(2,1)S(1)}, s32[]{:S(2)}) %slice-start.1) | async-done | bytes 1048600 | tf_op jit(solution)/shard_map/slice | solution.py:79
  19.9 1.3 %copy.45 = bf16[1024,512]{0,1:T(8,128)(2,1)} copy(bf16[1024,512]{1,0:T(8,128)(2,1)S(1)} %slice-done.1) | data formatting | bytes 2097152 | tf_op jit(solution)/shard_map/slice | solution.py:79
  21.2 2.8 %reshape.81 = bf16[4,256,16,32]{1,0,3,2:T(4,128)(2,1)} reshape(bf16[1024,512]{0,1:T(8,128)(2,1)} %copy.45) | data formatting | bytes 2097152 | tf_op jit(solution)/shard_map/reshape | solution.py:79
  24.0 6.0 %all-to-all-start.1 = ((bf16[8,32,512]{2,1,0:T(8,128)(2,1)}), bf16[8,32,512]{2,1,0:T(8,128)(2,1)S(1)}, u32[]{:S(2)}, u32[]{:S(2)}) async-start(bf16[8,32,512]{2,1,0:T(8,128)(2,1)} %bitcast.3), calls=%async_computation.1 | async-start | bytes 524288 | tf_op jit(solution)/shard_map/all_to_all | solution.py:70
  30.6 0.7 reduce.3
  31.3 1.8 %convolution_convert_fusion.2 = bf16[256,1024]{1,0:T(8,128)(2,1)S(1)} fusion(bf16[512,1536]{1,0:T(8,128)(2,1)} %param.15, bf16[128,512]{1,0:T(8,128)(2,1)} %collective-permute-done.1, bf16[128,512]{1,0:T(8,128)(2,1)} %collective-permute-done), kind=kOutput, calls=%fused_computation.36 | convolution fusion | flops 269221888 | bytes 1835008 | tf_op jit(solution)/shard_map/dot_general | solution.py:63
  33.2 1.8 %pad_maximum_fusion = bf16[1280,1024]{1,0:T(8,128)(2,1)} fusion(bf16[128,1024]{1,0:T(8,128)(2,1)S(1)} %get-tuple-element.10, bf16[1024,1024]{1,0:T(8,128)(2,1)S(1)} %slice-done, bf16[128,1024]{1,0:T(8,128)(2,1)S(1)} %get-tuple-element.9), kind=kLoop, calls=%fused_computation.19 | loop fusion | flops 7864320 | bytes 5242880 | tf_op jit(solution)/shard_map/concatenate | solution.py:66
  35.0 7.1 %gather_fusion = bf16[1024,1024]{1,0:T(8,128)(2,1)S(1)} fusion(bf16[1280,1024]{1,0:T(8,128)(2,1)} %pad_maximum_fusion, s32[1024]{0:T(1024)S(1)} %broadcast_clamp_fusion), kind=kCustom, calls=%fused_computation | custom fusion | bytes 4198400 | tf_op jit(solution)/shard_map/jit(_take)/gather | solution.py:68
  42.3 1.1 %fusion.61 = (bf16[1024,512]{1,0:T(8,128)(2,1)}, bf16[1024,512]{1,0:T(8,128)(2,1)S(1)}) fusion(bf16[1024,1024]{1,0:T(8,128)(2,1)S(1)} %broadcast_select_fusion), kind=kLoop, calls=%fused_computation.74 | loop fusion | bytes 4194304 | tf_op jit(solution)/shard_map/slice | solution.py:81
  43.4 0.5 copy.46
  43.9 1.6 %reshape.82 = bf16[4,256,16,32]{1,0,3,2:T(4,128)(2,1)} reshape(bf16[1024,512]{0,1:T(8,128)(2,1)S(1)} %copy.46) | data formatting | bytes 2097152 | tf_op jit(solution)/shard_map/reshape | solution.py:80
  45.5 1.5 %copy.44 = bf16[1024,512]{0,1:T(8,128)(2,1)S(1)} copy(bf16[1024,512]{1,0:T(8,128)(2,1)} %get-tuple-element.5) | data formatting | bytes 2097152 | tf_op jit(solution)/shard_map/slice | solution.py:81
  47.0 1.6 %reshape.80 = bf16[4,256,16,32]{1,0,3,2:T(4,128)(2,1)} reshape(bf16[1024,512]{0,1:T(8,128)(2,1)S(1)} %copy.44) | data formatting | bytes 2097152 | tf_op jit(solution)/shard_map/reshape | solution.py:81
  48.6 10.2 %fusion.66 = (f32[4,16,256]{2,1,0:T(8,128)S(1)}, f32[4,16,256,256]{2,3,1,0:T(8,128)}) fusion(bf16[4,256,16,32]{1,0,3,2:T(4,128)(2,1)} %reshape.82, bf16[4,256,16,32]{1,0,3,2:T(4,128)(2,1)S(1)} %copy-done.2), kind=kOutput, calls=%fused_computation.79 | convolution fusion | flops 281018624 | bytes 18939904 | tf_op jit(solution)/shard_map/sub | solution.py:38
  58.8 7.3 %fusion.27 = bf16[4,256,16,32]{1,3,2,0:T(8,128)(2,1)S(1)} fusion(f32[4,16,256,256]{2,3,1,0:T(8,128)} %get-tuple-element.16, f32[4,16,256]{2,1,0:T(8,128)S(1)} %get-tuple-element.15, bf16[4,256,16,32]{1,0,3,2:T(4,128)(2,1)S(1)} %copy-done.4), kind=kOutput, calls=%fused_computation.34 | convolution fusion | flops 277348352 | bytes 18939904 | tf_op jit(solution)/shard_map/whrs,wshe->wrhe/dot_general | solution.py:40
  66.1 0.9 %copy.51 = bf16[4,256,16,32]{1,0,3,2:T(4,128)(2,1)S(1)} copy(bf16[4,256,16,32]{1,3,2,0:T(8,128)(2,1)S(1)} %fusion.27) | data formatting | bytes 2097152 | tf_op jit(solution)/shard_map/convert_element_type | solution.py:41
  67.0 1.2 %copy.60 = bf16[64,8,4,256]{3,1,2,0:T(8,128)(2,1)} copy(bf16[64,8,4,256]{3,2,1,0:T(4,128)(2,1)S(1)} %bitcast.33) | data formatting | bytes 2097152
  68.2 1.8 %scatter_custom_fusion = bf16[256,512]{1,0:T(8,128)(2,1)S(1)} fusion(s32[256]{0:T(256)S(1)} %bitcast.38, bf16[256,512]{1,0:T(8,128)(2,1)S(1)} %bitcast.37, bf16[]{:T(256)} %constant.60.clone.1), kind=kCustom, calls=%fused_computation.58 | custom fusion | bytes 262146 | tf_op jit(solution)/shard_map/scatter | solution.py:73
  70.2 1.7 %convolution_convert_fusion.1 = bf16[256,1024]{1,0:T(8,128)(2,1)S(1)} fusion(bf16[512,1024]{1,0:T(8,128)(2,1)} %param.16, bf16[256,512]{1,0:T(8,128)(2,1)S(1)} %scatter_custom_fusion, f32[512]{0:T(512)S(1)} %copy-done.6, f32[256]{0:T(256)S(1)} %add_rsqrt_fusion.1), kind=kOutput, calls=%fused_computation.35 | convolution fusion | flops 269221888 | bytes 1838080 | tf_op jit(solution)/shard_map/dot_general | solution.py:74
  72.3 0.8 fusion.40
  73.1 3.0 %fusion.65 = (f32[4,16,256]{2,1,0:T(8,128)S(1)}, f32[4,16,256,64]{2,3,1,0:T(8,128)}) fusion(f32[4,16,256,64]{2,3,1,0:T(8,128)S(1)} %fusion.40), kind=kOutput, calls=%fused_computation.78 | output fusion | flops 4194367 | bytes 8454144 | tf_op jit(solution)/shard_map/sub | solution.py:38
  76.5 2.6 %fusion.26 = bf16[4,256,16,32]{1,3,2,0:T(8,128)(2,1)S(1)} fusion(f32[4,16,256,64]{2,3,1,0:T(8,128)} %get-tuple-element.14, f32[4,16,256]{2,1,0:T(8,128)S(1)} %get-tuple-element.13, bf16[4,64,16,32]{1,0,3,2:T(4,128)(2,1)S(1)} %reshape.84), kind=kOutput, calls=%fused_computation.33 | convolution fusion | flops 69730304 | bytes 5570560 | tf_op jit(solution)/shard_map/whrs,wshe->wrhe/dot_general | solution.py:40
  79.2 0.9 %copy.58 = bf16[4,256,16,32]{1,0,3,2:T(4,128)(2,1)S(1)} copy(bf16[4,256,16,32]{1,3,2,0:T(8,128)(2,1)S(1)} %fusion.26) | data formatting | bytes 2097152 | tf_op jit(solution)/shard_map/convert_element_type | solution.py:41
  80.7 2.3 %fusion.15 = bf16[1024,512]{1,0:T(8,128)(2,1)} fusion(bf16[1024,512]{1,0:T(8,128)(2,1)S(1)} %copy-done.1, bf16[1024,512]{1,0:T(8,128)(2,1)S(1)} %copy-done, bf16[1024,512]{0,1:T(8,128)(2,1)S(1)} %bitcast.36, bf16[1024,512]{0,1:T(8,128)(2,1)S(1)} %bitcast.35), kind=kOutput, calls=%fused_computation.23 | convolution fusion | flops 1079508992 | bytes 5242880 | tf_op jit(solution)/shard_map/dot_general | solution.py:87
  (39 shorter events, 2.5 us)
Async XLA Ops:
  0.0 80.3 %copy-start = (bf16[1024,512]{1,0:T(8,128)(2,1)S(1)}, bf16[1024,512]{1,0:T(8,128)(2,1)}, u32[]{:S(2)}) copy-start(bf16[1024,512]{1,0:T(8,128)(2,1)} %param.17) | copy-start | bytes 3145732
  0.0 9.8 %copy-start.7 = (s32[256]{0:T(256)S(1)}, s32[256]{0:T(256)}, u32[]{:S(2)}) copy-start(s32[256]{0:T(256)} %param.12) | copy-start | bytes 3076
  3.8 27.5 %collective-permute-start = (bf16[128,512]{1,0:T(8,128)(2,1)}, bf16[128,512]{1,0:T(8,128)(2,1)}, u32[]{:S(2)}, u32[]{:S(2)}) collective-permute-start(bf16[128,512]{1,0:T(8,128)(2,1)} %get-tuple-element.7), channel_id=1, source_target_pairs={{0,4},{4,8},{8,12},{12,16},{16,20},{20,24},{24,28},{28,0},{1,5},{5... | collective-permute-start | bytes 393224 | tf_op jit(solution)/shard_map/ppermute | solution.py:19
  6.8 24.5 %collective-permute-start.1 = (bf16[128,512]{1,0:T(8,128)(2,1)S(1)}, bf16[128,512]{1,0:T(8,128)(2,1)}, u32[]{:S(2)}, u32[]{:S(2)}) collective-permute-start(bf16[128,512]{1,0:T(8,128)(2,1)S(1)} %get-tuple-element.8), channel_id=1, source_target_pairs={{4,0},{8,4},{12,8},{16,12},{20,16},{24,20},{28,24},{0,28},{5,1},{9... | collective-permute-start | bytes 393224 | tf_op jit(solution)/shard_map/ppermute | solution.py:21
  10.5 13.5 %all-to-all-start = ((s32[8,32,1]{1,2,0:T(1,128)}), s32[8,32,1]{1,2,0:T(1,128)S(1)}, u32[]{:S(2)}, u32[]{:S(2)}) async-start(s32[8,32,1]{1,2,0:T(1,128)} %bitcast.1), calls=%async_computation | async-start | bytes 8192 | tf_op jit(solution)/shard_map/all_to_all | solution.py:71
  13.8 4.9 %copy-start.5 = (s32[1024]{0:T(1024)S(1)}, s32[1024]{0:T(1024)}, u32[]{:S(2)}) copy-start(s32[1024]{0:T(1024)} %param.11) | copy-start | bytes 12292
  18.7 1.2 %slice-start.1 = ((bf16[1024,1536]{1,0:T(8,128)(2,1)}), bf16[1024,512]{1,0:T(8,128)(2,1)S(1)}, s32[]{:S(2)}) async-start(bf16[1024,1536]{1,0:T(8,128)(2,1)} %convolution_convert_fusion), calls=%async_computation.3 | async-start | bytes 2097152 | tf_op jit(solution)/shard_map/slice | solution.py:79
  21.2 11.9 %slice-start = ((bf16[1024,1536]{1,0:T(8,128)(2,1)}), bf16[1024,1024]{1,0:T(8,128)(2,1)S(1)}, s32[]{:S(2)}) async-start(bf16[1024,1536]{1,0:T(8,128)(2,1)} %convolution_convert_fusion), calls=%async_computation.2 | async-start | bytes 4194304 | tf_op jit(solution)/shard_map/slice | solution.py:66
  24.0 44.2 %all-to-all-start.1 = ((bf16[8,32,512]{2,1,0:T(8,128)(2,1)}), bf16[8,32,512]{2,1,0:T(8,128)(2,1)S(1)}, u32[]{:S(2)}, u32[]{:S(2)}) async-start(bf16[8,32,512]{2,1,0:T(8,128)(2,1)} %bitcast.3), calls=%async_computation.1 | async-start | bytes 524288 | tf_op jit(solution)/shard_map/all_to_all | solution.py:70
  43.9 4.7 %copy-start.2 = (bf16[4,256,16,32]{1,0,3,2:T(4,128)(2,1)S(1)}, bf16[4,256,16,32]{1,0,3,2:T(4,128)(2,1)}, u32[]{:S(2)}) copy-start(bf16[4,256,16,32]{1,0,3,2:T(4,128)(2,1)} %reshape.81) | copy-start | bytes 3145732
  48.6 10.2 %copy-start.4 = (bf16[4,256,16,32]{1,0,3,2:T(4,128)(2,1)S(1)}, bf16[4,256,16,32]{1,0,3,2:T(4,128)(2,1)}, u32[]{:S(2)}) copy-start(bf16[4,256,16,32]{1,0,3,2:T(4,128)(2,1)} %reshape.80) | copy-start | bytes 3145732
  66.1 4.0 %copy-start.6 = (f32[512]{0:T(512)S(1)}, f32[512]{0:T(512)}, u32[]{:S(2)}) copy-start(f32[512]{0:T(512)} %param.14) | copy-start | bytes 6148
  79.1 1.2 %copy-start.1 = (bf16[1024,512]{1,0:T(8,128)(2,1)S(1)}, bf16[1024,512]{1,0:T(8,128)(2,1)}, u32[]{:S(2)}) copy-start(bf16[1024,512]{1,0:T(8,128)(2,1)} %param.9) | copy-start | bytes 3145732
  79.1 1.5 %copy-start.3 = (bf16[64,8,4,256]{3,1,2,0:T(8,128)(2,1)S(1)}, bf16[64,8,4,256]{3,1,2,0:T(8,128)(2,1)}, u32[]{:S(2)}) copy-start(bf16[64,8,4,256]{3,1,2,0:T(8,128)(2,1)} %copy.60) | copy-start | bytes 3145732
where the time goes:
time: 83.6 us; the launch traced here: 82.9 us
  matrix products  31.6 us (38%)
  local copies, waits for them, and re-layouts  26.8 us (32%)
  starting transfers between devices  15.3 us (18%)
  other arithmetic  9.01 us (11%)
    sub x1, matrix products, attend(): powers = jnp.exp(scores - highest)  10.2 us
    dot_general x2, matrix products, attend(): jnp.einsum('whrs,wshe->wrhe', weights, value_heads, preferred_element_typ...  9.92 us
    gather x1, local copies, waits for them, and re-layouts, on_device(): window_kv = jnp.take(extended, local_index, axis=0)  7.05 us
    all_to_all x1, starting transfers between devices, on_device(): lax.all_to_all(parent_tokens, 'pix', split_axis=0, concat_axis=0, tiled=T...  6 us
    dot_general x1, matrix products, on_device(): jnp.dot(normed, w_qkv, preferred_element_type=jnp.float32)  4.87 us
    all_to_all x1, starting transfers between devices, on_device(): lax.all_to_all(parent_slot, 'pix', split_axis=0, concat_axis=0, tiled=True)  3.3 us
    ppermute x1, starting transfers between devices, with_halo(): lax.ppermute(head, axis, [((i + 1) % count, i) for i in range(count)])  3.04 us
    sub x1, other arithmetic, attend(): powers = jnp.exp(scores - highest)  2.98 us
  transfers between devices with their start and end apart: 4, of which 0 were waited for; matrix products, arithmetic and copies ran while one was open for 57% of the time, Pallas kernels for 0%

commit v1 on v0

v1 whole, which is shorter than its diff:
```python
import functools
import math

import jax
import jax.numpy as jnp
from jax import lax
from jax.experimental import pallas as pl
from jax.experimental.pallas import tpu as pltpu
from jax.sharding import PartitionSpec as P

HEADS = 16
WIN = 256
HALO = 128
PWIN = 64
LANES = 128
F32 = jnp.float32
BF16 = jnp.bfloat16
VMEM = pl.BlockSpec(memory_space=pltpu.VMEM)


def mm(a, b, dims=((1,), (0,))):
    return lax.dot_general(a, b, (dims, ((), ())), preferred_element_type=F32)


def rms_rows(matrix, gain):
    values = matrix.astype(F32)
    factor = lax.rsqrt(jnp.mean(values * values, axis=-1, keepdims=True) + 1e-06)
    return (values * factor * gain).astype(BF16)


def softmax_down(scores, scale, groups):
    rows, cols = scores.shape
    scores = scores.reshape(groups, rows // groups, cols)
    highest = jnp.max(scores, axis=1, keepdims=True)
    powers = jnp.exp2((scores - highest) * scale)
    weights = powers * (1.0 / jnp.sum(powers, axis=1, keepdims=True))
    return weights.astype(BF16).reshape(rows, cols)


def column_of(row):
    wide = jnp.broadcast_to(row, (LANES, row.shape[1]))
    return jnp.concatenate(
        [wide[:, k : k + LANES].T for k in range(0, row.shape[1], LANES)], axis=0
    )


def one_hot_rows(row, base, width):
    column = column_of(row) - base
    lane = lax.broadcasted_iota(jnp.int32, column.shape, 1)
    return jnp.concatenate(
        [jnp.where(column == lane + k, 1.0, 0.0).astype(BF16) for k in range(0, width, LANES)], axis=1
    )


def self_attention(span, picks, query_t, w_kv, wv_t, head_size, store):
    features = span.shape[1]
    scale = math.log2(math.e) / math.sqrt(head_size)
    gathered = mm(picks, span).astype(BF16)
    keys = mm(gathered, w_kv[:, :features]).astype(BF16)
    values_t = mm(wv_t, gathered, ((1,), (1,))).astype(BF16)
    per_tile = LANES // head_size
    cols = query_t.shape[1]
    for head in range(features // head_size):
        tile, inside = head // per_tile, head % per_tile
        rows = query_t[head * head_size : (head + 1) * head_size]
        parts = []
        if inside:
            parts.append(jnp.zeros((inside * head_size, cols), BF16))
        parts.append(rows)
        if inside < per_tile - 1:
            parts.append(jnp.zeros(((per_tile - 1 - inside) * head_size, cols), BF16))
        scores = mm(keys[:, tile * LANES : (tile + 1) * LANES], jnp.concatenate(parts, axis=0))
        weights = softmax_down(scores, scale, 1)
        store(head, mm(values_t[head * head_size : (head + 1) * head_size], weights).astype(BF16))


def local_kernel(fine, index, gain, w_qkv, normed_out, query_out, self_out, wv_out, *, windows, head_size):
    rows, features = fine.shape
    wv_out[...] = w_qkv[:, 2 * features :].T
    wq_t = w_qkv[:, :features].T
    for w in range(windows):
        normed_out[w * WIN : (w + 1) * WIN] = rms_rows(fine[w * WIN : (w + 1) * WIN], gain[...])
    for w in range(windows):
        query_out[w] = mm(wq_t, normed_out[w * WIN : (w + 1) * WIN], ((1,), (1,))).astype(BF16)

    def window(w, carry):
        span = normed_out[pl.ds(pl.multiple_of(w * WIN - HALO, HALO), WIN + 2 * HALO)]
        picks = one_hot_rows(index[w], w * WIN, WIN + 2 * HALO)

        def store(head, value):
            self_out[w - 1, head * head_size : (head + 1) * head_size] = value

        self_attention(span, picks, query_out[w], w_qkv[:, features:], wv_out[...], head_size, store)
        return carry

    lax.fori_loop(1, windows - 1, window, 0)


def edge_kernel(
    fine, normed, query, self_in, wv_t, before, after, index, parents, slots, gain, parent_gain, w_qkv, w_parent,
    w_out, out, ends, self_all, p_keys, p_values, *, windows, head_size,
):
    rows, features = fine.shape
    span_rows = WIN + 2 * HALO
    ends[0, :HALO] = rms_rows(before[...], gain[...])
    ends[0, HALO:] = normed[: span_rows - HALO]
    ends[1, : span_rows - HALO] = normed[rows - (span_rows - HALO) :]
    ends[1, span_rows - HALO :] = rms_rows(after[...], gain[...])
    self_all[1 : windows - 1] = self_in[...]

    count = parents.shape[0]
    place = lax.broadcasted_iota(jnp.int32, (count, count), 0)
    picks = jnp.where(place == jnp.broadcast_to(slots[...], (count, count)), 1.0, 0.0).astype(BF16)
    ordered = mm(picks, parents[...]).astype(BF16)
    normed_parents = rms_rows(ordered, parent_gain[...])
    p_keys[...] = mm(normed_parents, w_parent[:, :features]).astype(BF16)
    p_values[...] = mm(normed_parents, w_parent[:, features:]).astype(BF16)

    def edge(e, carry):
        w = e * (windows - 1)
        picks = one_hot_rows(index[w], w * WIN, span_rows)

        def store(head, value):
            self_all[w, head * head_size : (head + 1) * head_size] = value

        self_attention(ends[e], picks, query[w], w_qkv[:, features:], wv_t[...], head_size, store)
        return carry

    lax.fori_loop(0, 2, edge, 0)

    scale = math.log2(math.e) / math.sqrt(head_size)
    per_tile = LANES // head_size
    lane_head = lax.broadcasted_iota(jnp.int32, (per_tile * PWIN, LANES), 1) // head_size
    row_head = lax.broadcasted_iota(jnp.int32, (per_tile * PWIN, LANES), 0) // PWIN
    own = lane_head == row_head

    def finish(w, carry):
        own_rows = pl.ds(pl.multiple_of(w * PWIN, PWIN), PWIN)
        keys, values = p_keys[own_rows], p_values[own_rows]
        crossed = []
        for tile in range(features // LANES):
            lanes = slice(tile * LANES, (tile + 1) * LANES)
            spread = jnp.where(own, jnp.concatenate([keys[:, lanes]] * per_tile, axis=0), 0)
            scores = mm(spread, query[w, lanes])
            weights = softmax_down(scores, scale, per_tile)
            spread = jnp.where(own, jnp.concatenate([values[:, lanes]] * per_tile, axis=0), 0)
            crossed.append(mm(spread, weights, ((0,), (0,))).astype(BF16))
        here = pl.ds(pl.multiple_of(w * WIN, WIN), WIN)
        branch = mm(self_all[w], w_out[:features], ((0,), (0,)))
        branch += mm(jnp.concatenate(crossed, axis=0), w_out[features:], ((0,), (0,)))
        out[here] = (fine[here].astype(F32) + branch).astype(BF16)
        return carry

    lax.fori_loop(0, windows, finish, 0)


def on_device(
    fine_tokens, parent_tokens, shift_table, parent_slot, fine_gain, parent_gain, w_qkv, w_parent, w_out,
):
    rows, features = fine_tokens.shape
    devices = lax.axis_size("pix")
    windows = rows // WIN
    head_size = features // HEADS
    offset = lax.axis_index("pix") * rows
    index = jnp.mod(shift_table - offset + HALO, rows * devices).reshape(windows, 1, WIN)
    ring = [(i, (i + 1) % devices) for i in range(devices)]
    before = lax.ppermute(fine_tokens[rows - HALO :], "pix", ring)
    after = lax.ppermute(fine_tokens[:HALO], "pix", [(j, i) for i, j in ring])
    arrived = lax.all_to_all(parent_tokens, "pix", split_axis=0, concat_axis=0, tiled=True)
    slots = lax.all_to_all(parent_slot, "pix", split_axis=0, concat_axis=0, tiled=True)
    gain = fine_gain.reshape(1, features)
    params = pltpu.CompilerParams(vmem_limit_bytes=48 * 1024 * 1024)

    normed, query, inner, wv_t = pl.pallas_call(
        functools.partial(local_kernel, windows=windows, head_size=head_size),
        out_shape=[
            jax.ShapeDtypeStruct((rows, features), BF16),
            jax.ShapeDtypeStruct((windows, features, WIN), BF16),
            jax.ShapeDtypeStruct((windows - 2, features, WIN), BF16),
            jax.ShapeDtypeStruct((features, features), BF16),
        ],
        in_specs=[VMEM] * 4,
        out_specs=[VMEM] * 4,
        compiler_params=params,
        cost_estimate=pl.CostEstimate(flops=8 * 10**9, bytes_accessed=4 * 10**6, transcendentals=2 * 10**6),
        name="local",
    )(fine_tokens, index, gain, w_qkv)

    return pl.pallas_call(
        functools.partial(edge_kernel, windows=windows, head_size=head_size),
        out_shape=jax.ShapeDtypeStruct((rows, features), BF16),
        in_specs=[VMEM] * 15,
        out_specs=VMEM,
        scratch_shapes=[
            pltpu.VMEM((2, WIN + 2 * HALO, features), BF16),
            pltpu.VMEM((windows, features, WIN), BF16),
            pltpu.VMEM((parent_tokens.shape[0], features), BF16),
            pltpu.VMEM((parent_tokens.shape[0], features), BF16),
        ],
        compiler_params=params,
        cost_estimate=pl.CostEstimate(flops=10 * 10**9, bytes_accessed=6 * 10**6, transcendentals=3 * 10**6),
        name="edges",
    )(
        fine_tokens, normed, query, inner, wv_t, before, after, index, arrived, slots.reshape(1, -1), gain,
        parent_gain.reshape(1, features), w_qkv, w_parent, w_out,
    )


def solution(mesh):
    return jax.shard_map(
        on_device,
        mesh=mesh,
        in_specs=(P(("batch", "pix"), None), P(("batch", "pix"), None), P("pix"), P("pix"), P(), P(), P(), P(), P()),
        out_specs=P(("batch", "pix"), None),
        check_vma=False,
    )
```

time: 83.6 us -> 65.4 us (0.78)
  Pallas kernels: 0 us -> 32.7 us
  matrix products: 31.6 us -> 0 us
  local copies, waits for them, and re-layouts: 26.8 us -> 12.6 us
  other arithmetic: 9.01 us -> 1.33 us
  starting transfers between devices: 15.3 us -> 18.1 us
    pallas_call x0 -> x2, Pallas kernels: none -> 32.7 us  [the longest x1 20.9 us: on_device(): pl.pallas_call(functools.partial(edge_kernel, windows=windows, head_size=...]
    dot_general x7 -> x0, matrix products: 21.3 us -> none  [the longest x2 9.92 us: attend(): jnp.einsum('whrs,wshe->wrhe', weights, value_heads, preferred_element_typ...]
    sub x1 -> x0, matrix products: 10.2 us -> none  [attend(): powers = jnp.exp(scores - highest)]
    unnamed x18 -> x26, local copies, waits for them, and re-layouts: 1.84 us -> 9.6 us
    gather x1 -> x0, local copies, waits for them, and re-layouts: 7.05 us -> none  [on_device(): window_kv = jnp.take(extended, local_index, axis=0)]
    reshape x5 -> x1, local copies, waits for them, and re-layouts: 6.43 us -> 0.08 us  [on_device(): slots.reshape(1, -1)]
    slice x13 -> x1, local copies, waits for them, and re-layouts: 6.64 us -> 0.98 us  [on_device(): after = lax.ppermute(fine_tokens[:HALO], 'pix', [(j, i) for i, j in ring])]
    all_to_all x1, starting transfers between devices: 3.3 us -> 7.28 us  [on_device(): lax.all_to_all(parent_slot, 'pix', split_axis=0, concat_axis=0, tiled=True)]
  transfers between devices with their start and end apart: 4 -> 4, of which waited for: 0 -> 0; matrix products, arithmetic and copies ran while one was open for 57% -> 5% of each run, Pallas kernels for 0% -> 18%
where the time goes in v1:
time: 65.4 us; the launch traced here: 64.8 us
  Pallas kernels  32.7 us (50%)
  starting transfers between devices  18.1 us (28%)
  local copies, waits for them, and re-layouts  12.6 us (19%)
  other arithmetic  1.33 us (2%)
    pallas_call x1, Pallas kernels, on_device(): pl.pallas_call(functools.partial(edge_kernel, windows=windows, head_size=...  20.9 us
    pallas_call x1, Pallas kernels, on_device(): pl.pallas_call(functools.partial(local_kernel, windows=windows, head_size...  11.8 us
    unnamed x26, local copies, waits for them, and re-layouts  9.6 us
    all_to_all x1, starting transfers between devices, on_device(): lax.all_to_all(parent_slot, 'pix', split_axis=0, concat_axis=0, tiled=True)  7.28 us
    all_to_all x1, starting transfers between devices, on_device(): lax.all_to_all(parent_tokens, 'pix', split_axis=0, concat_axis=0, tiled=T...  6.01 us
    ppermute x1, starting transfers between devices, on_device(): after = lax.ppermute(fine_tokens[:HALO], 'pix', [(j, i) for i, j in ring])  4.77 us
    all_to_all x2, local copies, waits for them, and re-layouts, on_device(): lax.all_to_all(parent_slot, 'pix', split_axis=0, concat_axis=0, tiled=True)  1.92 us
  transfers between devices with their start and end apart: 4, of which 0 were waited for; matrix products, arithmetic and copies ran while one was open for 5% of the time, Pallas kernels for 18%

profile of v1, /device:TPU:0, one launch (start us, length us, event | category | flops | bytes accessed | tf_op | source)
XLA Modules:
  0.0 64.8 jit_solution(1562364308115912741)
XLA Ops:
  0.0 1.4 %all_to_all.16 = s32[8,32,1]{1,2,0:T(1,128)} reshape(s32[256]{0:T(256)} %param.12) | data formatting | bytes 2048 | tf_op jit(solution)/shard_map/all_to_all | solution.py:170
  1.4 7.3 %all-to-all-start.1 = ((s32[8,32,1]{1,2,0:T(1,128)}), s32[8,32,1]{1,2,0:T(1,128)S(1)}, u32[]{:S(2)}, u32[]{:S(2)}) async-start(s32[8,32,1]{1,2,0:T(1,128)} %all_to_all.16), calls=%async_computation.1 | async-start | bytes 8192 | tf_op jit(solution)/shard_map/all_to_all | solution.py:170
  8.6 1.0 %fusion.1 = (bf16[128,512]{1,0:T(8,128)(2,1)S(1)}, bf16[128,512]{1,0:T(8,128)(2,1)S(1)}) fusion(bf16[1024,512]{1,0:T(8,128)(2,1)} %fine.3), kind=kLoop, calls=%fused_computation.4 | loop fusion | bytes 524288 | tf_op jit(solution)/shard_map/slice | solution.py:168
  9.6 4.8 %collective-permute-start.1 = (bf16[128,512]{1,0:T(8,128)(2,1)S(1)}, bf16[128,512]{1,0:T(8,128)(2,1)S(1)}, u32[]{:S(2)}, u32[]{:S(2)}) collective-permute-start(bf16[128,512]{1,0:T(8,128)(2,1)S(1)} %get-tuple-element.13), channel_id=1, source_target_pairs={{4,0},{8,4},{12,8},{16,12},{20,16},{24,20},{28,24},{0,28},{5,1},{9... | collective-permute-start | bytes 393224 | tf_op jit(solution)/shard_map/ppermute | solution.py:168
  14.4 0.0 collective-permute-start
  14.4 0.7 %add_select_fusion = s32[1024]{0:T(1024)S(1)} fusion(s32[1024]{0:T(1024)} %param.11, s32[]{:T(128)S(6)} %mul.3), kind=kLoop, calls=%fused_computation | loop fusion | flops 13312 | bytes 8196 | tf_op jit(solution)/shard_map/jit(remainder)/select_n | solution.py:165
  15.1 0.0 all-to-all-done.1
  15.1 6.0 %all-to-all-start = ((bf16[8,32,512]{2,1,0:T(8,128)(2,1)}), bf16[8,32,512]{2,1,0:T(8,128)(2,1)S(1)}, u32[]{:S(2)}, u32[]{:S(2)}) async-start(bf16[8,32,512]{2,1,0:T(8,128)(2,1)} %bitcast.12), calls=%async_computation | async-start | bytes 524288 | tf_op jit(solution)/shard_map/all_to_all | solution.py:169
  21.1 0.0 copy-start
  21.1 1.2 %copy-done = bf16[1024,512]{1,0:T(8,128)(2,1)S(1)} copy-done((bf16[1024,512]{1,0:T(8,128)(2,1)S(1)}, bf16[1024,512]{1,0:T(8,128)(2,1)}, u32[]{:S(2)}) %copy-start) | copy-done | bytes 1048600
  22.3 0.0 copy-start.2
  22.3 1.4 %copy-done.2 = bf16[512,1536]{1,0:T(8,128)(2,1)S(1)} copy-done((bf16[512,1536]{1,0:T(8,128)(2,1)S(1)}, bf16[512,1536]{1,0:T(8,128)(2,1)}, u32[]{:S(2)}) %copy-start.2) | copy-done | bytes 1572888
  23.7 0.7 %copy-done.4 = f32[512]{0:T(512)S(1)} copy-done((f32[512]{0:T(512)S(1)}, f32[512]{0:T(512)}, u32[]{:S(2)}) %copy-start.4) | copy-done | bytes 2072
  24.4 11.8 %local.1 = (bf16[1024,512]{1,0:T(8,128)(2,1)S(1)}, bf16[4,512,256]{2,1,0:T(8,128)(2,1)S(1)}, bf16[2,512,256]{2,1,0:T(8,128)(2,1)S(1)}, bf16[512,512]{1,0:T(8,128)(2,1)S(1)}) custom-call(bf16[1024,512]{1,0:T(8,128)(2,1)S(1)} %copy-done, s32[4,1,256]{2,1,0:T(1,128)S(1)} %bitcast.7, f32[1,512]{1,0:T(1,128)S(1)} %bitcast.9, bf16[512,1536]{1,0:T(8,128)(2,1)S(1)} %copy-done.2), custom_call_target="tpu_custom_call" | custom-call | flops 8000000000 | bytes 4000000 | tf_op jit(solution)/shard_map/local/pallas_call | solution.py:174
  36.3 1.0 %copy-done.7 = bf16[1024,512]{1,0:T(8,128)(2,1)} copy-done((bf16[1024,512]{1,0:T(8,128)(2,1)}, bf16[1024,512]{1,0:T(8,128)(2,1)S(1)}, u32[]{:S(2)}) %copy-start.7) | copy-done | bytes 1048600
  37.3 1.0 %copy-done.9 = bf16[4,512,256]{2,1,0:T(8,128)(2,1)} copy-done((bf16[4,512,256]{2,1,0:T(8,128)(2,1)}, bf16[4,512,256]{2,1,0:T(8,128)(2,1)S(1)}, u32[]{:S(2)}) %copy-start.9) | copy-done | bytes 1048600
  38.2 0.8 %copy-done.11 = bf16[512,512]{1,0:T(8,128)(2,1)} copy-done((bf16[512,512]{1,0:T(8,128)(2,1)}, bf16[512,512]{1,0:T(8,128)(2,1)S(1)}, u32[]{:S(2)}) %copy-start.11) | copy-done | bytes 524312
  39.1 0.6 broadcast.11
  39.6 0.6 reduce.3
  40.3 0.1 reshape.19.slots
  40.3 0.0 collective-permute-done.1.after
  40.4 0.0 collective-permute-done.before
  40.4 0.0 all-to-all-done
  40.4 0.0 copy-done.1
  40.4 0.0 copy-done.3
  40.4 0.0 copy-done.5
  40.4 0.0 copy-done.6
  40.4 0.0 copy-start.8
  40.4 1.2 %copy-done.8 = bf16[1024,512]{1,0:T(8,128)(2,1)S(1)} copy-done((bf16[1024,512]{1,0:T(8,128)(2,1)S(1)}, bf16[1024,512]{1,0:T(8,128)(2,1)}, u32[]{:S(2)}) %copy-start.8) | copy-done | bytes 1048600
  41.6 1.2 %copy-done.10 = bf16[4,512,256]{2,1,0:T(8,128)(2,1)S(1)} copy-done((bf16[4,512,256]{2,1,0:T(8,128)(2,1)S(1)}, bf16[4,512,256]{2,1,0:T(8,128)(2,1)}, u32[]{:S(2)}) %copy-start.10) | copy-done | bytes 1048600
  42.9 1.0 %copy-done.12 = bf16[512,512]{1,0:T(8,128)(2,1)S(1)} copy-done((bf16[512,512]{1,0:T(8,128)(2,1)S(1)}, bf16[512,512]{1,0:T(8,128)(2,1)}, u32[]{:S(2)}) %copy-start.12) | copy-done | bytes 524312
  43.9 20.9 %edges.1 = bf16[1024,512]{1,0:T(8,128)(2,1)} custom-call(bf16[1024,512]{1,0:T(8,128)(2,1)S(1)} %copy-done.1, bf16[1024,512]{1,0:T(8,128)(2,1)S(1)} %copy-done.8, bf16[4,512,256]{2,1,0:T(8,128)(2,1)S(1)} %copy-done.10, bf16[2,512,256]{2,1,0:T(8,128)(2,1)S(1)} %get-tuple-element.11.self_in, bf16[512,512]{1,0:T(8,128)(2,1)S(1)} %copy-done.12, ...), custom_call_target="tpu_custom_call" | custom-call | flops 10000000000 | bytes 6000000 | tf_op jit(solution)/shard_map/edges/pallas_call | solution.py:189
  (10 shorter events, 0.0 us)
Async XLA Ops:
  1.4 13.7 %all-to-all-start.1 = ((s32[8,32,1]{1,2,0:T(1,128)}), s32[8,32,1]{1,2,0:T(1,128)S(1)}, u32[]{:S(2)}, u32[]{:S(2)}) async-start(s32[8,32,1]{1,2,0:T(1,128)} %all_to_all.16), calls=%async_computation.1 | async-start | bytes 8192 | tf_op jit(solution)/shard_map/all_to_all | solution.py:170
  9.6 30.7 %collective-permute-start.1 = (bf16[128,512]{1,0:T(8,128)(2,1)S(1)}, bf16[128,512]{1,0:T(8,128)(2,1)S(1)}, u32[]{:S(2)}, u32[]{:S(2)}) collective-permute-start(bf16[128,512]{1,0:T(8,128)(2,1)S(1)} %get-tuple-element.13), channel_id=1, source_target_pairs={{4,0},{8,4},{12,8},{16,12},{20,16},{24,20},{28,24},{0,28},{5,1},{9... | collective-permute-start | bytes 393224 | tf_op jit(solution)/shard_map/ppermute | solution.py:168
  14.4 26.0 %collective-permute-start = (bf16[128,512]{1,0:T(8,128)(2,1)S(1)}, bf16[128,512]{1,0:T(8,128)(2,1)S(1)}, u32[]{:S(2)}, u32[]{:S(2)}) collective-permute-start(bf16[128,512]{1,0:T(8,128)(2,1)S(1)} %get-tuple-element.14), channel_id=1, source_target_pairs={{0,4},{4,8},{8,12},{12,16},{16,20},{20,24},{24,28},{28,0},{1,5},{5... | collective-permute-start | bytes 393224 | tf_op jit(solution)/shard_map/ppermute | solution.py:167
  15.1 25.3 %all-to-all-start = ((bf16[8,32,512]{2,1,0:T(8,128)(2,1)}), bf16[8,32,512]{2,1,0:T(8,128)(2,1)S(1)}, u32[]{:S(2)}, u32[]{:S(2)}) async-start(bf16[8,32,512]{2,1,0:T(8,128)(2,1)} %bitcast.12), calls=%async_computation | async-start | bytes 524288 | tf_op jit(solution)/shard_map/all_to_all | solution.py:169
  21.1 1.2 %copy-start = (bf16[1024,512]{1,0:T(8,128)(2,1)S(1)}, bf16[1024,512]{1,0:T(8,128)(2,1)}, u32[]{:S(2)}) copy-start(bf16[1024,512]{1,0:T(8,128)(2,1)} %fine.3) | copy-start | bytes 3145732
  22.3 1.4 %copy-start.2 = (bf16[512,1536]{1,0:T(8,128)(2,1)S(1)}, bf16[512,1536]{1,0:T(8,128)(2,1)}, u32[]{:S(2)}) copy-start(bf16[512,1536]{1,0:T(8,128)(2,1)} %w_qkv.3) | copy-start | bytes 4718596
  23.7 0.7 %copy-start.4 = (f32[512]{0:T(512)S(1)}, f32[512]{0:T(512)}, u32[]{:S(2)}) copy-start(f32[512]{0:T(512)} %param.13) | copy-start | bytes 6148
  24.4 15.9 %copy-start.1 = (bf16[1024,512]{1,0:T(8,128)(2,1)S(1)}, bf16[1024,512]{1,0:T(8,128)(2,1)}, u32[]{:S(2)}) copy-start(bf16[1024,512]{1,0:T(8,128)(2,1)} %fine.3) | copy-start | bytes 3145732
  24.4 15.9 %copy-start.3 = (bf16[512,1024]{1,0:T(8,128)(2,1)S(1)}, bf16[512,1024]{1,0:T(8,128)(2,1)}, u32[]{:S(2)}) copy-start(bf16[512,1024]{1,0:T(8,128)(2,1)} %w_parent.1) | copy-start | bytes 3145732
  24.4 16.0 %copy-start.5 = (f32[512]{0:T(512)S(1)}, f32[512]{0:T(512)}, u32[]{:S(2)}) copy-start(f32[512]{0:T(512)} %param.13) | copy-start | bytes 6148
  24.4 16.0 %copy-start.6 = (f32[512]{0:T(512)S(1)}, f32[512]{0:T(512)}, u32[]{:S(2)}) copy-start(f32[512]{0:T(512)} %param.14) | copy-start | bytes 6148
  36.3 1.0 %copy-start.7 = (bf16[1024,512]{1,0:T(8,128)(2,1)}, bf16[1024,512]{1,0:T(8,128)(2,1)S(1)}, u32[]{:S(2)}) copy-start(bf16[1024,512]{1,0:T(8,128)(2,1)S(1)} %get-tuple-element.9.normed) | copy-start | bytes 3145732
  37.3 1.0 %copy-start.9 = (bf16[4,512,256]{2,1,0:T(8,128)(2,1)}, bf16[4,512,256]{2,1,0:T(8,128)(2,1)S(1)}, u32[]{:S(2)}) copy-start(bf16[4,512,256]{2,1,0:T(8,128)(2,1)S(1)} %get-tuple-element.10.query) | copy-start | bytes 3145732
  38.2 0.8 %copy-start.11 = (bf16[512,512]{1,0:T(8,128)(2,1)}, bf16[512,512]{1,0:T(8,128)(2,1)S(1)}, u32[]{:S(2)}) copy-start(bf16[512,512]{1,0:T(8,128)(2,1)S(1)} %get-tuple-element.12.wv_t) | copy-start | bytes 1572868
  40.4 1.2 %copy-start.8 = (bf16[1024,512]{1,0:T(8,128)(2,1)S(1)}, bf16[1024,512]{1,0:T(8,128)(2,1)}, u32[]{:S(2)}) copy-start(bf16[1024,512]{1,0:T(8,128)(2,1)} %copy-done.7) | copy-start | bytes 3145732
  41.6 1.2 %copy-start.10 = (bf16[4,512,256]{2,1,0:T(8,128)(2,1)S(1)}, bf16[4,512,256]{2,1,0:T(8,128)(2,1)}, u32[]{:S(2)}) copy-start(bf16[4,512,256]{2,1,0:T(8,128)(2,1)} %copy-done.9) | copy-start | bytes 3145732
  42.9 1.0 %copy-start.12 = (bf16[512,512]{1,0:T(8,128)(2,1)S(1)}, bf16[512,512]{1,0:T(8,128)(2,1)}, u32[]{:S(2)}) copy-start(bf16[512,512]{1,0:T(8,128)(2,1)} %copy-done.11) | copy-start | bytes 1572868

commit v2 on v1

v2 whole, which is shorter than its diff:
```python
import functools
import math

import jax
import jax.numpy as jnp
from jax import lax
from jax.experimental import pallas as pl
from jax.experimental.pallas import tpu as pltpu
from jax.sharding import PartitionSpec as P

HEADS = 16
WIN = 256
HALO = 128
PWIN = 64
LANES = 128
SPAN = WIN + 2 * HALO
F32 = jnp.float32
BF16 = jnp.bfloat16
VMEM = pl.BlockSpec(memory_space=pltpu.VMEM)
HBM = pl.BlockSpec(memory_space=pltpu.HBM)
MIB = 1024 * 1024
NN, NT, TN = ((1,), (0,)), ((1,), (1,)), ((0,), (0,))


def mm(a, b, dims=NN):
    return lax.dot_general(a, b, (dims, ((), ())), preferred_element_type=F32)


def rms_rows(matrix, gain):
    values = matrix.astype(F32)
    factor = lax.rsqrt(jnp.mean(values * values, axis=-1, keepdims=True) + 1e-06)
    return (values * factor * gain).astype(BF16)


def softmax_down(scores, scale):
    powers = jnp.exp2((scores - jnp.max(scores, axis=0, keepdims=True)) * scale)
    return (powers * (1.0 / jnp.sum(powers, axis=0, keepdims=True))).astype(BF16)


def column_of(row):
    wide = jnp.broadcast_to(row, (LANES, row.shape[1]))
    return jnp.concatenate([wide[:, k : k + LANES].T for k in range(0, row.shape[1], LANES)], axis=0)


def one_hot(column, width):
    lane = lax.broadcasted_iota(jnp.int32, column.shape, 1)
    return jnp.concatenate(
        [jnp.where(column == lane + k, 1.0, 0.0).astype(BF16) for k in range(0, width, LANES)], axis=1
    )


def spread(rows, head_size):
    lane = lax.broadcasted_iota(jnp.int32, rows.shape, 1) // head_size
    return jnp.concatenate([jnp.where(lane == k, rows, 0) for k in range(LANES // head_size)], axis=0)


def gather_kv(span, row, base, w_key, w_value):
    gathered = mm(one_hot(column_of(row) - base, SPAN), span).astype(BF16)
    return mm(gathered, w_key).astype(BF16), mm(gathered, w_value).astype(BF16).T


def self_attention(keys, values_t, query, head_size, store):
    features = query.shape[1]
    scale = math.log2(math.e) / math.sqrt(head_size)
    tiles = [slice(k, k + LANES) for k in range(0, features, LANES)]
    scores = [mm(spread(keys[:, tile], head_size), query[:, tile], NT) for tile in tiles]
    count = keys.shape[0]
    per_tile = LANES // head_size
    for head in range(features // head_size):
        part = (head % per_tile) * count
        weights = softmax_down(scores[head // per_tile][part : part + count], scale)
        store(head, mm(values_t[head * head_size : (head + 1) * head_size], weights).astype(BF16))


def cross_attention(keys, values, query, head_size):
    scale = math.log2(math.e) / math.sqrt(head_size)
    per_tile = LANES // head_size
    tiles = [slice(k, k + LANES) for k in range(0, query.shape[1], LANES)]
    scores = [mm(spread(keys[:, tile], head_size), query[:, tile], NT) for tile in tiles]
    out = []
    for tile, score in zip(tiles, scores):
        weights = [softmax_down(score[k * PWIN : (k + 1) * PWIN], scale) for k in range(per_tile)]
        out.append(mm(spread(values[:, tile], head_size), jnp.concatenate(weights, axis=0), TN).astype(BF16))
    return jnp.concatenate(out, axis=0)


def block(w, size):
    return pl.ds(pl.multiple_of(w * size, size), size)


def pack_kernel(fine, parents, slots, first, second, packed, parents_s, slots_s, sems):
    rows, features = fine.shape
    odd = lax.rem(lax.axis_index("pix"), 2)
    ends = rows - HALO
    pieces = [
        (slots, slots_s),
        (parents, parents_s),
        (fine.at[pl.ds(pl.multiple_of((1 - odd) * ends, HALO), HALO)], first),
        (fine.at[pl.ds(pl.multiple_of(odd * ends, HALO), HALO)], second),
    ]
    copies = [pltpu.make_async_copy(src, dst, sems.at[k]) for k, (src, dst) in enumerate(pieces)]
    for copy in copies:
        copy.start()
    copies[0].wait()
    packed[:, features:] = column_of(slots_s[...]).astype(F32).astype(BF16)
    copies[1].wait()
    packed[:, :features] = parents_s[...]
    copies[2].wait()
    copies[3].wait()


def local_kernel(
    fine, w_qkv, index, gain, query, inner, fine_s, w_s, index_s, gain_s, normed, query_s, inner_s, sems,
    *, windows, head_size,
):
    rows, features = fine.shape
    small = [
        pltpu.make_async_copy(gain, gain_s, sems.at[0]),
        pltpu.make_async_copy(index, index_s, sems.at[1]),
    ]
    weigh = [
        pltpu.make_async_copy(w_qkv.at[:, c * features : (c + 1) * features], w_s.at[c], sems.at[2 + c])
        for c in range(3)
    ]
    fetch = [
        pltpu.make_async_copy(fine.at[w * WIN : (w + 1) * WIN], fine_s.at[w], sems.at[5 + w]) for w in range(windows)
    ]
    for copy in small + fetch + weigh:
        copy.start()
    for copy in small:
        copy.wait()
    for w, copy in enumerate(fetch):
        copy.wait()
        normed[w * WIN : (w + 1) * WIN] = rms_rows(fine_s[w], gain_s[...])
    for copy in weigh:
        copy.wait()
    query_s[...] = mm(normed[WIN : rows - WIN], w_s[0]).astype(BF16)
    queries = pltpu.make_async_copy(query_s, query, sems.at[5 + windows])
    queries.start()

    def window(i, carry):
        w = i + 1
        span = normed[pl.ds(pl.multiple_of(w * WIN - HALO, HALO), SPAN)]
        keys, values_t = gather_kv(span, index_s[w], w * WIN, w_s[1], w_s[2])

        def store(head, value):
            inner_s[i, head * head_size : (head + 1) * head_size] = value

        self_attention(keys, values_t, query_s[block(i, WIN)], head_size, store)
        pltpu.make_async_copy(inner_s.at[i], inner.at[i], sems.at[6 + windows]).start()
        return carry

    lax.fori_loop(0, windows - 2, window, 0)
    queries.wait()
    pltpu.make_async_copy(inner_s, inner, sems.at[6 + windows]).wait()


def edge_kernel(
    fine, query, inner, first, second, index, arrived, gain, parent_gain, w_qkv, w_parent, w_out,
    out, fine_s, query_s, inner_s, near_s, index_s, arrived_s, gain_s, w_s, wp_s, wo_s,
    out_s, spans, query_e, edge_self, p_keys, p_values, sems, *, windows, head_size,
):
    rows, features = fine.shape
    pieces = [
        (gain, gain_s.at[0]),
        (parent_gain, gain_s.at[1]),
        (arrived, arrived_s),
        (first, near_s.at[0]),
        (second, near_s.at[1]),
        (index, index_s),
        (fine, fine_s),
        (w_parent, wp_s),
        (w_qkv.at[:, :features], w_s.at[0]),
        (w_qkv.at[:, features : 2 * features], w_s.at[1]),
        (w_qkv.at[:, 2 * features :], w_s.at[2]),
        (query, query_s),
        (w_out, wo_s),
        (inner, inner_s),
    ]
    fetch = [pltpu.make_async_copy(src, dst, sems.at[1 + k]) for k, (src, dst) in enumerate(pieces)]
    for copy in fetch:
        copy.start()

    for copy in fetch[:3]:
        copy.wait()
    count = arrived.shape[0]
    places = one_hot(arrived_s[:, features:].astype(F32).astype(jnp.int32), count)
    ordered = mm(places, arrived_s[:, :features], TN).astype(BF16)
    normed_parents = rms_rows(ordered, gain_s[1])
    for copy in fetch[3:7]:
        copy.wait()
    odd = lax.rem(lax.axis_index("pix"), 2) == 1
    before = jnp.where(odd, near_s[0], near_s[1])
    after = jnp.where(odd, near_s[1], near_s[0])
    spans[0, :HALO] = rms_rows(before, gain_s[0])
    spans[0, HALO:] = rms_rows(fine_s[: SPAN - HALO], gain_s[0])
    spans[1, : SPAN - HALO] = rms_rows(fine_s[rows - (SPAN - HALO) :], gain_s[0])
    spans[1, SPAN - HALO :] = rms_rows(after, gain_s[0])
    for copy in fetch[7:11]:
        copy.wait()
    p_keys[...] = mm(normed_parents, wp_s[:, :features]).astype(BF16)
    p_values[...] = mm(normed_parents, wp_s[:, features:]).astype(BF16)
    for e in range(2):
        query_e[e] = mm(spans[e, HALO : HALO + WIN], w_s[0]).astype(BF16)
    for copy in fetch[11:]:
        copy.wait()

    def finish(w, query_w, self_t):
        here = block(w, WIN)
        own = block(w, PWIN)
        crossed = cross_attention(p_keys[own], p_values[own], query_w, head_size)
        branch = mm(self_t, wo_s[:features], TN) + mm(crossed, wo_s[features:], TN)
        out_s[here] = (fine_s[here].astype(F32) + branch).astype(BF16)
        pltpu.make_async_copy(out_s.at[here], out.at[here], sems.at[0]).start()

    def between(i, carry):
        finish(i + 1, query_s[block(i, WIN)], inner_s[i])
        return carry

    def edge(e, carry):
        w = e * (windows - 1)
        keys, values_t = gather_kv(spans[e], index_s[w], w * WIN, w_s[1], w_s[2])

        def store(head, value):
            edge_self[head * head_size : (head + 1) * head_size] = value

        self_attention(keys, values_t, query_e[e], head_size, store)
        finish(w, query_e[e], edge_self[...])
        return carry

    lax.fori_loop(0, windows - 2, between, 0)
    lax.fori_loop(0, 2, edge, 0)
    pltpu.make_async_copy(out_s, out, sems.at[0]).wait()


def on_device(
    fine_tokens, parent_tokens, shift_table, parent_slot, fine_gain, parent_gain, w_qkv, w_parent, w_out,
):
    rows, features = fine_tokens.shape
    parents = parent_tokens.shape[0]
    devices = lax.axis_size("pix")
    windows = rows // WIN
    head_size = features // HEADS
    offset = lax.axis_index("pix") * rows
    index = jnp.mod(shift_table - offset + HALO, rows * devices).reshape(windows, 1, WIN)
    gain = fine_gain.reshape(1, features)

    params = pltpu.CompilerParams(vmem_limit_bytes=60 * MIB)

    def array(*shape):
        return jax.ShapeDtypeStruct(shape, BF16)

    first, second, packed = pl.pallas_call(
        pack_kernel,
        out_shape=[array(HALO, features), array(HALO, features), array(parents, features + LANES)],
        in_specs=[HBM] * 3,
        out_specs=[VMEM] * 3,
        scratch_shapes=[
            pltpu.VMEM((parents, features), BF16),
            pltpu.VMEM((1, parents), jnp.int32),
            pltpu.SemaphoreType.DMA((4,)),
        ],
        compiler_params=params,
        name="pack",
    )(fine_tokens, parent_tokens, parent_slot.reshape(1, parents))
    pairs = [(i, i + 1 - 2 * (i % 2)) for i in range(devices)]
    across = [(i, (i - 1 + 2 * (i % 2)) % devices) for i in range(devices)]
    first = lax.ppermute(first, "pix", pairs)
    second = lax.ppermute(second, "pix", across)
    arrived = lax.all_to_all(packed, "pix", split_axis=0, concat_axis=0, tiled=True)

    query, inner = pl.pallas_call(
        functools.partial(local_kernel, windows=windows, head_size=head_size),
        out_shape=[array(rows - 2 * WIN, features), array(windows - 2, features, WIN)],
        in_specs=[HBM] * 4,
        out_specs=[HBM] * 2,
        scratch_shapes=[
            pltpu.VMEM((windows, WIN, features), BF16),
            pltpu.VMEM((3, features, features), BF16),
            pltpu.VMEM((windows, 1, WIN), jnp.int32),
            pltpu.VMEM((1, features), F32),
            pltpu.VMEM((rows, features), BF16),
            pltpu.VMEM((rows - 2 * WIN, features), BF16),
            pltpu.VMEM((windows - 2, features, WIN), BF16),
            pltpu.SemaphoreType.DMA((windows + 7,)),
        ],
        compiler_params=params,
        cost_estimate=pl.CostEstimate(flops=8 * 10**9, bytes_accessed=4 * 10**6, transcendentals=2 * 10**6),
        name="local",
    )(fine_tokens, w_qkv, index, gain)

    return pl.pallas_call(
        functools.partial(edge_kernel, windows=windows, head_size=head_size),
        out_shape=array(rows, features),
        in_specs=[HBM] * 12,
        out_specs=HBM,
        scratch_shapes=[
            pltpu.VMEM((rows, features), BF16),
            pltpu.VMEM((rows - 2 * WIN, features), BF16),
            pltpu.VMEM((windows - 2, features, WIN), BF16),
            pltpu.VMEM((2, HALO, features), BF16),
            pltpu.VMEM((windows, 1, WIN), jnp.int32),
            pltpu.VMEM((parents, features + LANES), BF16),
            pltpu.VMEM((2, 1, features), F32),
            pltpu.VMEM((3, features, features), BF16),
            pltpu.VMEM((features, 2 * features), BF16),
            pltpu.VMEM((2 * features, features), BF16),
            pltpu.VMEM((rows, features), BF16),
            pltpu.VMEM((2, SPAN, features), BF16),
            pltpu.VMEM((2, WIN, features), BF16),
            pltpu.VMEM((features, WIN), BF16),
            pltpu.VMEM((parents, features), BF16),
            pltpu.VMEM((parents, features), BF16),
            pltpu.SemaphoreType.DMA((15,)),
        ],
        compiler_params=params,
        cost_estimate=pl.CostEstimate(flops=10 * 10**9, bytes_accessed=6 * 10**6, transcendentals=3 * 10**6),
        name="edges",
    )(
        fine_tokens, query, inner, first, second, index, arrived, gain, parent_gain.reshape(1, features),
        w_qkv, w_parent, w_out,
    )


def solution(mesh):
    return jax.shard_map(
        on_device,
        mesh=mesh,
        in_specs=(P(("batch", "pix"), None), P(("batch", "pix"), None), P("pix"), P("pix"), P(), P(), P(), P(), P()),
        out_specs=P(("batch", "pix"), None),
        check_vma=False,
    )
```

time: 65.4 us -> 35.3 us (0.54)
  Pallas kernels: 32.7 us -> 20.8 us
  local copies, waits for them, and re-layouts: 12.6 us -> 0.79 us
  starting transfers between devices: 18.1 us -> 12.6 us
  other arithmetic: 1.33 us -> 0.6 us
    pallas_call x1, Pallas kernels: 20.9 us -> 11.9 us  [on_device(): pl.pallas_call(functools.partial(edge_kernel, windows=windows, head_size=...]
    unnamed x26 -> x8, local copies, waits for them, and re-layouts: 9.6 us -> 0.79 us
    all_to_all x2 -> x1, starting transfers between devices: 13.3 us -> 7.29 us  [on_device(): lax.all_to_all(packed, 'pix', split_axis=0, concat_axis=0, tiled=True)]
    pallas_call x1, Pallas kernels: 11.8 us -> 7.02 us  [on_device(): pl.pallas_call(functools.partial(local_kernel, windows=windows, head_size...]
    pallas_call x0 -> x1, Pallas kernels: none -> 1.92 us  [on_device(): pl.pallas_call(pack_kernel, out_shape=[array(HALO, features), array(HALO,...]
    all_to_all x2 -> x0, local copies, waits for them, and re-layouts: 1.92 us -> none  [on_device(): lax.all_to_all(parent_slot, 'pix', split_axis=0, concat_axis=0, tiled=True)]
    slice x1 -> x0, local copies, waits for them, and re-layouts: 0.98 us -> none  [on_device(): after = lax.ppermute(fine_tokens[:HALO], 'pix', [(j, i) for i, j in ring])]
  transfers between devices with their start and end apart: 4 -> 3, of which waited for: 0 -> 1; matrix products, arithmetic and copies ran while one was open for 5% -> 2% of each run, Pallas kernels for 18% -> 20%
where the time goes in v2:
time: 35.3 us; the launch traced here: 35 us
  Pallas kernels  20.8 us (59%)
  starting transfers between devices  12.6 us (36%)
  local copies, waits for them, and re-layouts  0.79 us (2%)
  other arithmetic  0.6 us (2%)
    pallas_call x1, Pallas kernels, on_device(): pl.pallas_call(functools.partial(edge_kernel, windows=windows, head_size=...  11.9 us
    all_to_all x1, starting transfers between devices, on_device(): lax.all_to_all(packed, 'pix', split_axis=0, concat_axis=0, tiled=True)  7.29 us
    pallas_call x1, Pallas kernels, on_device(): pl.pallas_call(functools.partial(local_kernel, windows=windows, head_size...  7.02 us
    ppermute x1, starting transfers between devices, on_device(): second = lax.ppermute(second, 'pix', across)  3.26 us
    ppermute x1, starting transfers between devices, on_device(): first = lax.ppermute(first, 'pix', pairs)  2.02 us
    pallas_call x1, Pallas kernels, on_device(): pl.pallas_call(pack_kernel, out_shape=[array(HALO, features), array(HALO,...  1.92 us
    unnamed x8, local copies, waits for them, and re-layouts  0.79 us
  transfers between devices with their start and end apart: 3, of which 1 were waited for; matrix products, arithmetic and copies ran while one was open for 2% of the time, Pallas kernels for 20%

profile of v2, /device:TPU:0, one launch (start us, length us, event | category | flops | bytes accessed | tf_op | source)
XLA Modules:
  0.0 35.0 jit_solution(13744220923956568422)
XLA Ops:
  0.0 0.0 copy-start.1
  0.0 1.9 %pack.1 = (bf16[128,512]{1,0:T(8,128)(2,1)}, bf16[128,512]{1,0:T(8,128)(2,1)}, bf16[256,640]{1,0:T(8,128)(2,1)}) custom-call(bf16[1024,512]{1,0:T(8,128)(2,1)} %fine.5, bf16[256,512]{1,0:T(8,128)(2,1)} %parents.1, s32[1,256]{1,0:T(1,128)} %bitcast.10), custom_call_target="tpu_custom_call" | custom-call | tf_op jit(solution)/shard_map/pack/pallas_call | solution.py:253
  1.9 7.3 %all-to-all-start = ((bf16[8,32,640]{2,1,0:T(8,128)(2,1)}), bf16[8,32,640]{2,1,0:T(8,128)(2,1)S(1)}, u32[]{:S(2)}, u32[]{:S(2)}) async-start(bf16[8,32,640]{2,1,0:T(8,128)(2,1)} %bitcast.7), calls=%async_computation | async-start | bytes 655360 | tf_op jit(solution)/shard_map/all_to_all | solution.py:270
  9.2 2.0 %collective-permute-start = (bf16[128,512]{1,0:T(8,128)(2,1)}, bf16[128,512]{1,0:T(8,128)(2,1)S(1)}, u32[]{:S(2)}, u32[]{:S(2)}) collective-permute-start(bf16[128,512]{1,0:T(8,128)(2,1)} %get-tuple-element.12), channel_id=1, source_target_pairs={{0,4},{4,0},{8,12},{12,8},{16,20},{20,16},{24,28},{28,24},{1,5},{5... | collective-permute-start | bytes 393224 | tf_op jit(solution)/shard_map/ppermute | solution.py:268
  11.2 3.3 %collective-permute-start.1 = (bf16[128,512]{1,0:T(8,128)(2,1)}, bf16[128,512]{1,0:T(8,128)(2,1)S(1)}, u32[]{:S(2)}, u32[]{:S(2)}) collective-permute-start(bf16[128,512]{1,0:T(8,128)(2,1)} %get-tuple-element.13), channel_id=1, source_target_pairs={{0,28},{4,8},{8,4},{12,16},{16,12},{20,24},{24,20},{28,0},{1,29},{... | collective-permute-start | bytes 393224 | tf_op jit(solution)/shard_map/ppermute | solution.py:269
  14.5 0.0 copy-done.1
  14.5 0.6 %add_select_fusion = s32[1024]{0:T(1024)} fusion(s32[1024]{0:T(1024)S(1)} %copy-done.1, s32[]{:T(128)S(6)} %mul.3), kind=kLoop, calls=%fused_computation | loop fusion | flops 13312 | bytes 8196 | tf_op jit(solution)/shard_map/jit(remainder)/select_n | solution.py:245
  15.1 7.0 %local.1 = (bf16[512,512]{1,0:T(8,128)(2,1)}, bf16[2,512,256]{2,1,0:T(8,128)(2,1)}) custom-call(bf16[1024,512]{1,0:T(8,128)(2,1)} %fine.5, bf16[512,1536]{1,0:T(8,128)(2,1)} %w_qkv.3, s32[4,1,256]{2,1,0:T(1,128)} %bitcast.8, f32[1,512]{1,0:T(1,128)} %bitcast.11), custom_call_target="tpu_custom_call" | custom-call | flops 8000000000 | bytes 4000000 | tf_op jit(solution)/shard_map/local/pallas_call | solution.py:272
  22.1 0.0 collective-permute-done.first
  22.2 0.0 copy-start.2
  22.2 0.2 collective-permute-done.1.second
  22.4 0.0 copy-start.3
  22.4 0.0 all-to-all-done
  22.4 0.0 copy-start
  22.4 0.4 %copy-done.2 = bf16[128,512]{1,0:T(8,128)(2,1)} copy-done((bf16[128,512]{1,0:T(8,128)(2,1)}, bf16[128,512]{1,0:T(8,128)(2,1)S(1)}, u32[]{:S(2)}) %copy-start.2) | copy-done | bytes 131096
  22.8 0.2 copy-done.3
  23.0 0.1 copy-done
  23.1 11.9 %edges.1 = bf16[1024,512]{1,0:T(8,128)(2,1)} custom-call(bf16[1024,512]{1,0:T(8,128)(2,1)} %fine.5, bf16[512,512]{1,0:T(8,128)(2,1)} %get-tuple-element.10.query, bf16[2,512,256]{2,1,0:T(8,128)(2,1)} %get-tuple-element.11.inner, bf16[128,512]{1,0:T(8,128)(2,1)} %copy-done.2, bf16[128,512]{1,0:T(8,128)(2,1)} %copy-done.3, s32[4,1,256]{2,1,0:T(1,128)} %bitcast.9, ...), custom_call_target="tpu_custom_call" | custom-call | flops 10000000000 | bytes 6000000 | tf_op jit(solution)/shard_map/edges/pallas_call | solution.py:292
Async XLA Ops:
  0.0 14.5 %copy-start.1 = (s32[1024]{0:T(1024)S(1)}, s32[1024]{0:T(1024)}, u32[]{:S(2)}) copy-start(s32[1024]{0:T(1024)} %param.11) | copy-start | bytes 12292
  1.9 20.4 %all-to-all-start = ((bf16[8,32,640]{2,1,0:T(8,128)(2,1)}), bf16[8,32,640]{2,1,0:T(8,128)(2,1)S(1)}, u32[]{:S(2)}, u32[]{:S(2)}) async-start(bf16[8,32,640]{2,1,0:T(8,128)(2,1)} %bitcast.7), calls=%async_computation | async-start | bytes 655360 | tf_op jit(solution)/shard_map/all_to_all | solution.py:270
  9.2 12.9 %collective-permute-start = (bf16[128,512]{1,0:T(8,128)(2,1)}, bf16[128,512]{1,0:T(8,128)(2,1)S(1)}, u32[]{:S(2)}, u32[]{:S(2)}) collective-permute-start(bf16[128,512]{1,0:T(8,128)(2,1)} %get-tuple-element.12), channel_id=1, source_target_pairs={{0,4},{4,0},{8,12},{12,8},{16,20},{20,16},{24,28},{28,24},{1,5},{5... | collective-permute-start | bytes 393224 | tf_op jit(solution)/shard_map/ppermute | solution.py:268
  11.2 11.1 %collective-permute-start.1 = (bf16[128,512]{1,0:T(8,128)(2,1)}, bf16[128,512]{1,0:T(8,128)(2,1)S(1)}, u32[]{:S(2)}, u32[]{:S(2)}) collective-permute-start(bf16[128,512]{1,0:T(8,128)(2,1)} %get-tuple-element.13), channel_id=1, source_target_pairs={{0,28},{4,8},{8,4},{12,16},{16,12},{20,24},{24,20},{28,0},{1,29},{... | collective-permute-start | bytes 393224 | tf_op jit(solution)/shard_map/ppermute | solution.py:269
  22.2 0.6 %copy-start.2 = (bf16[128,512]{1,0:T(8,128)(2,1)}, bf16[128,512]{1,0:T(8,128)(2,1)S(1)}, u32[]{:S(2)}) copy-start(bf16[128,512]{1,0:T(8,128)(2,1)S(1)} %collective-permute-done.first) | copy-start | bytes 393220
  22.4 0.6 %copy-start.3 = (bf16[128,512]{1,0:T(8,128)(2,1)}, bf16[128,512]{1,0:T(8,128)(2,1)S(1)}, u32[]{:S(2)}) copy-start(bf16[128,512]{1,0:T(8,128)(2,1)S(1)} %collective-permute-done.1.second) | copy-start | bytes 393220
  22.4 0.8 %copy-start = (bf16[8,32,640]{2,1,0:T(8,128)(2,1)}, bf16[8,32,640]{2,1,0:T(8,128)(2,1)S(1)}, u32[]{:S(2)}) copy-start(bf16[8,32,640]{2,1,0:T(8,128)(2,1)S(1)} %all-to-all-done) | copy-start | bytes 983044

commit v3 on v2

v3 whole, which is shorter than its diff:
```python
import functools
import math

import jax
import jax.numpy as jnp
from jax import lax
from jax.experimental import pallas as pl
from jax.experimental.pallas import tpu as pltpu
from jax.sharding import PartitionSpec as P

HEADS = 16
WIN = 256
HALO = 128
PWIN = 64
LANES = 128
SPAN = WIN + 2 * HALO
F32 = jnp.float32
BF16 = jnp.bfloat16
VMEM = pl.BlockSpec(memory_space=pltpu.VMEM)
HBM = pl.BlockSpec(memory_space=pltpu.HBM)
MIB = 1024 * 1024
NN, NT, TN = ((1,), (0,)), ((1,), (1,)), ((0,), (0,))


def mm(a, b, dims=NN):
    return lax.dot_general(a, b, (dims, ((), ())), preferred_element_type=F32)


def rms_rows(matrix, gain):
    values = matrix.astype(F32)
    factor = lax.rsqrt(jnp.mean(values * values, axis=-1, keepdims=True) + 1e-06)
    return (values * factor * gain).astype(BF16)


def softmax_down(scores, scale):
    powers = jnp.exp2((scores - jnp.max(scores, axis=0, keepdims=True)) * scale)
    return (powers * (1.0 / jnp.sum(powers, axis=0, keepdims=True))).astype(BF16)


def column_of(row):
    wide = jnp.broadcast_to(row, (LANES, row.shape[1]))
    return jnp.concatenate([wide[:, k : k + LANES].T for k in range(0, row.shape[1], LANES)], axis=0)


def one_hot(column, width):
    lane = lax.broadcasted_iota(jnp.int32, column.shape, 1)
    return jnp.concatenate(
        [jnp.where(column == lane + k, 1.0, 0.0).astype(BF16) for k in range(0, width, LANES)], axis=1
    )


def spread(rows, head_size):
    lane = lax.broadcasted_iota(jnp.int32, rows.shape, 1) // head_size
    return jnp.concatenate([jnp.where(lane == k, rows, 0) for k in range(LANES // head_size)], axis=0)


def gather_kv(span, row, first_row, all_rows, w_key, w_value):
    offset = row - first_row
    offset = jnp.where(offset < 0, offset + all_rows, offset)
    offset = jnp.where(offset >= all_rows, offset - all_rows, offset)
    gathered = mm(one_hot(column_of(offset), SPAN), span).astype(BF16)
    return mm(gathered, w_key).astype(BF16), mm(gathered, w_value).astype(BF16).T


def self_attention(keys, values_t, query, head_size, store):
    features = query.shape[1]
    scale = math.log2(math.e) / math.sqrt(head_size)
    tiles = [slice(k, k + LANES) for k in range(0, features, LANES)]
    scores = [mm(spread(keys[:, tile], head_size), query[:, tile], NT) for tile in tiles]
    count = keys.shape[0]
    per_tile = LANES // head_size
    for head in range(features // head_size):
        part = (head % per_tile) * count
        weights = softmax_down(scores[head // per_tile][part : part + count], scale)
        store(head, mm(values_t[head * head_size : (head + 1) * head_size], weights).astype(BF16))


def cross_attention(keys, values, query, head_size):
    scale = math.log2(math.e) / math.sqrt(head_size)
    per_tile = LANES // head_size
    tiles = [slice(k, k + LANES) for k in range(0, query.shape[1], LANES)]
    scores = [mm(spread(keys[:, tile], head_size), query[:, tile], NT) for tile in tiles]
    out = []
    for tile, score in zip(tiles, scores):
        weights = [softmax_down(score[k * PWIN : (k + 1) * PWIN], scale) for k in range(per_tile)]
        out.append(mm(spread(values[:, tile], head_size), jnp.concatenate(weights, axis=0), TN).astype(BF16))
    return jnp.concatenate(out, axis=0)


def span_start(w, rows):
    return lax.axis_index("pix") * rows + w * WIN - HALO


def block(w, size):
    return pl.ds(pl.multiple_of(w * size, size), size)


def pack_kernel(fine, parents, slots, first, second, packed, parents_s, slots_s, column_s, sems):
    rows, features = fine.shape
    odd = lax.rem(lax.axis_index("pix"), 2)
    pieces = [
        (slots, slots_s),
        (parents, parents_s),
        (fine.at[pl.ds(pl.multiple_of((1 - odd) * (rows - HALO), HALO), HALO)], first),
        (fine.at[pl.ds(pl.multiple_of(odd * (rows - HALO), HALO), HALO)], second),
        (parents_s, packed.at[:, :features]),
        (column_s, packed.at[:, features:]),
    ]
    copies = [pltpu.make_async_copy(src, dst, sems.at[k]) for k, (src, dst) in enumerate(pieces)]
    for copy in copies[:4]:
        copy.start()
    copies[0].wait()
    column_s[...] = column_of(slots_s[...]).astype(F32).astype(BF16)
    copies[5].start()
    copies[1].wait()
    copies[4].start()
    for copy in copies[2:]:
        copy.wait()


def gate_kernel(before, held, passed):
    pass


def local_kernel(
    fine, w_qkv, index, gain, parent_gain, query, inner, fine_v, index_v, gain_v, w_v, normed, sems,
    *, windows, head_size, all_rows,
):
    rows, features = fine.shape
    pieces = [
        (gain, gain_v.at[0]),
        (parent_gain, gain_v.at[1]),
        (index, index_v),
    ]
    pieces += [(fine.at[w * WIN : (w + 1) * WIN], fine_v.at[w * WIN : (w + 1) * WIN]) for w in range(windows)]
    pieces += [(w_qkv.at[:, c * features : (c + 1) * features], w_v.at[c]) for c in range(3)]
    fetch = [pltpu.make_async_copy(src, dst, sems.at[k]) for k, (src, dst) in enumerate(pieces)]
    for copy in fetch:
        copy.start()
    for copy in fetch[:3]:
        copy.wait()
    for w in range(windows):
        fetch[3 + w].wait()
        here = slice(w * WIN, (w + 1) * WIN)
        normed[here] = rms_rows(fine_v[here], gain_v[0])
    for copy in fetch[3 + windows :]:
        copy.wait()
    query[...] = mm(normed[...], w_v[0]).astype(BF16)

    def window(i, carry):
        w = i + 1
        span = normed[pl.ds(pl.multiple_of(w * WIN - HALO, HALO), SPAN)]
        keys, values_t = gather_kv(span, index_v[w], span_start(w, rows), all_rows, w_v[1], w_v[2])

        def store(head, value):
            inner[i, head * head_size : (head + 1) * head_size] = value

        self_attention(keys, values_t, query[block(w, WIN)], head_size, store)
        return carry

    lax.fori_loop(0, windows - 2, window, 0)


def edge_kernel(
    query, fine, index, gains, first, second, w_qkv, outer, w_kv, ends, sems, *, windows, head_size, all_rows,
):
    rows, features = fine.shape
    fetch = [
        pltpu.make_async_copy(w_qkv.at[:, (1 + c) * features : (2 + c) * features], w_kv.at[c], sems.at[c])
        for c in range(2)
    ]
    for copy in fetch:
        copy.start()
    odd = lax.rem(lax.axis_index("pix"), 2) == 1
    ends[0, :HALO] = rms_rows(jnp.where(odd, first[...], second[...]), gains[0])
    ends[0, HALO:] = rms_rows(fine[: SPAN - HALO], gains[0])
    ends[1, : SPAN - HALO] = rms_rows(fine[rows - (SPAN - HALO) :], gains[0])
    ends[1, SPAN - HALO :] = rms_rows(jnp.where(odd, second[...], first[...]), gains[0])
    for copy in fetch:
        copy.wait()

    def edge(e, carry):
        w = e * (windows - 1)
        keys, values_t = gather_kv(ends[e], index[w], span_start(w, rows), all_rows, w_kv[0], w_kv[1])

        def store(head, value):
            outer[e, head * head_size : (head + 1) * head_size] = value

        self_attention(keys, values_t, query[block(w, WIN)], head_size, store)
        return carry

    lax.fori_loop(0, 2, edge, 0)


def cross_kernel(
    query, inner, outer, gains, arrived, fine_h, w_parent, w_out, out, fine, wp, wo, out_s, p_keys, p_values, sems,
    *, windows, head_size, all_rows,
):
    rows, features = fine.shape
    fetch = [
        pltpu.make_async_copy(w_parent, wp, sems.at[1]),
        pltpu.make_async_copy(w_out, wo, sems.at[2]),
        pltpu.make_async_copy(fine_h, fine, sems.at[3]),
    ]
    for copy in fetch:
        copy.start()
    count = arrived.shape[0]
    places = one_hot(arrived[:, features:].astype(F32).astype(jnp.int32), count)
    ordered = mm(places, arrived[:, :features], TN).astype(BF16)
    normed_parents = rms_rows(ordered, gains[1])
    fetch[0].wait()
    p_keys[...] = mm(normed_parents, wp[:, :features]).astype(BF16)
    p_values[...] = mm(normed_parents, wp[:, features:]).astype(BF16)
    for copy in fetch[1:]:
        copy.wait()

    def finish(w, self_t):
        here = block(w, WIN)
        own = block(w, PWIN)
        crossed = cross_attention(p_keys[own], p_values[own], query[here], head_size)
        branch = mm(self_t, wo[:features], TN) + mm(crossed, wo[features:], TN)
        out_s[here] = (fine[here].astype(F32) + branch).astype(BF16)
        pltpu.make_async_copy(out_s.at[here], out.at[here], sems.at[0]).start()

    def between(i, carry):
        finish(i + 1, inner[i])
        return carry

    def edge(e, carry):
        finish(e * (windows - 1), outer[e])
        return carry

    lax.fori_loop(0, 2, edge, 0)
    lax.fori_loop(0, windows - 2, between, 0)
    pltpu.make_async_copy(out_s, out, sems.at[0]).wait()


def on_device(
    fine_tokens, parent_tokens, shift_table, parent_slot, fine_gain, parent_gain, w_qkv, w_parent, w_out,
):
    rows, features = fine_tokens.shape
    parents = parent_tokens.shape[0]
    devices = lax.axis_size("pix")
    windows = rows // WIN
    sizes = dict(windows=windows, head_size=features // HEADS, all_rows=rows * devices)
    params = pltpu.CompilerParams(vmem_limit_bytes=32 * MIB)
    semaphores = pltpu.SemaphoreType.DMA

    def near(*shape, dtype=BF16):
        return pltpu.VMEM(shape, dtype)

    def far(x):
        return pltpu.with_memory_space_constraint(x, pltpu.HBM)

    fine, weights = far(fine_tokens), far(w_qkv)
    first, second, packed = pl.pallas_call(
        pack_kernel,
        out_shape=[near(HALO, features), near(HALO, features), pltpu.HBM((parents, features + LANES), BF16)],
        in_specs=[HBM] * 3,
        out_specs=[VMEM, VMEM, HBM],
        scratch_shapes=[
            near(parents, features),
            near(1, parents, dtype=jnp.int32),
            near(parents, LANES),
            semaphores((6,)),
        ],
        compiler_params=params,
        name="pack",
    )(fine, far(parent_tokens), far(parent_slot.reshape(1, parents)))
    pairs = [(i, i + 1 - 2 * (i % 2)) for i in range(devices)]
    across = [(i, (i - 1 + 2 * (i % 2)) % devices) for i in range(devices)]
    first_in = lax.ppermute(first, "pix", pairs)
    second_in = lax.ppermute(second, "pix", across)
    packed = pl.pallas_call(
        gate_kernel,
        out_shape=pltpu.HBM((parents, features + LANES), BF16),
        in_specs=[VMEM, HBM],
        out_specs=HBM,
        input_output_aliases={1: 0},
        compiler_params=params,
        name="gate",
    )(second, far(packed))
    arrived = lax.all_to_all(packed, "pix", split_axis=0, concat_axis=0, tiled=True)

    query, inner, fine_v, index, gains = pl.pallas_call(
        functools.partial(local_kernel, **sizes),
        out_shape=[
            near(rows, features),
            near(windows - 2, features, WIN),
            near(rows, features),
            near(windows, 1, WIN, dtype=jnp.int32),
            near(2, 1, features, dtype=F32),
        ],
        in_specs=[HBM] * 5,
        out_specs=[VMEM] * 5,
        scratch_shapes=[near(3, features, features), near(rows, features), semaphores((windows + 6,))],
        compiler_params=params,
        cost_estimate=pl.CostEstimate(flops=8 * 10**9, bytes_accessed=4 * 10**6, transcendentals=2 * 10**6),
        name="local",
    )(
        fine, weights, far(shift_table.reshape(windows, 1, WIN)), far(fine_gain.reshape(1, features)),
        far(parent_gain.reshape(1, features)),
    )

    outer = pl.pallas_call(
        functools.partial(edge_kernel, **sizes),
        out_shape=near(2, features, WIN),
        in_specs=[VMEM] * 6 + [HBM],
        out_specs=VMEM,
        scratch_shapes=[near(2, features, features), near(2, SPAN, features), semaphores((2,))],
        compiler_params=params,
        cost_estimate=pl.CostEstimate(flops=8 * 10**9, bytes_accessed=2 * 10**6, transcendentals=2 * 10**6),
        name="edges",
    )(query, fine_v, index, gains, first_in, second_in, weights)

    return pl.pallas_call(
        functools.partial(cross_kernel, **sizes),
        out_shape=pltpu.HBM((rows, features), BF16),
        in_specs=[VMEM] * 5 + [HBM] * 3,
        out_specs=HBM,
        scratch_shapes=[
            near(rows, features),
            near(features, 2 * features),
            near(2 * features, features),
            near(rows, features),
            near(parents, features),
            near(parents, features),
            semaphores((4,)),
        ],
        compiler_params=params,
        cost_estimate=pl.CostEstimate(flops=5 * 10**9, bytes_accessed=6 * 10**6, transcendentals=10**6),
        name="cross",
    )(query, inner, outer, gains, arrived, fine, far(w_parent), far(w_out))


def solution(mesh):
    return jax.shard_map(
        on_device,
        mesh=mesh,
        in_specs=(P(("batch", "pix"), None), P(("batch", "pix"), None), P("pix"), P("pix"), P(), P(), P(), P(), P()),
        out_specs=P(("batch", "pix"), None),
        check_vma=False,
    )
```

time: 35.3 us -> 31 us (0.88)
  starting transfers between devices: 12.6 us -> 10 us
  local copies, waits for them, and re-layouts: 0.79 us -> 0 us
  other arithmetic: 0.6 us -> 0 us
    all_to_all x1, starting transfers between devices: 7.29 us -> 3.43 us  [on_device(): lax.all_to_all(packed, 'pix', split_axis=0, concat_axis=0, tiled=True)]
    ppermute x2, starting transfers between devices: 5.28 us -> 6.58 us  [the longest x1 3.54 us: on_device(): second_in = lax.ppermute(second, 'pix', across)]
    unnamed x8 -> x0, local copies, waits for them, and re-layouts: 0.79 us -> none
    select_n x1 -> x0, other arithmetic: 0.6 us -> none  [on_device(): jnp.mod(shift_table - offset + HALO, rows * devices)]
    pallas_call x3 -> x5, Pallas kernels: 20.8 us -> 20.6 us  [the longest x1 7 us: on_device(): pl.pallas_call(functools.partial(cross_kernel, **sizes), out_shape=pltpu....]
  transfers between devices with their start and end apart: 3 -> 3, of which waited for: 1 -> 0; matrix products, arithmetic and copies ran while one was open for 2% -> 0% of each run, Pallas kernels for 20% -> 39%
where the time goes in v3:
time: 31 us; the launch traced here: 30.7 us
  Pallas kernels  20.6 us (66%)
  starting transfers between devices  10 us (32%)
    pallas_call x1, Pallas kernels, on_device(): pl.pallas_call(functools.partial(cross_kernel, **sizes), out_shape=pltpu....  7 us
    pallas_call x1, Pallas kernels, on_device(): pl.pallas_call(functools.partial(local_kernel, **sizes), out_shape=[near(...  6.6 us
    pallas_call x1, Pallas kernels, on_device(): pl.pallas_call(functools.partial(edge_kernel, **sizes), out_shape=near(2,...  5.3 us
    ppermute x1, starting transfers between devices, on_device(): second_in = lax.ppermute(second, 'pix', across)  3.54 us
    all_to_all x1, starting transfers between devices, on_device(): lax.all_to_all(packed, 'pix', split_axis=0, concat_axis=0, tiled=True)  3.43 us
    ppermute x1, starting transfers between devices, on_device(): first_in = lax.ppermute(first, 'pix', pairs)  3.03 us
    pallas_call x1, Pallas kernels, on_device(): pl.pallas_call(pack_kernel, out_shape=[near(HALO, features), near(HALO, f...  1.72 us
  transfers between devices with their start and end apart: 3, of which 0 were waited for; matrix products, arithmetic and copies ran while one was open for 0% of the time, Pallas kernels for 39%

profile of v3, /device:TPU:0, one launch (start us, length us, event | category | flops | bytes accessed | tf_op | source)
XLA Modules:
  0.0 30.7 jit_solution(18394107615603079796)
XLA Ops:
  0.0 1.7 %pack.1 = (bf16[128,512]{1,0:T(8,128)(2,1)S(1)}, bf16[128,512]{1,0:T(8,128)(2,1)S(1)}, bf16[256,640]{1,0:T(8,128)(2,1)}) custom-call(bf16[1024,512]{1,0:T(8,128)(2,1)} %fine_h.1, bf16[256,512]{1,0:T(8,128)(2,1)} %parents.1, s32[1,256]{1,0:T(1,128)} %bitcast.8), custom_call_target="tpu_custom_call" | custom-call | tf_op jit(solution)/shard_map/pack/pallas_call | solution.py:256
  1.7 3.0 %collective-permute-start = (bf16[128,512]{1,0:T(8,128)(2,1)S(1)}, bf16[128,512]{1,0:T(8,128)(2,1)S(1)}, u32[]{:S(2)}, u32[]{:S(2)}) collective-permute-start(bf16[128,512]{1,0:T(8,128)(2,1)S(1)} %get-tuple-element.18), channel_id=1, source_target_pairs={{0,4},{4,0},{8,12},{12,8},{16,20},{20,16},{24,28},{28,24},{1,5},{5... | collective-permute-start | bytes 393224 | tf_op jit(solution)/shard_map/ppermute | solution.py:272
  4.8 3.5 %collective-permute-start.1 = (bf16[128,512]{1,0:T(8,128)(2,1)S(1)}, bf16[128,512]{1,0:T(8,128)(2,1)S(1)}, u32[]{:S(2)}, u32[]{:S(2)}) collective-permute-start(bf16[128,512]{1,0:T(8,128)(2,1)S(1)} %get-tuple-element.19.before), channel_id=1, source_target_pairs={{0,28},{4,8},{8,4},{12,16},{16,12},{20,24},{24,20},{28,0},{1,29},{... | collective-permute-start | bytes 393224 | tf_op jit(solution)/shard_map/ppermute | solution.py:273
  8.3 3.4 %all-to-all-start = ((bf16[8,32,640]{2,1,0:T(8,128)(2,1)}), bf16[8,32,640]{2,1,0:T(8,128)(2,1)S(1)}, u32[]{:S(2)}, u32[]{:S(2)}) async-start(bf16[8,32,640]{2,1,0:T(8,128)(2,1)} %bitcast.7), calls=%async_computation | async-start | bytes 655360 | tf_op jit(solution)/shard_map/all_to_all | solution.py:283
  11.7 6.6 %local.1 = (bf16[1024,512]{1,0:T(8,128)(2,1)S(1)}, bf16[2,512,256]{2,1,0:T(8,128)(2,1)S(1)}, bf16[1024,512]{1,0:T(8,128)(2,1)S(1)}, s32[4,1,256]{2,1,0:T(1,128)S(1)}, f32[2,1,512]{2,1,0:T(1,128)S(1)}) custom-call(bf16[1024,512]{1,0:T(8,128)(2,1)} %fine_h.1, bf16[512,1536]{1,0:T(8,128)(2,1)} %w_qkv.3, s32[4,1,256]{2,1,0:T(1,128)} %bitcast.9, ...), custom_call_target="tpu_custom_call" | custom-call | flops 8000000000 | bytes 4000000 | tf_op jit(solution)/shard_map/local/pallas_call | solution.py:285
  18.4 0.0 collective-permute-done.first
  18.4 0.0 collective-permute-done.1.second
  18.4 5.3 %edges.1.outer = bf16[2,512,256]{2,1,0:T(8,128)(2,1)S(1)} custom-call(bf16[1024,512]{1,0:T(8,128)(2,1)S(1)} %get-tuple-element.13.query, bf16[1024,512]{1,0:T(8,128)(2,1)S(1)} %get-tuple-element.15.fine, s32[4,1,256]{2,1,0:T(1,128)S(1)} %get-tuple-element.16.index, f32[2,1,512]{2,1,0:T(1,128)S(1)} %get-tuple-element.17.gains, ...), custom_call_target="tpu_custom_call" | custom-call | flops 8000000000 | bytes 2000000 | tf_op jit(solution)/shard_map/edges/pallas_call | solution.py:305
  23.7 0.0 all-to-all-done
  23.7 7.0 %cross.1 = bf16[1024,512]{1,0:T(8,128)(2,1)} custom-call(bf16[1024,512]{1,0:T(8,128)(2,1)S(1)} %get-tuple-element.13.query, bf16[2,512,256]{2,1,0:T(8,128)(2,1)S(1)} %get-tuple-element.14.inner, bf16[2,512,256]{2,1,0:T(8,128)(2,1)S(1)} %edges.1.outer, f32[2,1,512]{2,1,0:T(1,128)S(1)} %get-tuple-element.17.gains, bf16[256,640]{1,0:T(8,128)(2,1)S(1)} %bitcast.6, ...), custom_call_target="tpu_custom_call" | custom-call | flops 5000000000 | bytes 6000000 | tf_op jit(solution)/shard_map/cross/pallas_call | solution.py:316
  (1 shorter events, 0.0 us)
Async XLA Ops:
  1.7 16.6 %collective-permute-start = (bf16[128,512]{1,0:T(8,128)(2,1)S(1)}, bf16[128,512]{1,0:T(8,128)(2,1)S(1)}, u32[]{:S(2)}, u32[]{:S(2)}) collective-permute-start(bf16[128,512]{1,0:T(8,128)(2,1)S(1)} %get-tuple-element.18), channel_id=1, source_target_pairs={{0,4},{4,0},{8,12},{12,8},{16,20},{20,16},{24,28},{28,24},{1,5},{5... | collective-permute-start | bytes 393224 | tf_op jit(solution)/shard_map/ppermute | solution.py:272
  4.8 13.6 %collective-permute-start.1 = (bf16[128,512]{1,0:T(8,128)(2,1)S(1)}, bf16[128,512]{1,0:T(8,128)(2,1)S(1)}, u32[]{:S(2)}, u32[]{:S(2)}) collective-permute-start(bf16[128,512]{1,0:T(8,128)(2,1)S(1)} %get-tuple-element.19.before), channel_id=1, source_target_pairs={{0,28},{4,8},{8,4},{12,16},{16,12},{20,24},{24,20},{28,0},{1,29},{... | collective-permute-start | bytes 393224 | tf_op jit(solution)/shard_map/ppermute | solution.py:273
  8.3 15.4 %all-to-all-start = ((bf16[8,32,640]{2,1,0:T(8,128)(2,1)}), bf16[8,32,640]{2,1,0:T(8,128)(2,1)S(1)}, u32[]{:S(2)}, u32[]{:S(2)}) async-start(bf16[8,32,640]{2,1,0:T(8,128)(2,1)} %bitcast.7), calls=%async_computation | async-start | bytes 655360 | tf_op jit(solution)/shard_map/all_to_all | solution.py:283

commit v4 on v3

v4 whole, which is shorter than its diff:
```python
import functools
import math

import jax
import jax.numpy as jnp
from jax import lax
from jax.experimental import pallas as pl
from jax.experimental.pallas import tpu as pltpu
from jax.sharding import PartitionSpec as P

HEADS = 16
WIN = 256
HALO = 128
PWIN = 64
LANES = 128
SPAN = WIN + 2 * HALO
F32 = jnp.float32
BF16 = jnp.bfloat16
VMEM = pl.BlockSpec(memory_space=pltpu.VMEM)
HBM = pl.BlockSpec(memory_space=pltpu.HBM)
MIB = 1024 * 1024
NN, NT, TN = ((1,), (0,)), ((1,), (1,)), ((0,), (0,))


def mm(a, b, dims=NN):
    return lax.dot_general(a, b, (dims, ((), ())), preferred_element_type=F32)


def rms_rows(matrix, gain):
    values = matrix.astype(F32)
    factor = lax.rsqrt(jnp.mean(values * values, axis=-1, keepdims=True) + 1e-06)
    return (values * factor * gain).astype(BF16)


def softmax_down(scores, scale):
    powers = jnp.exp2((scores - jnp.max(scores, axis=0, keepdims=True)) * scale)
    return (powers * (1.0 / jnp.sum(powers, axis=0, keepdims=True))).astype(BF16)


def column_of(row):
    wide = jnp.broadcast_to(row, (LANES, row.shape[1]))
    return jnp.concatenate([wide[:, k : k + LANES].T for k in range(0, row.shape[1], LANES)], axis=0)


def one_hot(column, width):
    lane = lax.broadcasted_iota(jnp.int32, column.shape, 1)
    return jnp.concatenate(
        [jnp.where(column == lane + k, 1.0, 0.0).astype(BF16) for k in range(0, width, LANES)], axis=1
    )


def spread(rows, head_size):
    lane = lax.broadcasted_iota(jnp.int32, rows.shape, 1) // head_size
    return jnp.concatenate([jnp.where(lane == k, rows, 0) for k in range(LANES // head_size)], axis=0)


def gather(span, row, first_row, all_rows):
    offset = row - first_row
    offset = jnp.where(offset < 0, offset + all_rows, offset)
    offset = jnp.where(offset >= all_rows, offset - all_rows, offset)
    return mm(one_hot(column_of(offset), SPAN), span).astype(BF16)


def project_kv(gathered, w_kv, keys, values_t):
    keys[...] = mm(gathered[...], w_kv[0]).astype(BF16)
    values = mm(gathered[...], w_kv[1]).astype(BF16)
    for i in range(values_t.shape[0]):
        values_t[i] = values[i * WIN : (i + 1) * WIN].T


def self_attention(keys, values_t, query, head_size, store):
    features = query.shape[1]
    scale = math.log2(math.e) / math.sqrt(head_size)
    tiles = [slice(k, k + LANES) for k in range(0, features, LANES)]
    scores = [mm(spread(keys[:, tile], head_size), query[:, tile], NT) for tile in tiles]
    count = keys.shape[0]
    per_tile = LANES // head_size
    for head in range(features // head_size):
        part = (head % per_tile) * count
        weights = softmax_down(scores[head // per_tile][part : part + count], scale)
        store(head, mm(values_t[head * head_size : (head + 1) * head_size], weights).astype(BF16))


def cross_attention(keys, values, query, head_size):
    scale = math.log2(math.e) / math.sqrt(head_size)
    per_tile = LANES // head_size
    tiles = [slice(k, k + LANES) for k in range(0, query.shape[1], LANES)]
    scores = [mm(spread(keys[:, tile], head_size), query[:, tile], NT) for tile in tiles]
    out = []
    for tile, score in zip(tiles, scores):
        weights = [softmax_down(score[k * PWIN : (k + 1) * PWIN], scale) for k in range(per_tile)]
        out.append(mm(spread(values[:, tile], head_size), jnp.concatenate(weights, axis=0), TN).astype(BF16))
    return jnp.concatenate(out, axis=0)


def span_start(w, rows):
    return lax.axis_index("pix") * rows + w * WIN - HALO


def block(w, size):
    return pl.ds(pl.multiple_of(w * size, size), size)


def pack_kernel(
    fine, parents, slots, index, gain, parent_gain, w_qkv, first, second, packed, normed, index_v, gains, w_q,
    fine_s, parents_s, slots_s, column_s, sems, *, windows,
):
    rows, features = fine.shape
    odd = lax.rem(lax.axis_index("pix"), 2)
    pieces = [
        (slots, slots_s),
        (parents, parents_s),
        (fine.at[pl.ds(pl.multiple_of((1 - odd) * (rows - HALO), HALO), HALO)], first),
        (fine.at[pl.ds(pl.multiple_of(odd * (rows - HALO), HALO), HALO)], second),
        (gain, gains.at[0]),
        (parent_gain, gains.at[1]),
        (index, index_v),
    ]
    blocks = [slice(w * WIN, (w + 1) * WIN) for w in range(windows)]
    pieces += [(fine.at[here], fine_s.at[here]) for here in blocks]
    weigh = pltpu.make_async_copy(w_qkv.at[:, :features], w_q, sems.at[9 + windows])
    pieces += [(parents_s, packed.at[:, :features]), (column_s, packed.at[:, features:])]
    copies = [pltpu.make_async_copy(src, dst, sems.at[k]) for k, (src, dst) in enumerate(pieces)]
    for copy in copies[:-2] + [weigh]:
        copy.start()
    copies[0].wait()
    column_s[...] = column_of(slots_s[...]).astype(F32).astype(BF16)
    copies[-1].start()
    copies[1].wait()
    copies[-2].start()
    for copy in copies[2:7]:
        copy.wait()
    for here, copy in zip(blocks, copies[7:]):
        copy.wait()
        normed[here] = rms_rows(fine_s[here], gains[0])
    for copy in copies[-2:] + [weigh]:
        copy.wait()


def gate_kernel(before, held, passed):
    pass


def attend_windows(query, keys, values_t, out, head_size):
    def window(i, carry):
        def store(head, value):
            out[i, head * head_size : (head + 1) * head_size] = value

        self_attention(keys[block(i, WIN)], values_t[i], query(i), head_size, store)
        return carry

    lax.fori_loop(0, out.shape[0], window, 0, unroll=True)


def self_kernel(
    normed, index, gains, w_q, first, second, w_qkv, query_h, self_t, w_kv, query, ends, gathered, keys, values_t, sems,
    *, windows, head_size, all_rows,
):
    rows, features = normed.shape
    own = SPAN - HALO
    fetch = [
        pltpu.make_async_copy(w_qkv.at[:, (1 + c) * features : (2 + c) * features], w_kv.at[c], sems.at[c])
        for c in range(2)
    ]
    for copy in fetch:
        copy.start()
    odd = lax.rem(lax.axis_index("pix"), 2) == 1
    ends[0, :HALO] = rms_rows(jnp.where(odd, first[...], second[...]), gains[0])
    ends[0, HALO:] = normed[:own]
    ends[1, :own] = normed[rows - own :]
    ends[1, own:] = rms_rows(jnp.where(odd, second[...], first[...]), gains[0])

    def pick(w, span):
        gathered[block(w, WIN)] = gather(span, index[w], span_start(w, rows), all_rows)

    def pick_inner(w, carry):
        pick(w, normed[pl.ds(pl.multiple_of(w * WIN - HALO, HALO), SPAN)])
        return carry

    pick(0, ends[0])
    pick(windows - 1, ends[1])
    lax.fori_loop(1, windows - 1, pick_inner, 0)
    query[...] = mm(normed[...], w_q[...]).astype(BF16)
    leave = pltpu.make_async_copy(query, query_h, sems.at[2])
    leave.start()
    for copy in fetch:
        copy.wait()
    project_kv(gathered, w_kv, keys, values_t)
    attend_windows(lambda w: query[block(w, WIN)], keys, values_t, self_t, head_size)
    leave.wait()


def cross_kernel(
    self_t, gains, arrived, query_h, fine_h, w_parent, w_out, out, query, fine, wp, wo, out_s, p_keys, p_values, sems,
    *, windows, head_size, all_rows,
):
    rows, features = fine.shape
    fetch = [
        pltpu.make_async_copy(w_parent, wp, sems.at[1]),
        pltpu.make_async_copy(query_h, query, sems.at[4]),
        pltpu.make_async_copy(w_out, wo, sems.at[2]),
        pltpu.make_async_copy(fine_h, fine, sems.at[3]),
    ]
    for copy in fetch:
        copy.start()
    count = arrived.shape[0]
    places = one_hot(arrived[:, features:].astype(F32).astype(jnp.int32), count)
    ordered = mm(places, arrived[:, :features], TN).astype(BF16)
    normed_parents = rms_rows(ordered, gains[1])
    fetch[0].wait()
    p_keys[...] = mm(normed_parents, wp[:, :features]).astype(BF16)
    p_values[...] = mm(normed_parents, wp[:, features:]).astype(BF16)
    for copy in fetch[1:]:
        copy.wait()

    def finish(w, carry):
        here = block(w, WIN)
        own = block(w, PWIN)
        crossed = cross_attention(p_keys[own], p_values[own], query[here], head_size)
        joined = jnp.concatenate([self_t[w], crossed], axis=0).T
        branch = mm(joined, wo[...])
        out_s[here] = (fine[here].astype(F32) + branch).astype(BF16)
        pltpu.make_async_copy(out_s.at[here], out.at[here], sems.at[0]).start()
        return carry

    lax.fori_loop(0, windows, finish, 0, unroll=True)
    pltpu.make_async_copy(out_s, out, sems.at[0]).wait()


def on_device(
    fine_tokens, parent_tokens, shift_table, parent_slot, fine_gain, parent_gain, w_qkv, w_parent, w_out,
):
    rows, features = fine_tokens.shape
    parents = parent_tokens.shape[0]
    devices = lax.axis_size("pix")
    windows = rows // WIN
    sizes = dict(windows=windows, head_size=features // HEADS, all_rows=rows * devices)
    params = pltpu.CompilerParams(vmem_limit_bytes=32 * MIB)
    semaphores = pltpu.SemaphoreType.DMA

    def near(*shape, dtype=BF16):
        return pltpu.VMEM(shape, dtype)

    def far(x):
        return pltpu.with_memory_space_constraint(x, pltpu.HBM)

    fine, weights = far(fine_tokens), far(w_qkv)
    first, second, packed, normed, index, gains, w_q = pl.pallas_call(
        functools.partial(pack_kernel, windows=windows),
        out_shape=[
            near(HALO, features),
            near(HALO, features),
            pltpu.HBM((parents, features + LANES), BF16),
            near(rows, features),
            near(windows, 1, WIN, dtype=jnp.int32),
            near(2, 1, features, dtype=F32),
            near(features, features),
        ],
        in_specs=[HBM] * 7,
        out_specs=[VMEM, VMEM, HBM] + [VMEM] * 4,
        scratch_shapes=[
            near(rows, features),
            near(parents, features),
            near(1, parents, dtype=jnp.int32),
            near(parents, LANES),
            semaphores((windows + 10,)),
        ],
        compiler_params=params,
        name="pack",
    )(
        fine, far(parent_tokens), far(parent_slot.reshape(1, parents)), far(shift_table.reshape(windows, 1, WIN)),
        far(fine_gain.reshape(1, features)), far(parent_gain.reshape(1, features)), weights,
    )
    pairs = [(i, i + 1 - 2 * (i % 2)) for i in range(devices)]
    across = [(i, (i - 1 + 2 * (i % 2)) % devices) for i in range(devices)]
    first_in = lax.ppermute(first, "pix", pairs)
    second_in = lax.ppermute(second, "pix", across)
    packed = pl.pallas_call(
        gate_kernel,
        out_shape=pltpu.HBM((parents, features + LANES), BF16),
        in_specs=[VMEM, HBM],
        out_specs=HBM,
        input_output_aliases={1: 0},
        compiler_params=params,
        name="gate",
    )(second, far(packed))
    arrived = lax.all_to_all(packed, "pix", split_axis=0, concat_axis=0, tiled=True)

    query, self_t = pl.pallas_call(
        functools.partial(self_kernel, **sizes),
        out_shape=[pltpu.HBM((rows, features), BF16), near(windows, features, WIN)],
        in_specs=[VMEM] * 6 + [HBM],
        out_specs=[HBM, VMEM],
        scratch_shapes=[
            near(2, features, features),
            near(rows, features),
            near(2, SPAN, features),
            near(rows, features),
            near(rows, features),
            near(windows, features, WIN),
            semaphores((3,)),
        ],
        compiler_params=params,
        cost_estimate=pl.CostEstimate(flops=16 * 10**9, bytes_accessed=4 * 10**6, transcendentals=4 * 10**6),
        name="self",
    )(normed, index, gains, w_q, first_in, second_in, weights)

    return pl.pallas_call(
        functools.partial(cross_kernel, **sizes),
        out_shape=pltpu.HBM((rows, features), BF16),
        in_specs=[VMEM] * 3 + [HBM] * 4,
        out_specs=HBM,
        scratch_shapes=[
            near(rows, features),
            near(rows, features),
            near(features, 2 * features),
            near(2 * features, features),
            near(rows, features),
            near(parents, features),
            near(parents, features),
            semaphores((5,)),
        ],
        compiler_params=params,
        cost_estimate=pl.CostEstimate(flops=5 * 10**9, bytes_accessed=6 * 10**6, transcendentals=10**6),
        name="cross",
    )(self_t, gains, arrived, far(query), fine, far(w_parent), far(w_out))


def solution(mesh):
    return jax.shard_map(
        on_device,
        mesh=mesh,
        in_specs=(P(("batch", "pix"), None), P(("batch", "pix"), None), P("pix"), P("pix"), P(), P(), P(), P(), P()),
        out_specs=P(("batch", "pix"), None),
        check_vma=False,
    )
```

time: 31 us -> 28.5 us (0.919)
  Pallas kernels: 20.6 us -> 16.9 us
  waiting for transfers between devices: 0.01 us -> 1.28 us
    pallas_call x3 -> x2, Pallas kernels: 13.6 us -> 10.6 us  [the longest x1 8.66 us: on_device(): pl.pallas_call(functools.partial(self_kernel, **sizes), out_shape=[pltpu....]
    ppermute x1, waiting for transfers between devices: 0.01 us -> 0.67 us  [on_device(): second_in = lax.ppermute(second, 'pix', across)]
    pallas_call x1, Pallas kernels: 7 us -> 6.35 us  [on_device(): pl.pallas_call(functools.partial(cross_kernel, **sizes), out_shape=pltpu....]
    all_to_all x1, waiting for transfers between devices: 0.01 us -> 0.61 us  [on_device(): lax.all_to_all(packed, 'pix', split_axis=0, concat_axis=0, tiled=True)]
  transfers between devices with their start and end apart: 3 -> 3, of which waited for: 0 -> 2; matrix products, arithmetic and copies ran while one was open for 0% -> 0% of each run, Pallas kernels for 39% -> 31%
where the time goes in v4:
time: 28.5 us; the launch traced here: 28.3 us
  Pallas kernels  16.9 us (59%)
  starting transfers between devices  10 us (35%)
  waiting for transfers between devices  1.28 us (4%)
    pallas_call x1, Pallas kernels, on_device(): pl.pallas_call(functools.partial(self_kernel, **sizes), out_shape=[pltpu....  8.66 us
    pallas_call x1, Pallas kernels, on_device(): pl.pallas_call(functools.partial(cross_kernel, **sizes), out_shape=pltpu....  6.35 us
    ppermute x1, starting transfers between devices, on_device(): second_in = lax.ppermute(second, 'pix', across)  3.54 us
    all_to_all x1, starting transfers between devices, on_device(): lax.all_to_all(packed, 'pix', split_axis=0, concat_axis=0, tiled=True)  3.43 us
    ppermute x1, starting transfers between devices, on_device(): first_in = lax.ppermute(first, 'pix', pairs)  3.03 us
    pallas_call x1, Pallas kernels, on_device(): pl.pallas_call(functools.partial(pack_kernel, windows=windows), out_shape...  1.94 us
    ppermute x1, waiting for transfers between devices, on_device(): second_in = lax.ppermute(second, 'pix', across)  0.67 us
    all_to_all x1, waiting for transfers between devices, on_device(): lax.all_to_all(packed, 'pix', split_axis=0, concat_axis=0, tiled=True)  0.61 us
  transfers between devices with their start and end apart: 3, of which 2 were waited for; matrix products, arithmetic and copies ran while one was open for 0% of the time, Pallas kernels for 31%

profile of v4, /device:TPU:0, one launch (start us, length us, event | category | flops | bytes accessed | tf_op | source)
XLA Modules:
  0.0 28.3 jit_solution(5881448793589928511)
XLA Ops:
  0.0 1.9 %pack.1 = (bf16[128,512]{1,0:T(8,128)(2,1)S(1)}, bf16[128,512]{1,0:T(8,128)(2,1)S(1)}, bf16[256,640]{1,0:T(8,128)(2,1)}, bf16[1024,512]{1,0:T(8,128)(2,1)S(1)}, ...) custom-call(bf16[1024,512]{1,0:T(8,128)(2,1)} %fine_h.1, ...), custom_call_target="tpu_custom_call" | custom-call | tf_op jit(solution)/shard_map/pack/pallas_call | solution.py:248
  1.9 3.0 %collective-permute-start = (bf16[128,512]{1,0:T(8,128)(2,1)S(1)}, bf16[128,512]{1,0:T(8,128)(2,1)S(1)}, u32[]{:S(2)}, u32[]{:S(2)}) collective-permute-start(bf16[128,512]{1,0:T(8,128)(2,1)S(1)} %get-tuple-element.18), channel_id=1, source_target_pairs={{0,4},{4,0},{8,12},{12,8},{16,20},{20,16},{24,28},{28,24},{1,5},{5... | collective-permute-start | bytes 393224 | tf_op jit(solution)/shard_map/ppermute | solution.py:276
  5.0 3.5 %collective-permute-start.1 = (bf16[128,512]{1,0:T(8,128)(2,1)S(1)}, bf16[128,512]{1,0:T(8,128)(2,1)S(1)}, u32[]{:S(2)}, u32[]{:S(2)}) collective-permute-start(bf16[128,512]{1,0:T(8,128)(2,1)S(1)} %get-tuple-element.19.before), channel_id=1, source_target_pairs={{0,28},{4,8},{8,4},{12,16},{16,12},{20,24},{24,20},{28,0},{1,29},{... | collective-permute-start | bytes 393224 | tf_op jit(solution)/shard_map/ppermute | solution.py:277
  8.5 3.4 %all-to-all-start = ((bf16[8,32,640]{2,1,0:T(8,128)(2,1)}), bf16[8,32,640]{2,1,0:T(8,128)(2,1)S(1)}, u32[]{:S(2)}, u32[]{:S(2)}) async-start(bf16[8,32,640]{2,1,0:T(8,128)(2,1)} %bitcast.7), calls=%async_computation | async-start | bytes 655360 | tf_op jit(solution)/shard_map/all_to_all | solution.py:287
  12.0 0.0 collective-permute-done.first
  12.0 0.7 %collective-permute-done.1.second = bf16[128,512]{1,0:T(8,128)(2,1)S(1)} collective-permute-done((bf16[128,512]{1,0:T(8,128)(2,1)S(1)}, bf16[128,512]{1,0:T(8,128)(2,1)S(1)}, u32[]{:S(2)}, u32[]{:S(2)}) %collective-permute-start.1) | collective-permute-done | bytes 131104 | tf_op jit(solution)/shard_map/ppermute | solution.py:277
  12.6 8.7 %self.1 = (bf16[1024,512]{1,0:T(8,128)(2,1)}, bf16[4,512,256]{2,1,0:T(8,128)(2,1)S(1)}) custom-call(bf16[1024,512]{1,0:T(8,128)(2,1)S(1)} %get-tuple-element.14.normed, s32[4,1,256]{2,1,0:T(1,128)S(1)} %get-tuple-element.15.index, f32[2,1,512]{2,1,0:T(1,128)S(1)} %get-tuple-element.16.gains, bf16[512,512]{1,0:T(8,128)(2,1)S(1)} %get-tuple-element.17.w_q, ...), custom_call_target="tpu_custom_call" | custom-call | flops 16000000000 | bytes 4000000 | tf_op jit(solution)/shard_map/self/pallas_call | solution.py:289
  21.3 0.6 %all-to-all-done = bf16[8,32,640]{2,1,0:T(8,128)(2,1)S(1)} async-done(((bf16[8,32,640]{2,1,0:T(8,128)(2,1)}), bf16[8,32,640]{2,1,0:T(8,128)(2,1)S(1)}, u32[]{:S(2)}, u32[]{:S(2)}) %all-to-all-start) | async-done | bytes 327712 | tf_op jit(solution)/shard_map/all_to_all | solution.py:287
  21.9 6.3 %cross.1 = bf16[1024,512]{1,0:T(8,128)(2,1)} custom-call(bf16[4,512,256]{2,1,0:T(8,128)(2,1)S(1)} %get-tuple-element.20.self_t, f32[2,1,512]{2,1,0:T(1,128)S(1)} %get-tuple-element.16.gains, bf16[256,640]{1,0:T(8,128)(2,1)S(1)} %bitcast.6, bf16[1024,512]{1,0:T(8,128)(2,1)} %get-tuple-element.22.query_h, bf16[1024,512]{1,0:T(8,128)(2,1)} %fine_h.1, ...), custom_call_target="tpu_custom_call" | custom-call | flops 5000000000 | bytes 6000000 | tf_op jit(solution)/shard_map/cross/pallas_call | solution.py:308
  (1 shorter events, 0.0 us)
Async XLA Ops:
  1.9 10.0 %collective-permute-start = (bf16[128,512]{1,0:T(8,128)(2,1)S(1)}, bf16[128,512]{1,0:T(8,128)(2,1)S(1)}, u32[]{:S(2)}, u32[]{:S(2)}) collective-permute-start(bf16[128,512]{1,0:T(8,128)(2,1)S(1)} %get-tuple-element.18), channel_id=1, source_target_pairs={{0,4},{4,0},{8,12},{12,8},{16,20},{20,16},{24,28},{28,24},{1,5},{5... | collective-permute-start | bytes 393224 | tf_op jit(solution)/shard_map/ppermute | solution.py:276
  5.0 7.7 %collective-permute-start.1 = (bf16[128,512]{1,0:T(8,128)(2,1)S(1)}, bf16[128,512]{1,0:T(8,128)(2,1)S(1)}, u32[]{:S(2)}, u32[]{:S(2)}) collective-permute-start(bf16[128,512]{1,0:T(8,128)(2,1)S(1)} %get-tuple-element.19.before), channel_id=1, source_target_pairs={{0,28},{4,8},{8,4},{12,16},{16,12},{20,24},{24,20},{28,0},{1,29},{... | collective-permute-start | bytes 393224 | tf_op jit(solution)/shard_map/ppermute | solution.py:277
  8.5 13.4 %all-to-all-start = ((bf16[8,32,640]{2,1,0:T(8,128)(2,1)}), bf16[8,32,640]{2,1,0:T(8,128)(2,1)S(1)}, u32[]{:S(2)}, u32[]{:S(2)}) async-start(bf16[8,32,640]{2,1,0:T(8,128)(2,1)} %bitcast.7), calls=%async_computation | async-start | bytes 655360 | tf_op jit(solution)/shard_map/all_to_all | solution.py:287

commit v5 on v4

--- a/solution.py
+++ b/solution.py
@@ -68,17 +68,24 @@
         values_t[i] = values[i * WIN : (i + 1) * WIN].T
 
 
-def self_attention(keys, values_t, query, head_size, store):
-    features = query.shape[1]
+def self_scores(keys, query, tile, head_size):
+    lanes = slice(tile * LANES, (tile + 1) * LANES)
+    return mm(spread(keys[:, lanes], head_size), query[:, lanes], NT)
+
+
+def self_attention(pending, following, values_t, head_size, store):
     scale = math.log2(math.e) / math.sqrt(head_size)
-    tiles = [slice(k, k + LANES) for k in range(0, features, LANES)]
-    scores = [mm(spread(keys[:, tile], head_size), query[:, tile], NT) for tile in tiles]
-    count = keys.shape[0]
     per_tile = LANES // head_size
-    for head in range(features // head_size):
-        part = (head % per_tile) * count
-        weights = softmax_down(scores[head // per_tile][part : part + count], scale)
-        store(head, mm(values_t[head * head_size : (head + 1) * head_size], weights).astype(BF16))
+    coming = []
+    for tile, scores in enumerate(pending):
+        if following is not None:
+            coming.append(following(tile))
+        count = scores.shape[0] // per_tile
+        for k in range(per_tile):
+            head = tile * per_tile + k
+            weights = softmax_down(scores[k * count : (k + 1) * count], scale)
+            store(head, mm(values_t[head * head_size : (head + 1) * head_size], weights).astype(BF16))
+    return coming
 
 
 def cross_attention(keys, values, query, head_size):
@@ -102,7 +109,7 @@
 
 
 def pack_kernel(
-    fine, parents, slots, index, gain, parent_gain, w_qkv, first, second, packed, normed, index_v, gains, w_q,
+    fine, parents, slots, index, gain, parent_gain, first, second, packed, normed, index_v, gains,
     fine_s, parents_s, slots_s, column_s, sems, *, windows,
 ):
     rows, features = fine.shape
@@ -118,10 +125,9 @@
     ]
     blocks = [slice(w * WIN, (w + 1) * WIN) for w in range(windows)]
     pieces += [(fine.at[here], fine_s.at[here]) for here in blocks]
-    weigh = pltpu.make_async_copy(w_qkv.at[:, :features], w_q, sems.at[9 + windows])
     pieces += [(parents_s, packed.at[:, :features]), (column_s, packed.at[:, features:])]
     copies = [pltpu.make_async_copy(src, dst, sems.at[k]) for k, (src, dst) in enumerate(pieces)]
-    for copy in copies[:-2] + [weigh]:
+    for copy in copies[:-2]:
         copy.start()
     copies[0].wait()
     column_s[...] = column_of(slots_s[...]).astype(F32).astype(BF16)
@@ -133,7 +139,7 @@
     for here, copy in zip(blocks, copies[7:]):
         copy.wait()
         normed[here] = rms_rows(fine_s[here], gains[0])
-    for copy in copies[-2:] + [weigh]:
+    for copy in copies[-2:]:
         copy.wait()
 
 
@@ -141,26 +147,16 @@
     pass
 
 
-def attend_windows(query, keys, values_t, out, head_size):
-    def window(i, carry):
-        def store(head, value):
-            out[i, head * head_size : (head + 1) * head_size] = value
-
-        self_attention(keys[block(i, WIN)], values_t[i], query(i), head_size, store)
-        return carry
-
-    lax.fori_loop(0, out.shape[0], window, 0, unroll=True)
-
-
 def self_kernel(
-    normed, index, gains, w_q, first, second, w_qkv, query_h, self_t, w_kv, query, ends, gathered, keys, values_t, sems,
+    normed, index, gains, first, second, w_qkv, w_parent, query, early_h, late, wp, w_q, w_kv, early, ends, gathered, keys,
+    values_t, sems,
     *, windows, head_size, all_rows,
 ):
     rows, features = normed.shape
     own = SPAN - HALO
     fetch = [
-        pltpu.make_async_copy(w_qkv.at[:, (1 + c) * features : (2 + c) * features], w_kv.at[c], sems.at[c])
-        for c in range(2)
+        pltpu.make_async_copy(w_qkv.at[:, c * features : (c + 1) * features], to, sems.at[c])
+        for c, to in enumerate([w_q, w_kv.at[0], w_kv.at[1]])
     ]
     for copy in fetch:
         copy.start()
@@ -180,24 +176,48 @@
     pick(0, ends[0])
     pick(windows - 1, ends[1])
     lax.fori_loop(1, windows - 1, pick_inner, 0)
+    fetch[0].wait()
     query[...] = mm(normed[...], w_q[...]).astype(BF16)
-    leave = pltpu.make_async_copy(query, query_h, sems.at[2])
-    leave.start()
-    for copy in fetch:
+    for copy in fetch[1:]:
         copy.wait()
     project_kv(gathered, w_kv, keys, values_t)
-    attend_windows(lambda w: query[block(w, WIN)], keys, values_t, self_t, head_size)
-    leave.wait()
+    leave = [
+        pltpu.make_async_copy(
+            w_parent.at[:, c * features : (c + 1) * features], wp.at[c * features : (c + 1) * features], sems.at[3 + c]
+        )
+        for c in range(2)
+    ]
+    for copy in leave:
+        copy.start()
+    split = early.shape[0]
+
+    def scores(w):
+        here = slice(w * WIN, (w + 1) * WIN)
+        return lambda tile: self_scores(keys[here], query[here], tile, head_size)
+
+    pending = [scores(0)(tile) for tile in range(features // LANES)]
+    for w in range(windows):
+        out = early.at[w] if w < split else late.at[w - split]
+
+        def store(head, value):
+            out[head * head_size : (head + 1) * head_size] = value
+
+        following = scores(w + 1) if w + 1 < windows else None
+        pending = self_attention(pending, following, values_t[w], head_size, store)
+        if w < split:
+            leave.append(pltpu.make_async_copy(out, early_h.at[w], sems.at[5 + w]))
+            leave[-1].start()
+    for copy in leave:
+        copy.wait()
 
 
 def cross_kernel(
-    self_t, gains, arrived, query_h, fine_h, w_parent, w_out, out, query, fine, wp, wo, out_s, p_keys, p_values, sems,
+    query, late, gains, arrived, wp, early_h, fine_h, w_out, out, early, fine, wo, out_s, p_keys, p_values, sems,
     *, windows, head_size, all_rows,
 ):
     rows, features = fine.shape
     fetch = [
-        pltpu.make_async_copy(w_parent, wp, sems.at[1]),
-        pltpu.make_async_copy(query_h, query, sems.at[4]),
+        pltpu.make_async_copy(early_h, early, sems.at[1]),
         pltpu.make_async_copy(w_out, wo, sems.at[2]),
         pltpu.make_async_copy(fine_h, fine, sems.at[3]),
     ]
@@ -207,23 +227,26 @@
     places = one_hot(arrived[:, features:].astype(F32).astype(jnp.int32), count)
     ordered = mm(places, arrived[:, :features], TN).astype(BF16)
     normed_parents = rms_rows(ordered, gains[1])
-    fetch[0].wait()
-    p_keys[...] = mm(normed_parents, wp[:, :features]).astype(BF16)
-    p_values[...] = mm(normed_parents, wp[:, features:]).astype(BF16)
-    for copy in fetch[1:]:
-        copy.wait()
-
-    def finish(w, carry):
-        here = block(w, WIN)
-        own = block(w, PWIN)
-        crossed = cross_attention(p_keys[own], p_values[own], query[here], head_size)
-        joined = jnp.concatenate([self_t[w], crossed], axis=0).T
+    p_keys[...] = mm(normed_parents, wp[:features]).astype(BF16)
+    p_values[...] = mm(normed_parents, wp[features:]).astype(BF16)
+    split = early.shape[0]
+    rows_of = [slice(w * WIN, (w + 1) * WIN) for w in range(windows)]
+
+    def crossed(w):
+        own = slice(w * PWIN, (w + 1) * PWIN)
+        return cross_attention(p_keys[own], p_values[own], query[rows_of[w]], head_size)
+
+    ahead = [crossed(w) for w in range(2)]
+    for copy in fetch:
+        copy.wait()
+    for w, here in enumerate(rows_of):
+        self_t = early[w] if w < split else late[w - split]
+        joined = jnp.concatenate([self_t, ahead.pop(0)], axis=0).T
         branch = mm(joined, wo[...])
         out_s[here] = (fine[here].astype(F32) + branch).astype(BF16)
         pltpu.make_async_copy(out_s.at[here], out.at[here], sems.at[0]).start()
-        return carry
-
-    lax.fori_loop(0, windows, finish, 0, unroll=True)
+        if w + 2 < windows:
+            ahead.append(crossed(w + 2))
     pltpu.make_async_copy(out_s, out, sems.at[0]).wait()
 
 
@@ -245,7 +268,7 @@
         return pltpu.with_memory_space_constraint(x, pltpu.HBM)
 
     fine, weights = far(fine_tokens), far(w_qkv)
-    first, second, packed, normed, index, gains, w_q = pl.pallas_call(
+    first, second, packed, normed, index, gains = pl.pallas_call(
         functools.partial(pack_kernel, windows=windows),
         out_shape=[
             near(HALO, features),
@@ -254,22 +277,21 @@
             near(rows, features),
             near(windows, 1, WIN, dtype=jnp.int32),
             near(2, 1, features, dtype=F32),
-            near(features, features),
-        ],
-        in_specs=[HBM] * 7,
-        out_specs=[VMEM, VMEM, HBM] + [VMEM] * 4,
+        ],
+        in_specs=[HBM] * 6,
+        out_specs=[VMEM, VMEM, HBM] + [VMEM] * 3,
         scratch_shapes=[
             near(rows, features),
             near(parents, features),
             near(1, parents, dtype=jnp.int32),
             near(parents, LANES),
-            semaphores((windows + 10,)),
+            semaphores((windows + 9,)),
         ],
         compiler_params=params,
         name="pack",
     )(
         fine, far(parent_tokens), far(parent_slot.reshape(1, parents)), far(shift_table.reshape(windows, 1, WIN)),
-        far(fine_gain.reshape(1, features)), far(parent_gain.reshape(1, features)), weights,
+        far(fine_gain.reshape(1, features)), far(parent_gain.reshape(1, features)),
     )
     pairs = [(i, i + 1 - 2 * (i % 2)) for i in range(devices)]
     across = [(i, (i - 1 + 2 * (i % 2)) % devices) for i in range(devices)]
@@ -286,44 +308,51 @@
     )(second, far(packed))
     arrived = lax.all_to_all(packed, "pix", split_axis=0, concat_axis=0, tiled=True)
 
-    query, self_t = pl.pallas_call(
+    split = windows // 2
+    query, early, late, wp = pl.pallas_call(
         functools.partial(self_kernel, **sizes),
-        out_shape=[pltpu.HBM((rows, features), BF16), near(windows, features, WIN)],
-        in_specs=[VMEM] * 6 + [HBM],
-        out_specs=[HBM, VMEM],
+        out_shape=[
+            near(rows, features),
+            pltpu.HBM((split, features, WIN), BF16),
+            near(windows - split, features, WIN),
+            near(2 * features, features),
+        ],
+        in_specs=[VMEM] * 5 + [HBM] * 2,
+        out_specs=[VMEM, HBM, VMEM, VMEM],
+        input_output_aliases={0: 3} if rows == 2 * features else {},
         scratch_shapes=[
+            near(features, features),
             near(2, features, features),
-            near(rows, features),
+            near(split, features, WIN),
             near(2, SPAN, features),
             near(rows, features),
             near(rows, features),
             near(windows, features, WIN),
-            semaphores((3,)),
+            semaphores((5 + split,)),
         ],
         compiler_params=params,
         cost_estimate=pl.CostEstimate(flops=16 * 10**9, bytes_accessed=4 * 10**6, transcendentals=4 * 10**6),
         name="self",
-    )(normed, index, gains, w_q, first_in, second_in, weights)
+    )(normed, index, gains, first_in, second_in, weights, far(w_parent))
 
     return pl.pallas_call(
         functools.partial(cross_kernel, **sizes),
         out_shape=pltpu.HBM((rows, features), BF16),
-        in_specs=[VMEM] * 3 + [HBM] * 4,
+        in_specs=[VMEM] * 5 + [HBM] * 3,
         out_specs=HBM,
         scratch_shapes=[
-            near(rows, features),
-            near(rows, features),
-            near(features, 2 * features),
+            near(split, features, WIN),
+            near(rows, features),
             near(2 * features, features),
             near(rows, features),
             near(parents, features),
             near(parents, features),
-            semaphores((5,)),
+            semaphores((4,)),
         ],
         compiler_params=params,
         cost_estimate=pl.CostEstimate(flops=5 * 10**9, bytes_accessed=6 * 10**6, transcendentals=10**6),
         name="cross",
-    )(self_t, gains, arrived, far(query), fine, far(w_parent), far(w_out))
+    )(query, late, gains, arrived, wp, far(early), fine, far(w_out))
 
 
 def solution(mesh):

time: 28.5 us -> 27 us (0.947)
  Pallas kernels: 16.9 us -> 14.9 us
  waiting for transfers between devices: 1.28 us -> 1.83 us
    pallas_call x1, Pallas kernels: 6.35 us -> 4.88 us  [on_device(): pl.pallas_call(functools.partial(cross_kernel, **sizes), out_shape=pltpu....]
    all_to_all x1, waiting for transfers between devices: 0.61 us -> 1.16 us  [on_device(): lax.all_to_all(packed, 'pix', split_axis=0, concat_axis=0, tiled=True)]
    pallas_call x1, Pallas kernels: 8.66 us -> 8.12 us  [on_device(): pl.pallas_call(functools.partial(self_kernel, **sizes), out_shape=[near(r...]
  transfers between devices with their start and end apart: 3 -> 3, of which waited for: 2 -> 2; matrix products, arithmetic and copies ran while one was open for 0% -> 0% of each run, Pallas kernels for 31% -> 30%
where the time goes in v5:
time: 27 us; the launch traced here: 26.8 us
  Pallas kernels  14.9 us (55%)
  starting transfers between devices  10 us (37%)
  waiting for transfers between devices  1.83 us (7%)
    pallas_call x1, Pallas kernels, on_device(): pl.pallas_call(functools.partial(self_kernel, **sizes), out_shape=[near(r...  8.12 us
    pallas_call x1, Pallas kernels, on_device(): pl.pallas_call(functools.partial(cross_kernel, **sizes), out_shape=pltpu....  4.88 us
    ppermute x1, starting transfers between devices, on_device(): second_in = lax.ppermute(second, 'pix', across)  3.54 us
    all_to_all x1, starting transfers between devices, on_device(): lax.all_to_all(packed, 'pix', split_axis=0, concat_axis=0, tiled=True)  3.43 us
    ppermute x1, starting transfers between devices, on_device(): first_in = lax.ppermute(first, 'pix', pairs)  3.03 us
    pallas_call x1, Pallas kernels, on_device(): pl.pallas_call(functools.partial(pack_kernel, windows=windows), out_shape...  1.92 us
    all_to_all x1, waiting for transfers between devices, on_device(): lax.all_to_all(packed, 'pix', split_axis=0, concat_axis=0, tiled=True)  1.16 us
    ppermute x1, waiting for transfers between devices, on_device(): second_in = lax.ppermute(second, 'pix', across)  0.67 us
  transfers between devices with their start and end apart: 3, of which 2 were waited for; matrix products, arithmetic and copies ran while one was open for 0% of the time, Pallas kernels for 30%

profile of v5, /device:TPU:0, one launch (start us, length us, event | category | flops | bytes accessed | tf_op | source)
XLA Modules:
  0.0 26.8 jit_solution(4058773692686067583)
XLA Ops:
  0.0 1.9 %pack.1 = (bf16[128,512]{1,0:T(8,128)(2,1)S(1)}, bf16[128,512]{1,0:T(8,128)(2,1)S(1)}, bf16[256,640]{1,0:T(8,128)(2,1)}, bf16[1024,512]{1,0:T(8,128)(2,1)S(1)}, ...) custom-call(bf16[1024,512]{1,0:T(8,128)(2,1)} %fine_h.1, bf16[256,512]{1,0:T(8,128)(2,1)} %parents.1, ...), custom_call_target="tpu_custom_call" | custom-call | tf_op jit(solution)/shard_map/pack/pallas_call | solution.py:271
  1.9 3.0 %collective-permute-start = (bf16[128,512]{1,0:T(8,128)(2,1)S(1)}, bf16[128,512]{1,0:T(8,128)(2,1)S(1)}, u32[]{:S(2)}, u32[]{:S(2)}) collective-permute-start(bf16[128,512]{1,0:T(8,128)(2,1)S(1)} %get-tuple-element.18), channel_id=1, source_target_pairs={{0,4},{4,0},{8,12},{12,8},{16,20},{20,16},{24,28},{28,24},{1,5},{5... | collective-permute-start | bytes 393224 | tf_op jit(solution)/shard_map/ppermute | solution.py:298
  5.0 3.5 %collective-permute-start.1 = (bf16[128,512]{1,0:T(8,128)(2,1)S(1)}, bf16[128,512]{1,0:T(8,128)(2,1)S(1)}, u32[]{:S(2)}, u32[]{:S(2)}) collective-permute-start(bf16[128,512]{1,0:T(8,128)(2,1)S(1)} %get-tuple-element.19.before), channel_id=1, source_target_pairs={{0,28},{4,8},{8,4},{12,16},{16,12},{20,24},{24,20},{28,0},{1,29},{... | collective-permute-start | bytes 393224 | tf_op jit(solution)/shard_map/ppermute | solution.py:299
  8.5 3.4 %all-to-all-start = ((bf16[8,32,640]{2,1,0:T(8,128)(2,1)}), bf16[8,32,640]{2,1,0:T(8,128)(2,1)S(1)}, u32[]{:S(2)}, u32[]{:S(2)}) async-start(bf16[8,32,640]{2,1,0:T(8,128)(2,1)} %bitcast.7), calls=%async_computation | async-start | bytes 655360 | tf_op jit(solution)/shard_map/all_to_all | solution.py:309
  12.0 0.0 collective-permute-done.first
  12.0 0.7 %collective-permute-done.1.second = bf16[128,512]{1,0:T(8,128)(2,1)S(1)} collective-permute-done((bf16[128,512]{1,0:T(8,128)(2,1)S(1)}, bf16[128,512]{1,0:T(8,128)(2,1)S(1)}, u32[]{:S(2)}, u32[]{:S(2)}) %collective-permute-start.1) | collective-permute-done | bytes 131104 | tf_op jit(solution)/shard_map/ppermute | solution.py:299
  12.6 8.1 %self.1 = (bf16[1024,512]{1,0:T(8,128)(2,1)S(1)}, bf16[2,512,256]{2,1,0:T(8,128)(2,1)}, bf16[2,512,256]{2,1,0:T(8,128)(2,1)S(1)}, bf16[1024,512]{1,0:T(8,128)(2,1)S(1)}) custom-call(bf16[1024,512]{1,0:T(8,128)(2,1)S(1)} %get-tuple-element.15.normed, s32[4,1,256]{2,1,0:T(1,128)S(1)} %get-tuple-element.16.index, ...), custom_call_target="tpu_custom_call", output_to_operand_aliasing={{3}: (0, {})} | custom-call | flops 16000000000 | bytes 4000000 | tf_op jit(solution)/shard_map/self/pallas_call | solution.py:312
  20.8 1.2 %all-to-all-done = bf16[8,32,640]{2,1,0:T(8,128)(2,1)S(1)} async-done(((bf16[8,32,640]{2,1,0:T(8,128)(2,1)}), bf16[8,32,640]{2,1,0:T(8,128)(2,1)S(1)}, u32[]{:S(2)}, u32[]{:S(2)}) %all-to-all-start) | async-done | bytes 327712 | tf_op jit(solution)/shard_map/all_to_all | solution.py:309
  21.9 4.9 %cross.1 = bf16[1024,512]{1,0:T(8,128)(2,1)} custom-call(bf16[1024,512]{1,0:T(8,128)(2,1)S(1)} %get-tuple-element.20.query, bf16[2,512,256]{2,1,0:T(8,128)(2,1)S(1)} %get-tuple-element.21.late, f32[2,1,512]{2,1,0:T(1,128)S(1)} %get-tuple-element.17.gains, bf16[256,640]{1,0:T(8,128)(2,1)S(1)} %bitcast.6, bf16[1024,512]{1,0:T(8,128)(2,1)S(1)} %get-tuple-element.23.wp, ...), custom_call_target="tpu_custom_call" | custom-call | flops 5000000000 | bytes 6000000 | tf_op jit(solution)/shard_map/cross/pallas_call | solution.py:338
  (1 shorter events, 0.0 us)
Async XLA Ops:
  1.9 10.0 %collective-permute-start = (bf16[128,512]{1,0:T(8,128)(2,1)S(1)}, bf16[128,512]{1,0:T(8,128)(2,1)S(1)}, u32[]{:S(2)}, u32[]{:S(2)}) collective-permute-start(bf16[128,512]{1,0:T(8,128)(2,1)S(1)} %get-tuple-element.18), channel_id=1, source_target_pairs={{0,4},{4,0},{8,12},{12,8},{16,20},{20,16},{24,28},{28,24},{1,5},{5... | collective-permute-start | bytes 393224 | tf_op jit(solution)/shard_map/ppermute | solution.py:298
  5.0 7.7 %collective-permute-start.1 = (bf16[128,512]{1,0:T(8,128)(2,1)S(1)}, bf16[128,512]{1,0:T(8,128)(2,1)S(1)}, u32[]{:S(2)}, u32[]{:S(2)}) collective-permute-start(bf16[128,512]{1,0:T(8,128)(2,1)S(1)} %get-tuple-element.19.before), channel_id=1, source_target_pairs={{0,28},{4,8},{8,4},{12,16},{16,12},{20,24},{24,20},{28,0},{1,29},{... | collective-permute-start | bytes 393224 | tf_op jit(solution)/shard_map/ppermute | solution.py:299
  8.5 13.4 %all-to-all-start = ((bf16[8,32,640]{2,1,0:T(8,128)(2,1)}), bf16[8,32,640]{2,1,0:T(8,128)(2,1)S(1)}, u32[]{:S(2)}, u32[]{:S(2)}) async-start(bf16[8,32,640]{2,1,0:T(8,128)(2,1)} %bitcast.7), calls=%async_computation | async-start | bytes 655360 | tf_op jit(solution)/shard_map/all_to_all | solution.py:309

commit v6 on v5

--- a/solution.py
+++ b/solution.py
@@ -61,31 +61,16 @@
     return mm(one_hot(column_of(offset), SPAN), span).astype(BF16)
 
 
-def project_kv(gathered, w_kv, keys, values_t):
-    keys[...] = mm(gathered[...], w_kv[0]).astype(BF16)
-    values = mm(gathered[...], w_kv[1]).astype(BF16)
-    for i in range(values_t.shape[0]):
-        values_t[i] = values[i * WIN : (i + 1) * WIN].T
-
-
 def self_scores(keys, query, tile, head_size):
     lanes = slice(tile * LANES, (tile + 1) * LANES)
     return mm(spread(keys[:, lanes], head_size), query[:, lanes], NT)
 
 
-def self_attention(pending, following, values_t, head_size, store):
+def self_weights(scores, head_size):
     scale = math.log2(math.e) / math.sqrt(head_size)
-    per_tile = LANES // head_size
-    coming = []
-    for tile, scores in enumerate(pending):
-        if following is not None:
-            coming.append(following(tile))
-        count = scores.shape[0] // per_tile
-        for k in range(per_tile):
-            head = tile * per_tile + k
-            weights = softmax_down(scores[k * count : (k + 1) * count], scale)
-            store(head, mm(values_t[head * head_size : (head + 1) * head_size], weights).astype(BF16))
-    return coming
+    heads = LANES // head_size
+    count = scores.shape[0] // heads
+    return [softmax_down(scores[k * count : (k + 1) * count], scale) for k in range(heads)]
 
 
 def cross_attention(keys, values, query, head_size):
@@ -108,9 +93,44 @@
     return pl.ds(pl.multiple_of(w * size, size), size)
 
 
+def pack_rows(parents, slots, packed):
+    chunks, height, _ = packed.shape
+    count = parents.shape[0] // chunks
+    wide = jnp.broadcast_to(slots, (height - count * (parents.shape[1] // LANES), slots.shape[1])).astype(F32)
+    for d in range(chunks):
+        for c in range(parents.shape[1] // LANES):
+            packed[d, c * count : (c + 1) * count] = parents[d * count : (d + 1) * count, c * LANES : (c + 1) * LANES]
+        shift = (-d * count) % slots.shape[1]
+        turned = pltpu.roll(wide, shift, 1) if shift else wide
+        packed[d, height - wide.shape[0] :] = turned[:, :LANES].astype(BF16)
+
+
+def unpack_rows(arrived, parents, features):
+    chunks, height, _ = arrived.shape
+    count = parents // chunks
+    tiles = features // LANES
+    rows = jnp.concatenate(
+        [
+            jnp.concatenate([arrived[d, c * count : (c + 1) * count] for d in range(chunks)], axis=0)
+            for c in range(tiles)
+        ],
+        axis=1,
+    )
+    slots = []
+    for d in range(chunks):
+        begin = d * count % LANES
+        part = arrived[d, tiles * count :].astype(F32)
+        if begin == 0:
+            slots.append(part)
+        else:
+            lane = lax.broadcasted_iota(jnp.int32, part.shape, 1)
+            slots[-1] = jnp.where(lane < begin, slots[-1], pltpu.roll(part, begin, 1))
+    return rows, jnp.concatenate(slots, axis=1)[:1].astype(jnp.int32)
+
+
 def pack_kernel(
     fine, parents, slots, index, gain, parent_gain, first, second, packed, normed, index_v, gains,
-    fine_s, parents_s, slots_s, column_s, sems, *, windows,
+    fine_s, parents_s, slots_s, packed_s, sems, *, windows, tight,
 ):
     rows, features = fine.shape
     odd = lax.rem(lax.axis_index("pix"), 2)
@@ -125,22 +145,24 @@
     ]
     blocks = [slice(w * WIN, (w + 1) * WIN) for w in range(windows)]
     pieces += [(fine.at[here], fine_s.at[here]) for here in blocks]
-    pieces += [(parents_s, packed.at[:, :features]), (column_s, packed.at[:, features:])]
+    pieces += [(packed_s, packed)]
     copies = [pltpu.make_async_copy(src, dst, sems.at[k]) for k, (src, dst) in enumerate(pieces)]
-    for copy in copies[:-2]:
+    for copy in copies[:-1]:
         copy.start()
     copies[0].wait()
-    column_s[...] = column_of(slots_s[...]).astype(F32).astype(BF16)
+    copies[1].wait()
+    if tight:
+        pack_rows(parents_s, slots_s[...], packed_s)
+    else:
+        packed_s[:, :features] = parents_s[...]
+        packed_s[:, features:] = column_of(slots_s[...]).astype(F32).astype(BF16)
     copies[-1].start()
-    copies[1].wait()
-    copies[-2].start()
     for copy in copies[2:7]:
         copy.wait()
     for here, copy in zip(blocks, copies[7:]):
         copy.wait()
         normed[here] = rms_rows(fine_s[here], gains[0])
-    for copy in copies[-2:]:
-        copy.wait()
+    copies[-1].wait()
 
 
 def gate_kernel(before, held, passed):
@@ -180,7 +202,7 @@
     query[...] = mm(normed[...], w_q[...]).astype(BF16)
     for copy in fetch[1:]:
         copy.wait()
-    project_kv(gathered, w_kv, keys, values_t)
+    keys[...] = mm(gathered[...], w_kv[0]).astype(BF16)
     leave = [
         pltpu.make_async_copy(
             w_parent.at[:, c * features : (c + 1) * features], wp.at[c * features : (c + 1) * features], sems.at[3 + c]
@@ -190,30 +212,48 @@
     for copy in leave:
         copy.start()
     split = early.shape[0]
-
-    def scores(w):
+    tiles = range(features // LANES)
+
+    def scores(w, tile):
         here = slice(w * WIN, (w + 1) * WIN)
-        return lambda tile: self_scores(keys[here], query[here], tile, head_size)
-
-    pending = [scores(0)(tile) for tile in range(features // LANES)]
-    for w in range(windows):
+        return self_scores(keys[here], query[here], tile, head_size)
+
+    def project_values(begin, end):
+        values = mm(gathered[...], w_kv[1][:, begin:end]).astype(BF16)
+        for w in range(windows):
+            values_t[w, begin:end] = values[w * WIN : (w + 1) * WIN].T
+
+    def apply(w, tile, weights):
         out = early.at[w] if w < split else late.at[w - split]
-
-        def store(head, value):
-            out[head * head_size : (head + 1) * head_size] = value
-
-        following = scores(w + 1) if w + 1 < windows else None
-        pending = self_attention(pending, following, values_t[w], head_size, store)
-        if w < split:
+        for k, weight in enumerate(weights):
+            head = slice(tile * LANES + k * head_size, tile * LANES + (k + 1) * head_size)
+            out[head] = mm(values_t[w, head], weight).astype(BF16)
+        if tile == tiles[-1] and w < split:
             leave.append(pltpu.make_async_copy(out, early_h.at[w], sems.at[5 + w]))
             leave[-1].start()
+
+    pending = [scores(0, tile) for tile in tiles]
+    before = []
+    for w in range(windows):
+        coming, weights = [], []
+        for tile in tiles:
+            if w + 1 < windows:
+                coming.append(scores(w + 1, tile))
+            weights.append(self_weights(pending[tile], head_size))
+            if w == 0 and tile % 2 == 0:
+                project_values(tile * LANES, min(tile + 2, len(tiles)) * LANES)
+            if w > 0:
+                apply(w - 1, tile, before[tile])
+        pending, before = coming, weights
+    for tile in tiles:
+        apply(windows - 1, tile, before[tile])
     for copy in leave:
         copy.wait()
 
 
 def cross_kernel(
     query, late, gains, arrived, wp, early_h, fine_h, w_out, out, early, fine, wo, out_s, p_keys, p_values, sems,
-    *, windows, head_size, all_rows,
+    *, windows, head_size, all_rows, tight,
 ):
     rows, features = fine.shape
     fetch = [
@@ -223,9 +263,15 @@
     ]
     for copy in fetch:
         copy.start()
-    count = arrived.shape[0]
-    places = one_hot(arrived[:, features:].astype(F32).astype(jnp.int32), count)
-    ordered = mm(places, arrived[:, :features], TN).astype(BF16)
+    count = p_keys.shape[0]
+    if tight:
+        parents, slots = unpack_rows(arrived, count, features)
+        place = lax.broadcasted_iota(jnp.int32, (count, count), 0)
+        places = jnp.where(place == jnp.broadcast_to(slots, (count, count)), 1.0, 0.0).astype(BF16)
+        ordered = mm(places, parents).astype(BF16)
+    else:
+        places = one_hot(arrived[:, features:].astype(F32).astype(jnp.int32), count)
+        ordered = mm(places, arrived[:, :features], TN).astype(BF16)
     normed_parents = rms_rows(ordered, gains[1])
     p_keys[...] = mm(normed_parents, wp[:features]).astype(BF16)
     p_values[...] = mm(normed_parents, wp[features:]).astype(BF16)
@@ -257,6 +303,9 @@
     parents = parent_tokens.shape[0]
     devices = lax.axis_size("pix")
     windows = rows // WIN
+    share = parents // devices
+    tight = share % 16 == 0 and LANES % share == 0 and features % LANES == 0
+    packing = (devices, share * (features // LANES) + 16, LANES) if tight else (parents, features + LANES)
     sizes = dict(windows=windows, head_size=features // HEADS, all_rows=rows * devices)
     params = pltpu.CompilerParams(vmem_limit_bytes=32 * MIB)
     semaphores = pltpu.SemaphoreType.DMA
@@ -269,11 +318,11 @@
 
     fine, weights = far(fine_tokens), far(w_qkv)
     first, second, packed, normed, index, gains = pl.pallas_call(
-        functools.partial(pack_kernel, windows=windows),
+        functools.partial(pack_kernel, windows=windows, tight=tight),
         out_shape=[
             near(HALO, features),
             near(HALO, features),
-            pltpu.HBM((parents, features + LANES), BF16),
+            pltpu.HBM(packing, BF16),
             near(rows, features),
             near(windows, 1, WIN, dtype=jnp.int32),
             near(2, 1, features, dtype=F32),
@@ -284,8 +333,8 @@
             near(rows, features),
             near(parents, features),
             near(1, parents, dtype=jnp.int32),
-            near(parents, LANES),
-            semaphores((windows + 9,)),
+            near(*packing),
+            semaphores((windows + 8,)),
         ],
         compiler_params=params,
         name="pack",
@@ -299,7 +348,7 @@
     second_in = lax.ppermute(second, "pix", across)
     packed = pl.pallas_call(
         gate_kernel,
-        out_shape=pltpu.HBM((parents, features + LANES), BF16),
+        out_shape=pltpu.HBM(packing, BF16),
         in_specs=[VMEM, HBM],
         out_specs=HBM,
         input_output_aliases={1: 0},
@@ -336,7 +385,7 @@
     )(normed, index, gains, first_in, second_in, weights, far(w_parent))
 
     return pl.pallas_call(
-        functools.partial(cross_kernel, **sizes),
+        functools.partial(cross_kernel, tight=tight, **sizes),
         out_shape=pltpu.HBM((rows, features), BF16),
         in_specs=[VMEM] * 5 + [HBM] * 3,
         out_specs=HBM,

time: 27 us -> 26.3 us (0.974)
  waiting for transfers between devices: 1.83 us -> 1.3 us
    all_to_all x1, waiting for transfers between devices: 1.16 us -> 0.62 us  [on_device(): lax.all_to_all(packed, 'pix', split_axis=0, concat_axis=0, tiled=True)]
where the time goes in v6:
time: 26.3 us; the launch traced here: 26.1 us
  Pallas kernels  14.8 us (56%)
  starting transfers between devices  10 us (38%)
  waiting for transfers between devices  1.3 us (5%)
    pallas_call x1, Pallas kernels, on_device(): pl.pallas_call(functools.partial(self_kernel, **sizes), out_shape=[near(r...  7.93 us
    pallas_call x1, Pallas kernels, on_device(): pl.pallas_call(functools.partial(cross_kernel, tight=tight, **sizes), out...  4.9 us
    ppermute x1, starting transfers between devices, on_device(): second_in = lax.ppermute(second, 'pix', across)  3.54 us
    all_to_all x1, starting transfers between devices, on_device(): lax.all_to_all(packed, 'pix', split_axis=0, concat_axis=0, tiled=True)  3.42 us
    ppermute x1, starting transfers between devices, on_device(): first_in = lax.ppermute(first, 'pix', pairs)  3.03 us
    pallas_call x1, Pallas kernels, on_device(): pl.pallas_call(functools.partial(pack_kernel, windows=windows, tight=tigh...  1.91 us
    ppermute x1, waiting for transfers between devices, on_device(): second_in = lax.ppermute(second, 'pix', across)  0.68 us
    all_to_all x1, waiting for transfers between devices, on_device(): lax.all_to_all(packed, 'pix', split_axis=0, concat_axis=0, tiled=True)  0.62 us
  transfers between devices with their start and end apart: 3, of which 2 were waited for; matrix products, arithmetic and copies ran while one was open for 0% of the time, Pallas kernels for 30%

profile of v6, /device:TPU:0, one launch (start us, length us, event | category | flops | bytes accessed | tf_op | source)
XLA Modules:
  0.0 26.1 jit_solution(13738059244838666550)
XLA Ops:
  0.0 1.9 %pack.1 = (bf16[128,512]{1,0:T(8,128)(2,1)S(1)}, bf16[128,512]{1,0:T(8,128)(2,1)S(1)}, bf16[8,144,128]{2,1,0:T(8,128)(2,1)}, bf16[1024,512]{1,0:T(8,128)(2,1)S(1...) custom-call(bf16[1024,512]{1,0:T(8,128)(2,1)} %fine_h.1, bf16[256,512]{1,0:T(8,128)(2,1)} %parents.1, ...), custom_call_target="tpu_custom_call" | custom-call | tf_op jit(solution)/shard_map/pack/pallas_call | solution.py:320
  1.9 3.0 %collective-permute-start = (bf16[128,512]{1,0:T(8,128)(2,1)S(1)}, bf16[128,512]{1,0:T(8,128)(2,1)S(1)}, u32[]{:S(2)}, u32[]{:S(2)}) collective-permute-start(bf16[128,512]{1,0:T(8,128)(2,1)S(1)} %get-tuple-element.18), channel_id=1, source_target_pairs={{0,4},{4,0},{8,12},{12,8},{16,20},{20,16},{24,28},{28,24},{1,5},{5... | collective-permute-start | bytes 393224 | tf_op jit(solution)/shard_map/ppermute | solution.py:347
  5.0 3.5 %collective-permute-start.1 = (bf16[128,512]{1,0:T(8,128)(2,1)S(1)}, bf16[128,512]{1,0:T(8,128)(2,1)S(1)}, u32[]{:S(2)}, u32[]{:S(2)}) collective-permute-start(bf16[128,512]{1,0:T(8,128)(2,1)S(1)} %get-tuple-element.19.before), channel_id=1, source_target_pairs={{0,28},{4,8},{8,4},{12,16},{16,12},{20,24},{24,20},{28,0},{1,29},{... | collective-permute-start | bytes 393224 | tf_op jit(solution)/shard_map/ppermute | solution.py:348
  8.5 3.4 %all-to-all-start = ((bf16[8,144,128]{2,1,0:T(8,128)(2,1)}), bf16[8,144,128]{2,1,0:T(8,128)(2,1)S(1)}, u32[]{:S(2)}, u32[]{:S(2)}) async-start(bf16[8,144,128]{2,1,0:T(8,128)(2,1)} %gate.1), calls=%async_computation | async-start | bytes 589824 | tf_op jit(solution)/shard_map/all_to_all | solution.py:358
  11.9 0.0 collective-permute-done.first
  11.9 0.7 %collective-permute-done.1.second = bf16[128,512]{1,0:T(8,128)(2,1)S(1)} collective-permute-done((bf16[128,512]{1,0:T(8,128)(2,1)S(1)}, bf16[128,512]{1,0:T(8,128)(2,1)S(1)}, u32[]{:S(2)}, u32[]{:S(2)}) %collective-permute-start.1) | collective-permute-done | bytes 131104 | tf_op jit(solution)/shard_map/ppermute | solution.py:348
  12.6 7.9 %self.1 = (bf16[1024,512]{1,0:T(8,128)(2,1)S(1)}, bf16[2,512,256]{2,1,0:T(8,128)(2,1)}, bf16[2,512,256]{2,1,0:T(8,128)(2,1)S(1)}, bf16[1024,512]{1,0:T(8,128)(2,1)S(1)}) custom-call(bf16[1024,512]{1,0:T(8,128)(2,1)S(1)} %get-tuple-element.15.normed, s32[4,1,256]{2,1,0:T(1,128)S(1)} %get-tuple-element.16.index, ...), custom_call_target="tpu_custom_call", output_to_operand_aliasing={{3}: (0, {})} | custom-call | flops 16000000000 | bytes 4000000 | tf_op jit(solution)/shard_map/self/pallas_call | solution.py:361
  20.6 0.6 %all-to-all-done.arrived = bf16[8,144,128]{2,1,0:T(8,128)(2,1)S(1)} async-done(((bf16[8,144,128]{2,1,0:T(8,128)(2,1)}), bf16[8,144,128]{2,1,0:T(8,128)(2,1)S(1)}, u32[]{:S(2)}, u32[]{:S(2)}) %all-to-all-start) | async-done | bytes 294944 | tf_op jit(solution)/shard_map/all_to_all | solution.py:358
  21.2 4.9 %cross.1 = bf16[1024,512]{1,0:T(8,128)(2,1)} custom-call(bf16[1024,512]{1,0:T(8,128)(2,1)S(1)} %get-tuple-element.20.query, bf16[2,512,256]{2,1,0:T(8,128)(2,1)S(1)} %get-tuple-element.21.late, f32[2,1,512]{2,1,0:T(1,128)S(1)} %get-tuple-element.17.gains, bf16[8,144,128]{2,1,0:T(8,128)(2,1)S(1)} %all-to-all-done.arrived, ...), custom_call_target="tpu_custom_call" | custom-call | flops 5000000000 | bytes 6000000 | tf_op jit(solution)/shard_map/cross/pallas_call | solution.py:387
  (1 shorter events, 0.0 us)
Async XLA Ops:
  1.9 10.0 %collective-permute-start = (bf16[128,512]{1,0:T(8,128)(2,1)S(1)}, bf16[128,512]{1,0:T(8,128)(2,1)S(1)}, u32[]{:S(2)}, u32[]{:S(2)}) collective-permute-start(bf16[128,512]{1,0:T(8,128)(2,1)S(1)} %get-tuple-element.18), channel_id=1, source_target_pairs={{0,4},{4,0},{8,12},{12,8},{16,20},{20,16},{24,28},{28,24},{1,5},{5... | collective-permute-start | bytes 393224 | tf_op jit(solution)/shard_map/ppermute | solution.py:347
  5.0 7.7 %collective-permute-start.1 = (bf16[128,512]{1,0:T(8,128)(2,1)S(1)}, bf16[128,512]{1,0:T(8,128)(2,1)S(1)}, u32[]{:S(2)}, u32[]{:S(2)}) collective-permute-start(bf16[128,512]{1,0:T(8,128)(2,1)S(1)} %get-tuple-element.19.before), channel_id=1, source_target_pairs={{0,28},{4,8},{8,4},{12,16},{16,12},{20,24},{24,20},{28,0},{1,29},{... | collective-permute-start | bytes 393224 | tf_op jit(solution)/shard_map/ppermute | solution.py:348
  8.5 12.7 %all-to-all-start = ((bf16[8,144,128]{2,1,0:T(8,128)(2,1)}), bf16[8,144,128]{2,1,0:T(8,128)(2,1)S(1)}, u32[]{:S(2)}, u32[]{:S(2)}) async-start(bf16[8,144,128]{2,1,0:T(8,128)(2,1)} %gate.1), calls=%async_computation | async-start | bytes 589824 | tf_op jit(solution)/shard_map/all_to_all | solution.py:358

commit v7 on v6

--- a/solution.py
+++ b/solution.py
@@ -93,14 +93,15 @@
     return pl.ds(pl.multiple_of(w * size, size), size)
 
 
-def pack_rows(parents, slots, packed):
+def pack_rows(parents, slots, packed, order):
     chunks, height, _ = packed.shape
     count = parents.shape[0] // chunks
     wide = jnp.broadcast_to(slots, (height - count * (parents.shape[1] // LANES), slots.shape[1])).astype(F32)
-    for d in range(chunks):
+    for d, owner in enumerate(order):
+        own = slice(owner * count, (owner + 1) * count)
         for c in range(parents.shape[1] // LANES):
-            packed[d, c * count : (c + 1) * count] = parents[d * count : (d + 1) * count, c * LANES : (c + 1) * LANES]
-        shift = (-d * count) % slots.shape[1]
+            packed[d, c * count : (c + 1) * count] = parents[own, c * LANES : (c + 1) * LANES]
+        shift = (-owner * count) % slots.shape[1]
         turned = pltpu.roll(wide, shift, 1) if shift else wide
         packed[d, height - wide.shape[0] :] = turned[:, :LANES].astype(BF16)
 
@@ -130,7 +131,7 @@
 
 def pack_kernel(
     fine, parents, slots, index, gain, parent_gain, first, second, packed, normed, index_v, gains,
-    fine_s, parents_s, slots_s, packed_s, sems, *, windows, tight,
+    fine_s, parents_s, slots_s, packed_s, sems, *, windows, order,
 ):
     rows, features = fine.shape
     odd = lax.rem(lax.axis_index("pix"), 2)
@@ -151,8 +152,8 @@
         copy.start()
     copies[0].wait()
     copies[1].wait()
-    if tight:
-        pack_rows(parents_s, slots_s[...], packed_s)
+    if order:
+        pack_rows(parents_s, slots_s[...], packed_s, order)
     else:
         packed_s[:, :features] = parents_s[...]
         packed_s[:, features:] = column_of(slots_s[...]).astype(F32).astype(BF16)
@@ -306,6 +307,7 @@
     share = parents // devices
     tight = share % 16 == 0 and LANES % share == 0 and features % LANES == 0
     packing = (devices, share * (features // LANES) + 16, LANES) if tight else (parents, features + LANES)
+    order = tuple((d + devices // 4) % devices for d in range(devices)) if tight else None
     sizes = dict(windows=windows, head_size=features // HEADS, all_rows=rows * devices)
     params = pltpu.CompilerParams(vmem_limit_bytes=32 * MIB)
     semaphores = pltpu.SemaphoreType.DMA
@@ -318,7 +320,7 @@
 
     fine, weights = far(fine_tokens), far(w_qkv)
     first, second, packed, normed, index, gains = pl.pallas_call(
-        functools.partial(pack_kernel, windows=windows, tight=tight),
+        functools.partial(pack_kernel, windows=windows, order=order),
         out_shape=[
             near(HALO, features),
             near(HALO, features),
@@ -355,7 +357,8 @@
         compiler_params=params,
         name="gate",
     )(second, far(packed))
-    arrived = lax.all_to_all(packed, "pix", split_axis=0, concat_axis=0, tiled=True)
+    groups = [list(order)] if tight else None
+    arrived = lax.all_to_all(packed, "pix", split_axis=0, concat_axis=0, tiled=True, axis_index_groups=groups)
 
     split = windows // 2
     query, early, late, wp = pl.pallas_call(

time: 26.3 us -> 25.7 us (0.977)
  waiting for transfers between devices: 1.3 us -> 0.73 us
    all_to_all x1, waiting for transfers between devices: 0.62 us -> 0.01 us  [on_device(): lax.all_to_all(packed, 'pix', split_axis=0, concat_axis=0, tiled=True, ax...]
  transfers between devices with their start and end apart: 3 -> 3, of which waited for: 2 -> 1; matrix products, arithmetic and copies ran while one was open for 0% -> 0% of each run, Pallas kernels for 30% -> 31%
where the time goes in v7:
time: 25.7 us; the launch traced here: 25.5 us
  Pallas kernels  14.7 us (57%)
  starting transfers between devices  9.95 us (39%)
  waiting for transfers between devices  0.73 us (3%)
    pallas_call x1, Pallas kernels, on_device(): pl.pallas_call(functools.partial(self_kernel, **sizes), out_shape=[near(r...  7.93 us
    pallas_call x1, Pallas kernels, on_device(): pl.pallas_call(functools.partial(cross_kernel, tight=tight, **sizes), out...  4.89 us
    ppermute x1, starting transfers between devices, on_device(): second_in = lax.ppermute(second, 'pix', across)  3.54 us
    all_to_all x1, starting transfers between devices, on_device(): lax.all_to_all(packed, 'pix', split_axis=0, concat_axis=0, tiled=True, ax...  3.37 us
    ppermute x1, starting transfers between devices, on_device(): first_in = lax.ppermute(first, 'pix', pairs)  3.03 us
    pallas_call x1, Pallas kernels, on_device(): pl.pallas_call(functools.partial(pack_kernel, windows=windows, order=orde...  1.91 us
    ppermute x1, waiting for transfers between devices, on_device(): second_in = lax.ppermute(second, 'pix', across)  0.73 us
  transfers between devices with their start and end apart: 3, of which 1 were waited for; matrix products, arithmetic and copies ran while one was open for 0% of the time, Pallas kernels for 31%

profile of v7, /device:TPU:0, one launch (start us, length us, event | category | flops | bytes accessed | tf_op | source)
XLA Modules:
  0.0 25.5 jit_solution(10570677511797702992)
XLA Ops:
  0.0 1.9 %pack.1 = (bf16[128,512]{1,0:T(8,128)(2,1)S(1)}, bf16[128,512]{1,0:T(8,128)(2,1)S(1)}, bf16[8,144,128]{2,1,0:T(8,128)(2,1)}, bf16[1024,512]{1,0:T(8,128)(2,1)S(1...) custom-call(bf16[1024,512]{1,0:T(8,128)(2,1)} %fine_h.1, bf16[256,512]{1,0:T(8,128)(2,1)} %parents.1, ...), custom_call_target="tpu_custom_call" | custom-call | tf_op jit(solution)/shard_map/pack/pallas_call | solution.py:322
  1.9 3.0 %collective-permute-start = (bf16[128,512]{1,0:T(8,128)(2,1)S(1)}, bf16[128,512]{1,0:T(8,128)(2,1)S(1)}, u32[]{:S(2)}, u32[]{:S(2)}) collective-permute-start(bf16[128,512]{1,0:T(8,128)(2,1)S(1)} %get-tuple-element.18), channel_id=1, source_target_pairs={{0,4},{4,0},{8,12},{12,8},{16,20},{20,16},{24,28},{28,24},{1,5},{5... | collective-permute-start | bytes 393224 | tf_op jit(solution)/shard_map/ppermute | solution.py:349
  5.0 3.5 %collective-permute-start.1 = (bf16[128,512]{1,0:T(8,128)(2,1)S(1)}, bf16[128,512]{1,0:T(8,128)(2,1)S(1)}, u32[]{:S(2)}, u32[]{:S(2)}) collective-permute-start(bf16[128,512]{1,0:T(8,128)(2,1)S(1)} %get-tuple-element.19.before), channel_id=1, source_target_pairs={{0,28},{4,8},{8,4},{12,16},{16,12},{20,24},{24,20},{28,0},{1,29},{... | collective-permute-start | bytes 393224 | tf_op jit(solution)/shard_map/ppermute | solution.py:350
  8.5 3.4 %all-to-all-start = ((bf16[8,144,128]{2,1,0:T(8,128)(2,1)}), bf16[8,144,128]{2,1,0:T(8,128)(2,1)S(1)}, u32[]{:S(2)}, u32[]{:S(2)}) async-start(bf16[8,144,128]{2,1,0:T(8,128)(2,1)} %gate.1), calls=%async_computation | async-start | bytes 589824 | tf_op jit(solution)/shard_map/all_to_all | solution.py:361
  11.9 0.0 collective-permute-done.first
  11.9 0.7 %collective-permute-done.1.second = bf16[128,512]{1,0:T(8,128)(2,1)S(1)} collective-permute-done((bf16[128,512]{1,0:T(8,128)(2,1)S(1)}, bf16[128,512]{1,0:T(8,128)(2,1)S(1)}, u32[]{:S(2)}, u32[]{:S(2)}) %collective-permute-start.1) | collective-permute-done | bytes 131104 | tf_op jit(solution)/shard_map/ppermute | solution.py:350
  12.6 7.9 %self.1 = (bf16[1024,512]{1,0:T(8,128)(2,1)S(1)}, bf16[2,512,256]{2,1,0:T(8,128)(2,1)}, bf16[2,512,256]{2,1,0:T(8,128)(2,1)S(1)}, bf16[1024,512]{1,0:T(8,128)(2,1)S(1)}) custom-call(bf16[1024,512]{1,0:T(8,128)(2,1)S(1)} %get-tuple-element.15.normed, s32[4,1,256]{2,1,0:T(1,128)S(1)} %get-tuple-element.16.index, ...), custom_call_target="tpu_custom_call", output_to_operand_aliasing={{3}: (0, {})} | custom-call | flops 16000000000 | bytes 4000000 | tf_op jit(solution)/shard_map/self/pallas_call | solution.py:364
  20.6 0.0 all-to-all-done.arrived
  20.6 4.9 %cross.1 = bf16[1024,512]{1,0:T(8,128)(2,1)} custom-call(bf16[1024,512]{1,0:T(8,128)(2,1)S(1)} %get-tuple-element.20.query, bf16[2,512,256]{2,1,0:T(8,128)(2,1)S(1)} %get-tuple-element.21.late, f32[2,1,512]{2,1,0:T(1,128)S(1)} %get-tuple-element.17.gains, bf16[8,144,128]{2,1,0:T(8,128)(2,1)S(1)} %all-to-all-done.arrived, ...), custom_call_target="tpu_custom_call" | custom-call | flops 5000000000 | bytes 6000000 | tf_op jit(solution)/shard_map/cross/pallas_call | solution.py:390
  (1 shorter events, 0.0 us)
Async XLA Ops:
  1.9 10.0 %collective-permute-start = (bf16[128,512]{1,0:T(8,128)(2,1)S(1)}, bf16[128,512]{1,0:T(8,128)(2,1)S(1)}, u32[]{:S(2)}, u32[]{:S(2)}) collective-permute-start(bf16[128,512]{1,0:T(8,128)(2,1)S(1)} %get-tuple-element.18), channel_id=1, source_target_pairs={{0,4},{4,0},{8,12},{12,8},{16,20},{20,16},{24,28},{28,24},{1,5},{5... | collective-permute-start | bytes 393224 | tf_op jit(solution)/shard_map/ppermute | solution.py:349
  5.0 7.7 %collective-permute-start.1 = (bf16[128,512]{1,0:T(8,128)(2,1)S(1)}, bf16[128,512]{1,0:T(8,128)(2,1)S(1)}, u32[]{:S(2)}, u32[]{:S(2)}) collective-permute-start(bf16[128,512]{1,0:T(8,128)(2,1)S(1)} %get-tuple-element.19.before), channel_id=1, source_target_pairs={{0,28},{4,8},{8,4},{12,16},{16,12},{20,24},{24,20},{28,0},{1,29},{... | collective-permute-start | bytes 393224 | tf_op jit(solution)/shard_map/ppermute | solution.py:350
  8.5 12.1 %all-to-all-start = ((bf16[8,144,128]{2,1,0:T(8,128)(2,1)}), bf16[8,144,128]{2,1,0:T(8,128)(2,1)S(1)}, u32[]{:S(2)}, u32[]{:S(2)}) async-start(bf16[8,144,128]{2,1,0:T(8,128)(2,1)} %gate.1), calls=%async_computation | async-start | bytes 589824 | tf_op jit(solution)/shard_map/all_to_all | solution.py:361

commit v8 on v7

--- a/solution.py
+++ b/solution.py
@@ -130,8 +130,8 @@
 
 
 def pack_kernel(
-    fine, parents, slots, index, gain, parent_gain, first, second, packed, normed, index_v, gains,
-    fine_s, parents_s, slots_s, packed_s, sems, *, windows, order,
+    fine, parents, slots, index, gain, parent_gain, first, second, packed, fine_v, index_v, gains, parents_s, slots_s, sems,
+    *, order,
 ):
     rows, features = fine.shape
     odd = lax.rem(lax.axis_index("pix"), 2)
@@ -143,31 +143,28 @@
         (gain, gains.at[0]),
         (parent_gain, gains.at[1]),
         (index, index_v),
+        (fine, fine_v),
     ]
-    blocks = [slice(w * WIN, (w + 1) * WIN) for w in range(windows)]
-    pieces += [(fine.at[here], fine_s.at[here]) for here in blocks]
-    pieces += [(packed_s, packed)]
     copies = [pltpu.make_async_copy(src, dst, sems.at[k]) for k, (src, dst) in enumerate(pieces)]
-    for copy in copies[:-1]:
+    for copy in copies:
         copy.start()
     copies[0].wait()
     copies[1].wait()
     if order:
-        pack_rows(parents_s, slots_s[...], packed_s, order)
+        pack_rows(parents_s, slots_s[...], packed, order)
     else:
-        packed_s[:, :features] = parents_s[...]
-        packed_s[:, features:] = column_of(slots_s[...]).astype(F32).astype(BF16)
-    copies[-1].start()
-    for copy in copies[2:7]:
+        packed[:, :features] = parents_s[...]
+        packed[:, features:] = column_of(slots_s[...]).astype(F32).astype(BF16)
+    for copy in copies[2:]:
         copy.wait()
-    for here, copy in zip(blocks, copies[7:]):
-        copy.wait()
-        normed[here] = rms_rows(fine_s[here], gains[0])
-    copies[-1].wait()
-
-
-def gate_kernel(before, held, passed):
-    pass
+
+
+def norm_kernel(before, packed, fine, gains, passed, normed, sem):
+    copy = pltpu.make_async_copy(packed, passed, sem)
+    copy.start()
+    for start in range(0, fine.shape[0], WIN):
+        normed[start : start + WIN] = rms_rows(fine[start : start + WIN], gains[0])
+    copy.wait()
 
 
 def self_kernel(
@@ -319,24 +316,22 @@
         return pltpu.with_memory_space_constraint(x, pltpu.HBM)
 
     fine, weights = far(fine_tokens), far(w_qkv)
-    first, second, packed, normed, index, gains = pl.pallas_call(
-        functools.partial(pack_kernel, windows=windows, order=order),
+    first, second, packed, fine_v, index, gains = pl.pallas_call(
+        functools.partial(pack_kernel, order=order),
         out_shape=[
             near(HALO, features),
             near(HALO, features),
-            pltpu.HBM(packing, BF16),
+            near(*packing),
             near(rows, features),
             near(windows, 1, WIN, dtype=jnp.int32),
             near(2, 1, features, dtype=F32),
         ],
         in_specs=[HBM] * 6,
-        out_specs=[VMEM, VMEM, HBM] + [VMEM] * 3,
+        out_specs=[VMEM] * 6,
         scratch_shapes=[
-            near(rows, features),
             near(parents, features),
             near(1, parents, dtype=jnp.int32),
-            near(*packing),
-            semaphores((windows + 8,)),
+            semaphores((8,)),
         ],
         compiler_params=params,
         name="pack",
@@ -348,15 +343,16 @@
     across = [(i, (i - 1 + 2 * (i % 2)) % devices) for i in range(devices)]
     first_in = lax.ppermute(first, "pix", pairs)
     second_in = lax.ppermute(second, "pix", across)
-    packed = pl.pallas_call(
-        gate_kernel,
-        out_shape=pltpu.HBM(packing, BF16),
-        in_specs=[VMEM, HBM],
-        out_specs=HBM,
-        input_output_aliases={1: 0},
+    packed, normed = pl.pallas_call(
+        norm_kernel,
+        out_shape=[pltpu.HBM(packing, BF16), near(rows, features)],
+        in_specs=[VMEM] * 4,
+        out_specs=[HBM, VMEM],
+        input_output_aliases={2: 1},
+        scratch_shapes=[semaphores],
         compiler_params=params,
-        name="gate",
-    )(second, far(packed))
+        name="norm",
+    )(second, packed, fine_v, gains)
     groups = [list(order)] if tight else None
     arrived = lax.all_to_all(packed, "pix", split_axis=0, concat_axis=0, tiled=True, axis_index_groups=groups)
 

time: 25.7 us -> 25.4 us (0.988)
  waiting for transfers between devices: 0.73 us -> 0.01 us
  Pallas kernels: 14.7 us -> 15.1 us
    ppermute x1, waiting for transfers between devices: 0.73 us -> 0.01 us  [on_device(): second_in = lax.ppermute(second, 'pix', across)]
    pallas_call x2, Pallas kernels: 1.91 us -> 2.29 us  [the longest x1 1.57 us: on_device(): pl.pallas_call(functools.partial(pack_kernel, order=order), out_shape=[ne...]
  transfers between devices with their start and end apart: 3 -> 3, of which waited for: 1 -> 0; matrix products, arithmetic and copies ran while one was open for 0% -> 0% of each run, Pallas kernels for 31% -> 34%
where the time goes in v8:
time: 25.4 us; the launch traced here: 25.2 us
  Pallas kernels  15.1 us (59%)
  starting transfers between devices  9.96 us (39%)
    pallas_call x1, Pallas kernels, on_device(): pl.pallas_call(functools.partial(self_kernel, **sizes), out_shape=[near(r...  7.94 us
    pallas_call x1, Pallas kernels, on_device(): pl.pallas_call(functools.partial(cross_kernel, tight=tight, **sizes), out...  4.89 us
    ppermute x1, starting transfers between devices, on_device(): second_in = lax.ppermute(second, 'pix', across)  3.54 us
    all_to_all x1, starting transfers between devices, on_device(): lax.all_to_all(packed, 'pix', split_axis=0, concat_axis=0, tiled=True, ax...  3.39 us
    ppermute x1, starting transfers between devices, on_device(): first_in = lax.ppermute(first, 'pix', pairs)  3.03 us
    pallas_call x1, Pallas kernels, on_device(): pl.pallas_call(functools.partial(pack_kernel, order=order), out_shape=[ne...  1.57 us
    pallas_call x1, Pallas kernels, on_device(): pl.pallas_call(norm_kernel, out_shape=[pltpu.HBM(packing, BF16), near(row...  0.72 us
  transfers between devices with their start and end apart: 3, of which 0 were waited for; matrix products, arithmetic and copies ran while one was open for 0% of the time, Pallas kernels for 34%

profile of v8, /device:TPU:0, one launch (start us, length us, event | category | flops | bytes accessed | tf_op | source)
XLA Modules:
  0.0 25.2 jit_solution(1292548420413450033)
XLA Ops:
  0.0 1.6 %pack.1 = (bf16[128,512]{1,0:T(8,128)(2,1)S(1)}, bf16[128,512]{1,0:T(8,128)(2,1)S(1)}, bf16[8,144,128]{2,1,0:T(8,128)(2,1)S(1)}, bf16[1024,512]{1,0:T(8,128)(2,1...) custom-call(bf16[1024,512]{1,0:T(8,128)(2,1)} %fine_h.1, bf16[256,512]{1,0:T(8,128)(2,1)} %parents.1, ...), custom_call_target="tpu_custom_call" | custom-call | tf_op jit(solution)/shard_map/pack/pallas_call | solution.py:319
  1.6 3.0 %collective-permute-start = (bf16[128,512]{1,0:T(8,128)(2,1)S(1)}, bf16[128,512]{1,0:T(8,128)(2,1)S(1)}, u32[]{:S(2)}, u32[]{:S(2)}) collective-permute-start(bf16[128,512]{1,0:T(8,128)(2,1)S(1)} %get-tuple-element.23), channel_id=1, source_target_pairs={{0,4},{4,0},{8,12},{12,8},{16,20},{20,16},{24,28},{28,24},{1,5},{5... | collective-permute-start | bytes 393224 | tf_op jit(solution)/shard_map/ppermute | solution.py:344
  4.6 3.5 %collective-permute-start.1 = (bf16[128,512]{1,0:T(8,128)(2,1)S(1)}, bf16[128,512]{1,0:T(8,128)(2,1)S(1)}, u32[]{:S(2)}, u32[]{:S(2)}) collective-permute-start(bf16[128,512]{1,0:T(8,128)(2,1)S(1)} %get-tuple-element.17.before), channel_id=1, source_target_pairs={{0,28},{4,8},{8,4},{12,16},{16,12},{20,24},{24,20},{28,0},{1,29},{... | collective-permute-start | bytes 393224 | tf_op jit(solution)/shard_map/ppermute | solution.py:345
  8.2 0.7 %norm.1 = (bf16[8,144,128]{2,1,0:T(8,128)(2,1)}, bf16[1024,512]{1,0:T(8,128)(2,1)S(1)}) custom-call(bf16[128,512]{1,0:T(8,128)(2,1)S(1)} %get-tuple-element.17.before, bf16[8,144,128]{2,1,0:T(8,128)(2,1)S(1)} %get-tuple-element.18.packed, bf16[1024,512]{1,0:T(8,128)(2,1)S(1)} %get-tuple-element.19.fine, ...), custom_call_target="tpu_custom_call", output_to_operand_aliasing={{1}: (2, {})} | custom-call | tf_op jit(solution)/shard_map/norm/pallas_call | solution.py:346
  8.9 3.4 %all-to-all-start = ((bf16[8,144,128]{2,1,0:T(8,128)(2,1)}), bf16[8,144,128]{2,1,0:T(8,128)(2,1)S(1)}, u32[]{:S(2)}, u32[]{:S(2)}) async-start(bf16[8,144,128]{2,1,0:T(8,128)(2,1)} %get-tuple-element.26), calls=%async_computation | async-start | bytes 589824 | tf_op jit(solution)/shard_map/all_to_all | solution.py:357
  12.3 0.0 collective-permute-done.first
  12.3 0.0 collective-permute-done.1.second
  12.3 7.9 %self.1 = (bf16[1024,512]{1,0:T(8,128)(2,1)S(1)}, bf16[2,512,256]{2,1,0:T(8,128)(2,1)}, bf16[2,512,256]{2,1,0:T(8,128)(2,1)S(1)}, bf16[1024,512]{1,0:T(8,128)(2,1)S(1)}) custom-call(bf16[1024,512]{1,0:T(8,128)(2,1)S(1)} %get-tuple-element.21.normed, s32[4,1,256]{2,1,0:T(1,128)S(1)} %get-tuple-element.22.index, ...), custom_call_target="tpu_custom_call", output_to_operand_aliasing={{3}: (0, {})} | custom-call | flops 16000000000 | bytes 4000000 | tf_op jit(solution)/shard_map/self/pallas_call | solution.py:360
  20.2 0.0 all-to-all-done.arrived
  20.3 4.9 %cross.1 = bf16[1024,512]{1,0:T(8,128)(2,1)} custom-call(bf16[1024,512]{1,0:T(8,128)(2,1)S(1)} %get-tuple-element.24.query, bf16[2,512,256]{2,1,0:T(8,128)(2,1)S(1)} %get-tuple-element.25.late, f32[2,1,512]{2,1,0:T(1,128)S(1)} %get-tuple-element.20.gains, bf16[8,144,128]{2,1,0:T(8,128)(2,1)S(1)} %all-to-all-done.arrived, ...), custom_call_target="tpu_custom_call" | custom-call | flops 5000000000 | bytes 6000000 | tf_op jit(solution)/shard_map/cross/pallas_call | solution.py:386
Async XLA Ops:
  1.6 10.7 %collective-permute-start = (bf16[128,512]{1,0:T(8,128)(2,1)S(1)}, bf16[128,512]{1,0:T(8,128)(2,1)S(1)}, u32[]{:S(2)}, u32[]{:S(2)}) collective-permute-start(bf16[128,512]{1,0:T(8,128)(2,1)S(1)} %get-tuple-element.23), channel_id=1, source_target_pairs={{0,4},{4,0},{8,12},{12,8},{16,20},{20,16},{24,28},{28,24},{1,5},{5... | collective-permute-start | bytes 393224 | tf_op jit(solution)/shard_map/ppermute | solution.py:344
  4.6 7.7 %collective-permute-start.1 = (bf16[128,512]{1,0:T(8,128)(2,1)S(1)}, bf16[128,512]{1,0:T(8,128)(2,1)S(1)}, u32[]{:S(2)}, u32[]{:S(2)}) collective-permute-start(bf16[128,512]{1,0:T(8,128)(2,1)S(1)} %get-tuple-element.17.before), channel_id=1, source_target_pairs={{0,28},{4,8},{8,4},{12,16},{16,12},{20,24},{24,20},{28,0},{1,29},{... | collective-permute-start | bytes 393224 | tf_op jit(solution)/shard_map/ppermute | solution.py:345
  8.9 11.4 %all-to-all-start = ((bf16[8,144,128]{2,1,0:T(8,128)(2,1)}), bf16[8,144,128]{2,1,0:T(8,128)(2,1)S(1)}, u32[]{:S(2)}, u32[]{:S(2)}) async-start(bf16[8,144,128]{2,1,0:T(8,128)(2,1)} %get-tuple-element.26), calls=%async_computation | async-start | bytes 589824 | tf_op jit(solution)/shard_map/all_to_all | solution.py:357

commit v9 on v8

--- a/solution.py
+++ b/solution.py
@@ -266,11 +266,11 @@
         parents, slots = unpack_rows(arrived, count, features)
         place = lax.broadcasted_iota(jnp.int32, (count, count), 0)
         places = jnp.where(place == jnp.broadcast_to(slots, (count, count)), 1.0, 0.0).astype(BF16)
-        ordered = mm(places, parents).astype(BF16)
+        normed_parents = mm(places, rms_rows(parents, gains[1])).astype(BF16)
     else:
         places = one_hot(arrived[:, features:].astype(F32).astype(jnp.int32), count)
         ordered = mm(places, arrived[:, :features], TN).astype(BF16)
-    normed_parents = rms_rows(ordered, gains[1])
+        normed_parents = rms_rows(ordered, gains[1])
     p_keys[...] = mm(normed_parents, wp[:features]).astype(BF16)
     p_values[...] = mm(normed_parents, wp[features:]).astype(BF16)
     split = early.shape[0]

time: 25.4 us -> 25.3 us (level)
  transfers between devices with their start and end apart: 3 -> 3, of which waited for: 0 -> 0; matrix products, arithmetic and copies ran while one was open for 0% -> 0% of each run, Pallas kernels for 34% -> 35%
where the time goes in v9:
time: 25.3 us; the launch traced here: 25.1 us
  Pallas kernels  15 us (59%)
  starting transfers between devices  9.96 us (39%)
    pallas_call x1, Pallas kernels, on_device(): pl.pallas_call(functools.partial(self_kernel, **sizes), out_shape=[near(r...  7.94 us
    pallas_call x1, Pallas kernels, on_device(): pl.pallas_call(functools.partial(cross_kernel, tight=tight, **sizes), out...  4.82 us
    ppermute x1, starting transfers between devices, on_device(): second_in = lax.ppermute(second, 'pix', across)  3.54 us
    all_to_all x1, starting transfers between devices, on_device(): lax.all_to_all(packed, 'pix', split_axis=0, concat_axis=0, tiled=True, ax...  3.39 us
    ppermute x1, starting transfers between devices, on_device(): first_in = lax.ppermute(first, 'pix', pairs)  3.03 us
    pallas_call x1, Pallas kernels, on_device(): pl.pallas_call(functools.partial(pack_kernel, order=order), out_shape=[ne...  1.57 us
    pallas_call x1, Pallas kernels, on_device(): pl.pallas_call(norm_kernel, out_shape=[pltpu.HBM(packing, BF16), near(row...  0.72 us
  transfers between devices with their start and end apart: 3, of which 0 were waited for; matrix products, arithmetic and copies ran while one was open for 0% of the time, Pallas kernels for 35%

profile of v9, /device:TPU:0, one launch (start us, length us, event | category | flops | bytes accessed | tf_op | source)
XLA Modules:
  0.0 25.1 jit_solution(2383718760654940892)
XLA Ops:
  0.0 1.6 %pack.1 = (bf16[128,512]{1,0:T(8,128)(2,1)S(1)}, bf16[128,512]{1,0:T(8,128)(2,1)S(1)}, bf16[8,144,128]{2,1,0:T(8,128)(2,1)S(1)}, bf16[1024,512]{1,0:T(8,128)(2,1...) custom-call(bf16[1024,512]{1,0:T(8,128)(2,1)} %fine_h.1, bf16[256,512]{1,0:T(8,128)(2,1)} %parents.1, ...), custom_call_target="tpu_custom_call" | custom-call | tf_op jit(solution)/shard_map/pack/pallas_call | solution.py:319
  1.6 3.0 %collective-permute-start = (bf16[128,512]{1,0:T(8,128)(2,1)S(1)}, bf16[128,512]{1,0:T(8,128)(2,1)S(1)}, u32[]{:S(2)}, u32[]{:S(2)}) collective-permute-start(bf16[128,512]{1,0:T(8,128)(2,1)S(1)} %get-tuple-element.23), channel_id=1, source_target_pairs={{0,4},{4,0},{8,12},{12,8},{16,20},{20,16},{24,28},{28,24},{1,5},{5... | collective-permute-start | bytes 393224 | tf_op jit(solution)/shard_map/ppermute | solution.py:344
  4.6 3.5 %collective-permute-start.1 = (bf16[128,512]{1,0:T(8,128)(2,1)S(1)}, bf16[128,512]{1,0:T(8,128)(2,1)S(1)}, u32[]{:S(2)}, u32[]{:S(2)}) collective-permute-start(bf16[128,512]{1,0:T(8,128)(2,1)S(1)} %get-tuple-element.17.before), channel_id=1, source_target_pairs={{0,28},{4,8},{8,4},{12,16},{16,12},{20,24},{24,20},{28,0},{1,29},{... | collective-permute-start | bytes 393224 | tf_op jit(solution)/shard_map/ppermute | solution.py:345
  8.2 0.7 %norm.1 = (bf16[8,144,128]{2,1,0:T(8,128)(2,1)}, bf16[1024,512]{1,0:T(8,128)(2,1)S(1)}) custom-call(bf16[128,512]{1,0:T(8,128)(2,1)S(1)} %get-tuple-element.17.before, bf16[8,144,128]{2,1,0:T(8,128)(2,1)S(1)} %get-tuple-element.18.packed, bf16[1024,512]{1,0:T(8,128)(2,1)S(1)} %get-tuple-element.19.fine, ...), custom_call_target="tpu_custom_call", output_to_operand_aliasing={{1}: (2, {})} | custom-call | tf_op jit(solution)/shard_map/norm/pallas_call | solution.py:346
  8.9 3.4 %all-to-all-start = ((bf16[8,144,128]{2,1,0:T(8,128)(2,1)}), bf16[8,144,128]{2,1,0:T(8,128)(2,1)S(1)}, u32[]{:S(2)}, u32[]{:S(2)}) async-start(bf16[8,144,128]{2,1,0:T(8,128)(2,1)} %get-tuple-element.26), calls=%async_computation | async-start | bytes 589824 | tf_op jit(solution)/shard_map/all_to_all | solution.py:357
  12.3 0.0 collective-permute-done.first
  12.3 0.0 collective-permute-done.1.second
  12.3 7.9 %self.1 = (bf16[1024,512]{1,0:T(8,128)(2,1)S(1)}, bf16[2,512,256]{2,1,0:T(8,128)(2,1)}, bf16[2,512,256]{2,1,0:T(8,128)(2,1)S(1)}, bf16[1024,512]{1,0:T(8,128)(2,1)S(1)}) custom-call(bf16[1024,512]{1,0:T(8,128)(2,1)S(1)} %get-tuple-element.21.normed, s32[4,1,256]{2,1,0:T(1,128)S(1)} %get-tuple-element.22.index, ...), custom_call_target="tpu_custom_call", output_to_operand_aliasing={{3}: (0, {})} | custom-call | flops 16000000000 | bytes 4000000 | tf_op jit(solution)/shard_map/self/pallas_call | solution.py:360
  20.2 0.0 all-to-all-done.arrived
  20.3 4.8 %cross.1 = bf16[1024,512]{1,0:T(8,128)(2,1)} custom-call(bf16[1024,512]{1,0:T(8,128)(2,1)S(1)} %get-tuple-element.24.query, bf16[2,512,256]{2,1,0:T(8,128)(2,1)S(1)} %get-tuple-element.25.late, f32[2,1,512]{2,1,0:T(1,128)S(1)} %get-tuple-element.20.gains, bf16[8,144,128]{2,1,0:T(8,128)(2,1)S(1)} %all-to-all-done.arrived, ...), custom_call_target="tpu_custom_call" | custom-call | flops 5000000000 | bytes 6000000 | tf_op jit(solution)/shard_map/cross/pallas_call | solution.py:386
Async XLA Ops:
  1.6 10.7 %collective-permute-start = (bf16[128,512]{1,0:T(8,128)(2,1)S(1)}, bf16[128,512]{1,0:T(8,128)(2,1)S(1)}, u32[]{:S(2)}, u32[]{:S(2)}) collective-permute-start(bf16[128,512]{1,0:T(8,128)(2,1)S(1)} %get-tuple-element.23), channel_id=1, source_target_pairs={{0,4},{4,0},{8,12},{12,8},{16,20},{20,16},{24,28},{28,24},{1,5},{5... | collective-permute-start | bytes 393224 | tf_op jit(solution)/shard_map/ppermute | solution.py:344
  4.6 7.7 %collective-permute-start.1 = (bf16[128,512]{1,0:T(8,128)(2,1)S(1)}, bf16[128,512]{1,0:T(8,128)(2,1)S(1)}, u32[]{:S(2)}, u32[]{:S(2)}) collective-permute-start(bf16[128,512]{1,0:T(8,128)(2,1)S(1)} %get-tuple-element.17.before), channel_id=1, source_target_pairs={{0,28},{4,8},{8,4},{12,16},{16,12},{20,24},{24,20},{28,0},{1,29},{... | collective-permute-start | bytes 393224 | tf_op jit(solution)/shard_map/ppermute | solution.py:345
  8.9 11.4 %all-to-all-start = ((bf16[8,144,128]{2,1,0:T(8,128)(2,1)}), bf16[8,144,128]{2,1,0:T(8,128)(2,1)S(1)}, u32[]{:S(2)}, u32[]{:S(2)}) async-start(bf16[8,144,128]{2,1,0:T(8,128)(2,1)} %get-tuple-element.26), calls=%async_computation | async-start | bytes 589824 | tf_op jit(solution)/shard_map/all_to_all | solution.py:357

commit v10 on v8

--- a/solution.py
+++ b/solution.py
@@ -143,8 +143,8 @@
         (gain, gains.at[0]),
         (parent_gain, gains.at[1]),
         (index, index_v),
-        (fine, fine_v),
     ]
+    pieces += [(fine.at[k : k + WIN], fine_v.at[k : k + WIN]) for k in range(0, rows, WIN)]
     copies = [pltpu.make_async_copy(src, dst, sems.at[k]) for k, (src, dst) in enumerate(pieces)]
     for copy in copies:
         copy.start()
@@ -331,7 +331,7 @@
         scratch_shapes=[
             near(parents, features),
             near(1, parents, dtype=jnp.int32),
-            semaphores((8,)),
+            semaphores((7 + windows,)),
         ],
         compiler_params=params,
         name="pack",

time: 25.4 us -> 25.4 us (level)
  transfers between devices with their start and end apart: 3 -> 3, of which waited for: 0 -> 0; matrix products, arithmetic and copies ran while one was open for 0% -> 0% of each run, Pallas kernels for 34% -> 35%
where the time goes in v10:
time: 25.4 us; the launch traced here: 25.1 us
  Pallas kernels  15.1 us (59%)
  starting transfers between devices  9.96 us (39%)
    pallas_call x1, Pallas kernels, on_device(): pl.pallas_call(functools.partial(self_kernel, **sizes), out_shape=[near(r...  7.95 us
    pallas_call x1, Pallas kernels, on_device(): pl.pallas_call(functools.partial(cross_kernel, tight=tight, **sizes), out...  4.89 us
    ppermute x1, starting transfers between devices, on_device(): second_in = lax.ppermute(second, 'pix', across)  3.54 us
    all_to_all x1, starting transfers between devices, on_device(): lax.all_to_all(packed, 'pix', split_axis=0, concat_axis=0, tiled=True, ax...  3.39 us
    ppermute x1, starting transfers between devices, on_device(): first_in = lax.ppermute(first, 'pix', pairs)  3.03 us
    pallas_call x1, Pallas kernels, on_device(): pl.pallas_call(functools.partial(pack_kernel, order=order), out_shape=[ne...  1.55 us
    pallas_call x1, Pallas kernels, on_device(): pl.pallas_call(norm_kernel, out_shape=[pltpu.HBM(packing, BF16), near(row...  0.72 us
  transfers between devices with their start and end apart: 3, of which 0 were waited for; matrix products, arithmetic and copies ran while one was open for 0% of the time, Pallas kernels for 35%

profile of v10, /device:TPU:0, one launch (start us, length us, event | category | flops | bytes accessed | tf_op | source)
XLA Modules:
  0.0 25.1 jit_solution(18062025399408743663)
XLA Ops:
  0.0 1.5 %pack.1 = (bf16[128,512]{1,0:T(8,128)(2,1)S(1)}, bf16[128,512]{1,0:T(8,128)(2,1)S(1)}, bf16[8,144,128]{2,1,0:T(8,128)(2,1)S(1)}, bf16[1024,512]{1,0:T(8,128)(2,1...) custom-call(bf16[1024,512]{1,0:T(8,128)(2,1)} %fine_h.1, bf16[256,512]{1,0:T(8,128)(2,1)} %parents.1, ...), custom_call_target="tpu_custom_call" | custom-call | tf_op jit(solution)/shard_map/pack/pallas_call | solution.py:319
  1.6 3.0 %collective-permute-start = (bf16[128,512]{1,0:T(8,128)(2,1)S(1)}, bf16[128,512]{1,0:T(8,128)(2,1)S(1)}, u32[]{:S(2)}, u32[]{:S(2)}) collective-permute-start(bf16[128,512]{1,0:T(8,128)(2,1)S(1)} %get-tuple-element.23), channel_id=1, source_target_pairs={{0,4},{4,0},{8,12},{12,8},{16,20},{20,16},{24,28},{28,24},{1,5},{5... | collective-permute-start | bytes 393224 | tf_op jit(solution)/shard_map/ppermute | solution.py:344
  4.6 3.5 %collective-permute-start.1 = (bf16[128,512]{1,0:T(8,128)(2,1)S(1)}, bf16[128,512]{1,0:T(8,128)(2,1)S(1)}, u32[]{:S(2)}, u32[]{:S(2)}) collective-permute-start(bf16[128,512]{1,0:T(8,128)(2,1)S(1)} %get-tuple-element.17.before), channel_id=1, source_target_pairs={{0,28},{4,8},{8,4},{12,16},{16,12},{20,24},{24,20},{28,0},{1,29},{... | collective-permute-start | bytes 393224 | tf_op jit(solution)/shard_map/ppermute | solution.py:345
  8.1 0.7 %norm.1 = (bf16[8,144,128]{2,1,0:T(8,128)(2,1)}, bf16[1024,512]{1,0:T(8,128)(2,1)S(1)}) custom-call(bf16[128,512]{1,0:T(8,128)(2,1)S(1)} %get-tuple-element.17.before, bf16[8,144,128]{2,1,0:T(8,128)(2,1)S(1)} %get-tuple-element.18.packed, bf16[1024,512]{1,0:T(8,128)(2,1)S(1)} %get-tuple-element.19.fine, ...), custom_call_target="tpu_custom_call", output_to_operand_aliasing={{1}: (2, {})} | custom-call | tf_op jit(solution)/shard_map/norm/pallas_call | solution.py:346
  8.9 3.4 %all-to-all-start = ((bf16[8,144,128]{2,1,0:T(8,128)(2,1)}), bf16[8,144,128]{2,1,0:T(8,128)(2,1)S(1)}, u32[]{:S(2)}, u32[]{:S(2)}) async-start(bf16[8,144,128]{2,1,0:T(8,128)(2,1)} %get-tuple-element.26), calls=%async_computation | async-start | bytes 589824 | tf_op jit(solution)/shard_map/all_to_all | solution.py:357
  12.3 0.0 collective-permute-done.first
  12.3 0.0 collective-permute-done.1.second
  12.3 7.9 %self.1 = (bf16[1024,512]{1,0:T(8,128)(2,1)S(1)}, bf16[2,512,256]{2,1,0:T(8,128)(2,1)}, bf16[2,512,256]{2,1,0:T(8,128)(2,1)S(1)}, bf16[1024,512]{1,0:T(8,128)(2,1)S(1)}) custom-call(bf16[1024,512]{1,0:T(8,128)(2,1)S(1)} %get-tuple-element.21.normed, s32[4,1,256]{2,1,0:T(1,128)S(1)} %get-tuple-element.22.index, ...), custom_call_target="tpu_custom_call", output_to_operand_aliasing={{3}: (0, {})} | custom-call | flops 16000000000 | bytes 4000000 | tf_op jit(solution)/shard_map/self/pallas_call | solution.py:360
  20.2 0.0 all-to-all-done.arrived
  20.2 4.9 %cross.1 = bf16[1024,512]{1,0:T(8,128)(2,1)} custom-call(bf16[1024,512]{1,0:T(8,128)(2,1)S(1)} %get-tuple-element.24.query, bf16[2,512,256]{2,1,0:T(8,128)(2,1)S(1)} %get-tuple-element.25.late, f32[2,1,512]{2,1,0:T(1,128)S(1)} %get-tuple-element.20.gains, bf16[8,144,128]{2,1,0:T(8,128)(2,1)S(1)} %all-to-all-done.arrived, ...), custom_call_target="tpu_custom_call" | custom-call | flops 5000000000 | bytes 6000000 | tf_op jit(solution)/shard_map/cross/pallas_call | solution.py:386
Async XLA Ops:
  1.6 10.7 %collective-permute-start = (bf16[128,512]{1,0:T(8,128)(2,1)S(1)}, bf16[128,512]{1,0:T(8,128)(2,1)S(1)}, u32[]{:S(2)}, u32[]{:S(2)}) collective-permute-start(bf16[128,512]{1,0:T(8,128)(2,1)S(1)} %get-tuple-element.23), channel_id=1, source_target_pairs={{0,4},{4,0},{8,12},{12,8},{16,20},{20,16},{24,28},{28,24},{1,5},{5... | collective-permute-start | bytes 393224 | tf_op jit(solution)/shard_map/ppermute | solution.py:344
  4.6 7.7 %collective-permute-start.1 = (bf16[128,512]{1,0:T(8,128)(2,1)S(1)}, bf16[128,512]{1,0:T(8,128)(2,1)S(1)}, u32[]{:S(2)}, u32[]{:S(2)}) collective-permute-start(bf16[128,512]{1,0:T(8,128)(2,1)S(1)} %get-tuple-element.17.before), channel_id=1, source_target_pairs={{0,28},{4,8},{8,4},{12,16},{16,12},{20,24},{24,20},{28,0},{1,29},{... | collective-permute-start | bytes 393224 | tf_op jit(solution)/shard_map/ppermute | solution.py:345
  8.9 11.4 %all-to-all-start = ((bf16[8,144,128]{2,1,0:T(8,128)(2,1)}), bf16[8,144,128]{2,1,0:T(8,128)(2,1)S(1)}, u32[]{:S(2)}, u32[]{:S(2)}) async-start(bf16[8,144,128]{2,1,0:T(8,128)(2,1)} %get-tuple-element.26), calls=%async_computation | async-start | bytes 589824 | tf_op jit(solution)/shard_map/all_to_all | solution.py:357
